TPU v7x, 32 devices: a whole 2x2x4 slice. The times are simulated.
32 devices in a mesh: patch: 16 (over z, y, x), vec: 2 (over core).
Axes of the slice: x: 2, y: 2, z: 4, core: 2. Of those that a mesh axis runs over, the one named last changes fastest.
Arguments:
- vectors: float32 [8192, 512], P('patch', 'vec'), may hold values from -6 to 6
- blocks: bfloat16 [1024, 256, 256], P('patch'), may hold values from -0.075 to 0.075, as said below
- block_row: int32 [1024], P('patch'), may hold values from 0 to 31, as said below
- block_col: int32 [1024], P('patch'), may hold values from 0 to 31, as said below
- block_count: int32 [16], P('patch'), may hold values from 0 to 58, as said below
Outputs:
- subspace: float32 [8192, 512], P('patch', 'vec')
- residual: float32 [8192, 512], P('patch', 'vec')
Inputs may be any that keep to these rules, and one draw needn't show every extreme that they name: `block_row`: device p owns entries p * 64 to (p + 1) * 64 - 1. Its used slots come first and hold tiles of block rows 4 * (p // 2) to 4 * (p // 2) + 3 whose block column is at most the row and at least 4 * (p // 2) - 12; both devices of a pair p // 2 share these rows, tiles grouped by 4 x 4 patches each on one device. Every lower tile of the pattern stands in exactly one used slot, every diagonal tile is present, and unused slots name block row and column 4 * (p // 2). `block_col`: the block column of the tile in the same slot, as described for block_row. `block_count`: at most 58 used slots on a device, reached by some device in every draw; the loads are uneven. `blocks`: entries of unused slots are never read.
All inputs are finite; a program needn't handle non-finite values.
Results may differ from a plain program's by a relative error of at most 0.0038.
Values may be sent and summed in bfloat16 or wider, within the bound.
No kernel may reach another device: no remote copies, remote signals or barrier semaphores. Data moves between devices by JAX's collectives and lax.ppermute only.
A program may use at most 128 MiB of HBM per device.

v0:
```python
import jax
import jax.numpy as jnp
from jax import lax
from jax.experimental import pallas as pl
from jax.experimental.pallas import tpu as pltpu
from jax.sharding import PartitionSpec as P

STEPS = 2
STEP_RATE = 0.25
GROUP = 8
REACH = 4

f32, bf16 = jnp.float32, jnp.bfloat16
SEGMENT_KINDS = (f32, f32, f32, f32, f32, bf16, bf16, bf16)
TILES_VMEM = 48
VMEM, SMEM = pltpu.VMEM, pltpu.SMEM


def dot_nn(a, b):
    return lax.dot_general(a, b, (((1,), (0,)), ((), ())), preferred_element_type=f32)


def dot_nt(a, b):
    return lax.dot_general(a, b, (((1,), (1,)), ((), ())), preferred_element_type=f32)


def split(a):
    high = a.astype(bf16)
    return high, (a - high.astype(f32)).astype(bf16)


def dot3(dot, a, b):
    (ah, al), (bh, bl) = a, b
    return dot(ah, bh) + (dot(ah, bl) + dot(al, bh))


def call(kernel, out, args, scratch=(), smem=0, flops=1 << 28, vmem=16):
    moved = sum(a.size * a.dtype.itemsize for a in args) + sum(o.size * o.dtype.itemsize for o in out)
    return pl.pallas_call(
        kernel,
        out_shape=out,
        in_specs=[pl.BlockSpec(memory_space=SMEM)] * smem + [pl.BlockSpec(memory_space=VMEM)] * (len(args) - smem),
        out_specs=[pl.BlockSpec(memory_space=VMEM)] * len(out),
        scratch_shapes=list(scratch),
        compiler_params=pltpu.CompilerParams(vmem_limit_bytes=vmem << 20),
        cost_estimate=pl.CostEstimate(flops=flops, bytes_accessed=moved, transcendentals=0),
    )(*args)


def shape(dtype, *dims):
    return jax.ShapeDtypeStruct(dims, dtype)


def pack_kernel(vectors, columns, chunk):
    size = chunk.shape[2]
    for t in range(chunk.shape[0]):
        turned = vectors[pl.ds(t * size, size), :].T
        columns[:, pl.ds(t * size, size)] = turned
        chunk[t] = turned.astype(bf16)


def place(tile, meta):
    start, odd, pair_odd = meta[1], meta[2], meta[3]
    w = tile - start
    back = REACH - 1 - w // 4
    role = jnp.where(back % 2 == 1, 2 + ((back // 2) ^ pair_odd ^ 1), back // 2)
    return role * 4 + 2 * (((w % 4) // 2) ^ odd) + w % 2


def gather(pieces, window, sems):
    return [pltpu.make_async_copy(piece, window.at[pl.ds(2 * s, 2)], sems.at[s]) for s, piece in enumerate(pieces)]


def each_tile(meta, rows, cols, blocks, tiles, sems, ready, product, total):
    used = meta[0]
    groups = (used + GROUP - 1) // GROUP

    def fetch(group):
        part = pl.ds(group * GROUP, GROUP)
        return pltpu.make_async_copy(blocks.at[part], tiles.at[part], sems.at[group])

    for group in range(tiles.shape[0] // GROUP):

        @pl.when(group < groups)
        def _():
            fetch(group).start()

    for copy in ready:
        copy.start()
    total[...] = jnp.zeros_like(total)
    for copy in ready:
        copy.wait()

    def multiply(group, carry):
        fetch(group).wait()
        found = []
        for k in range(GROUP):
            slot = group * GROUP + k
            row, col = rows[slot], cols[slot]
            tile = tiles[slot]
            tile = jnp.where(slot < used, tile, jnp.zeros_like(tile))
            found.append(product(tile, place(row, meta), place(col, meta)) + (row == col,))
        for at, part, diagonal in found:
            total[at] += part * jnp.where(diagonal, 0.5, 1.0).astype(f32)
        return carry

    lax.fori_loop(0, groups, multiply, 0)


def mirror_kernel(meta, rows, cols, *refs):
    pieces, blocks, out = refs[:2], refs[2], refs[3:-5]
    window, total, tiles, piece_sems, tile_sems = refs[-5:]

    def product(tile, row, col):
        return col, dot_nn(window[row], tile)

    each_tile(meta, rows, cols, blocks, tiles, tile_sems, gather(pieces, window, piece_sems), product, total)
    for s, segment in enumerate(out):
        segment[...] = total[pl.ds(2 * s, 2)].astype(segment.dtype)


def direct_kernel(meta, rows, cols, *refs):
    pieces, blocks = refs[: 2 * REACH], refs[2 * REACH]
    x_other, cross_other, kept, near, kept_out, near_out, inner = refs[2 * REACH + 1 : -5]
    window, total, tiles, piece_sems, tile_sems = refs[-5:]

    def product(tile, row, col):
        return row, dot_nt(window[col], tile)

    each_tile(meta, rows, cols, blocks, tiles, tile_sems, gather(pieces, window, piece_sems), product, total)
    kept_out[...] = kept[...] + total[pl.ds(0, 2)]
    near_out[...] = (near[...] + total[pl.ds(2, 2)]).astype(bf16)
    size = inner.shape[1]
    own = jnp.zeros((size, size), f32)
    other = jnp.zeros((size, size), f32)
    for s in range(4):
        mine = total[s].astype(bf16)
        there = x_other[:, pl.ds(s * size, size)].astype(bf16) if s < 2 else cross_other[s - 2]
        own += dot_nt(mine, window[s])
        other += dot_nt(mine, there)
    inner[pl.ds(0, size), :] = own + own.T
    inner[pl.ds(size, size), :] = other


def tiles_call(kernel, out, meta, blocks, rows, cols, pieces, more, window, total):
    size, width = blocks.shape[1], pieces[0].shape[1]
    return pl.pallas_call(
        kernel,
        in_specs=[pl.BlockSpec(memory_space=SMEM)] * 3
        + [pl.BlockSpec(memory_space=pl.ANY)] * len(pieces)
        + [pl.BlockSpec(memory_space=pltpu.HBM)]
        + [pl.BlockSpec(memory_space=VMEM)] * len(more),
        out_specs=[pl.BlockSpec(memory_space=VMEM)] * len(out),
        scratch_shapes=[
            VMEM((window, width, size), bf16),
            VMEM((total, width, size), f32),
            VMEM(blocks.shape, bf16),
            pltpu.SemaphoreType.DMA((len(pieces),)),
            pltpu.SemaphoreType.DMA((blocks.shape[0] // GROUP,)),
        ],
        out_shape=out,
        compiler_params=pltpu.CompilerParams(vmem_limit_bytes=TILES_VMEM << 20),
        cost_estimate=pl.CostEstimate(flops=4 << 30, bytes_accessed=12 << 20, transcendentals=0),
    )(meta, rows, cols, *pieces, blocks, *more)


def descend_kernel(x, kept, near, far, two, out):
    size = kept.shape[2]
    for t in range(x.shape[1] // size):
        part = pl.ds(t * size, size)
        applied = kept[t] + near[t].astype(f32) + (far[t].astype(f32) + two[t].astype(f32))
        out[:, part] = x[:, part] - STEP_RATE * applied


def gram_kernel(core, mine, theirs, out):
    width = mine.shape[0]
    half = width // 2
    own, other = split(mine[...]), split(theirs[...])
    out[pl.ds(0, width), :] = dot3(dot_nt, own, own)
    ahead = core[0] == 0
    high = jnp.where(ahead, theirs[pl.ds(0, half), :], mine[pl.ds(half, half), :])
    low = [jnp.where(ahead, a, b) for a, b in zip(own, other)]
    out[pl.ds(width, half), :] = dot3(dot_nt, split(high), low)


def inverse_factor(g, w, high, low):
    n = g.shape[0]
    at_row = lax.broadcasted_iota(jnp.int32, (n, n), 0)
    at_col = lax.broadcasted_iota(jnp.int32, (n, n), 1)
    eye = jnp.where(at_row == at_col, 1.0, 0.0).astype(f32)
    diagonal = eye * g[...]
    by_row = lax.rsqrt(jnp.sum(diagonal, axis=1, keepdims=True))
    by_col = lax.rsqrt(jnp.sum(diagonal, axis=0, keepdims=True))
    unit = g[...] * by_row * by_col
    rounded = unit.astype(bf16)
    square = dot_nn(rounded, rounded).astype(bf16)
    fourth = dot_nn(square, square)
    scale = 1.9 / jnp.sqrt(jnp.sqrt(jnp.sqrt(jnp.sum(fourth * fourth, keepdims=True))))
    scaled = unit * scale
    high[...], low[...] = split(scaled)

    half = n // 2
    top, bottom = pl.ds(0, half), pl.ds(half, half)
    small = eye[:half, :half]
    triangle = (at_row > at_col)[:half, :half]

    def lower(e):
        return jnp.where(triangle, e, 0.5 * small * e)

    def read(ref):
        return ref[top, top], ref[bottom, top], ref[bottom, bottom]

    def product(a, b):
        return dot_nn(a[0], b[0]), dot_nn(a[1], b[0]) + dot_nn(a[2], b[1]), dot_nn(a[2], b[2])

    def narrow(blocks):
        return tuple(block.astype(bf16) for block in blocks)

    p = (lower(scaled[:half, :half] - small), scaled[half:, :half], lower(scaled[half:, half:] - small))
    pb = narrow(p)
    square = product(pb, pb)
    w[top, bottom] = jnp.zeros((half, half), f32)
    w[top, top] = small - p[0] + square[0]
    w[bottom, top] = square[1] - p[1]
    w[bottom, bottom] = small - p[2] + square[2]

    def improve(e, old):
        p = (lower(e[0] - small), e[1], lower(e[2] - small))
        pb = narrow(p)
        first = product(pb, narrow(old))
        second = product(pb, narrow(first))
        w[top, top] = old[0] - first[0] + second[0]
        w[bottom, top] = old[1] - first[1] + second[1]
        w[bottom, bottom] = old[2] - first[2] + second[2]
        return jnp.sqrt(sum(jnp.sum(block * block) for block in p))

    def congruence(nn, nt, cut, w, s):
        s00, s10, s11, s01 = s
        left = nn(w[0], s00)
        below, right = nn(w[1], s00) + nn(w[2], s10), nn(w[1], s01) + nn(w[2], s11)
        left, below, right = cut(left), cut(below), cut(right)
        return nt(left, w[0]), nt(below, w[0]), nt(below, w[1]) + nt(right, w[2])

    def whole(ref):
        return read(ref) + (ref[top, bottom],)

    def rough(state):
        old = read(w)
        e = congruence(dot_nn, dot_nt, lambda a: a.astype(bf16), narrow(old), whole(high))
        return state[0] + 1, improve(e, old)

    def fine(state):
        old = read(w)
        nn, nt = (lambda a, b: dot3(dot_nn, a, b)), (lambda a, b: dot3(dot_nt, a, b))
        e = congruence(nn, nt, split, [split(a) for a in old], list(zip(whole(high), whole(low))))
        return state[0] + 1, improve(e, old)

    def until(bound, most):
        return lambda state: (state[0] < most) & jnp.logical_not(state[1] <= bound)

    lax.while_loop(until(0.4, 16), rough, (0, jnp.float32(1e9)))
    _, error = lax.while_loop(until(0.1, 6), fine, (0, jnp.float32(1e9)))
    done = error <= 0.1

    @pl.when(done)
    def _():
        w[...] = w[...] * (by_col * jnp.sqrt(scale))

    @pl.when(jnp.logical_not(done))
    def _():
        w[...] = eye

        def eliminate(k, carry):
            lane = lax.broadcasted_iota(jnp.int32, (1, n), 1)
            below = lax.broadcasted_iota(jnp.int32, (n, 1), 0)
            row = g[pl.ds(k, 1), :]
            pivot = jnp.sum(jnp.where(lane == k, row, 0.0), axis=1, keepdims=True)
            column = jnp.sum(jnp.where(at_col == k, g[...], 0.0), axis=1, keepdims=True)
            ratio = jnp.where(below > k, column / pivot, 0.0)
            solved = w[pl.ds(k, 1), :]
            g[...] = g[...] - ratio * row
            w[...] = w[...] - ratio * solved
            w[pl.ds(k, 1), :] = solved * lax.rsqrt(pivot)
            return carry

        lax.fori_loop(0, n, eliminate, 0)


def lay_out(out, first, second):
    width = first.shape[1]
    out[pl.ds(0, width), pl.ds(0, width)] = first[:width]
    out[pl.ds(width, width), pl.ds(width, width)] = second[:width]
    below = jnp.concatenate([first[width:], second[width:]], axis=0)
    out[pl.ds(width, width), pl.ds(0, width)] = below
    out[pl.ds(0, width), pl.ds(width, width)] = below.T


def factor_kernel(rows_total, first_step, last, core, v, v_other, x, x_other, gram, gram_other, inner, inner_other, *refs):
    out, (g, w, high, low, update, rayleigh) = refs[:-6], refs[-6:]
    width, count = v.shape
    ahead = core[0] == 0

    def ordered(mine, theirs):
        mine, theirs = mine / rows_total, theirs / rows_total
        return jnp.where(ahead, mine, theirs), jnp.where(ahead, theirs, mine)

    first, second = ordered(inner[pl.ds(0, 2 * width), :], inner_other[pl.ds(0, 2 * width), :])
    rayleigh[pl.ds(0, width), pl.ds(0, width)] = first[:width]
    rayleigh[pl.ds(width, width), pl.ds(width, width)] = second[:width]
    across = first[width:] + second[width:].T
    rayleigh[pl.ds(0, width), pl.ds(width, width)] = across
    rayleigh[pl.ds(width, width), pl.ds(0, width)] = across.T
    lay_out(g, *ordered(gram[...], gram_other[...]))
    r = split(rayleigh[...])
    if first_step:
        extra = pl.ds(2 * width, width + width // 2)
        lay_out(w, *ordered(inner[extra, :], inner_other[extra, :]))
        turned = dot3(dot_nn, split(w[...]), r)
        g[...] += STEP_RATE * (turned + turned.T)
        g[...] += dot3(dot_nn, r, split(STEP_RATE**2 * turned - (2 * STEP_RATE**2) * rayleigh[...]))
    else:
        g[...] += 2 * STEP_RATE * rayleigh[...] - STEP_RATE**2 * dot3(dot_nn, r, r)
    inverse_factor(g, w, high, low)
    start = pl.multiple_of(core[0] * width, width)
    there = width - start
    update[pl.ds(start, width), :] = x[...]
    update[pl.ds(there, width), :] = x_other[...]
    mix = split(w[pl.ds(start, width), :])
    mine = split(rayleigh[pl.ds(start, width), :])
    theirs = split(rayleigh[pl.ds(there, width), :])
    for t in range(count // width):
        part = pl.ds(t * width, width)
        old = split(update[:, part])
        here = v[:, part] + STEP_RATE * dot3(dot_nn, mine, old)
        update[pl.ds(there, width), part] = v_other[:, part] + STEP_RATE * dot3(dot_nn, theirs, old)
        update[pl.ds(start, width), part] = here
        solved = dot3(dot_nn, mix, split(update[:, part]))
        if last:
            out[0][part, :] = solved.T
            out[1][part, :] = ((x[:, part] - here) * (1 / STEP_RATE)).T
        else:
            out[0][:, part] = solved
            out[1][t] = solved.astype(bf16)


def swap_cores(a):
    return lax.ppermute(a, "vec", [(0, 1), (1, 0)])


def flip(a, mask):
    return lax.ppermute(a, "patch", [(i, i ^ mask) for i in range(lax.axis_size("patch"))])


def shift(a, pairs):
    devices = range(lax.axis_size("patch"))
    return lax.ppermute(a, "patch", [(i - 2 * pairs, i) for i in devices if i - 2 * pairs in devices])


def stride(a, back=False):
    devices = range(lax.axis_size("patch"))
    route = [(i - (2 if i // 2 % 2 else 6), i) for i in devices]
    return lax.ppermute(a, "patch", [(d, s) if back else (s, d) for s, d in route if s in devices])


def together(*arrays):
    return lax.optimization_barrier(arrays)


def reach(u, own_x):
    two, far = shift(u, 2), stride(together(u, own_x)[0])
    return two, flip(two, 1), far, flip(two, 2)


def place_order(parts, place):
    radix = len(parts)
    bit = 1
    while bit < radix:
        swapped = [parts[j ^ bit] for j in range(radix)]
        parts = [jnp.where(place & bit, b, a) for a, b in zip(parts, swapped)]
        bit *= 2
    return parts


def stages_of():
    left, step, stages = lax.axis_size("patch"), 1, []
    while left > 1:
        radix = 4 if left % 4 == 0 else 2
        stages.append((radix, step))
        left, step = left // radix, step * radix
    return stages


def scatter(a, stage):
    radix, step = stage
    place = (lax.axis_index("patch") // step) % radix
    parts = a.reshape(radix, a.shape[0] // radix, a.shape[1])
    a = lax.dynamic_index_in_dim(parts, place, 0, False)
    for m in range(1, radix):
        a = a + flip(lax.dynamic_index_in_dim(parts, place ^ m, 0, False), m * step)
    return a


def exchange(a, stage):
    radix, step = stage
    return sum([flip(a, m * step) for m in range(1, radix)], a)


def collect(a, stage):
    radix, step = stage
    place = (lax.axis_index("patch") // step) % radix
    return jnp.concatenate(place_order([a] + [flip(a, m * step) for m in range(1, radix)], place), axis=0)


def sum_both(a, b, stages):
    steps_a = [(scatter, stage) for stage in stages[1:]] + [(collect, stage) for stage in stages[::-1]]
    steps_b = [(scatter, stage) for stage in stages[:-1]] + [(exchange, stages[-1])]
    steps_b += [(collect, stage) for stage in stages[-2::-1]]
    for (go_a, stage_a), (go_b, stage_b) in zip(steps_a, steps_b, strict=True):
        a, b = together(go_a(a, stage_a), go_b(b, stage_b))
    return a, b


def shards(vectors, blocks, block_row, block_col, block_count):
    count, width = vectors.shape
    size = blocks.shape[1]
    rows_total = float(count * lax.axis_size("patch"))
    position = lax.axis_index("patch")
    odd = position % 2
    meta = jnp.stack([block_count[0], 2 * (position - odd) - 4 * (REACH - 1), odd, position // 2 % 2]).astype(jnp.int32)
    core = lax.axis_index("vec").astype(jnp.int32).reshape(1)
    stages = stages_of()
    flat, chunk = shape(f32, width, count), shape(bf16, count // size, width, size)
    x, u = call(pack_kernel, [flat, chunk], [vectors])
    for step in range(STEPS):
        last = step == STEPS - 1
        own_x = flip(u, 1)
        x_other = swap_cores(x)
        cross_other = swap_cores(own_x)
        table = (meta, blocks, block_row, block_col)
        segment = (2, width, size)
        sums = tiles_call(
            mirror_kernel, [shape(kind, *segment) for kind in SEGMENT_KINDS], *table, [u, own_x], [], 4, 4 * REACH
        )
        same, cross = sums[::2], sums[1::2]
        two, two_x, far, side = reach(u, own_x)
        out_side_x, out_far, out_side = together(cross[3], cross[2], same[3], far, two_x, side)[:3]
        pieces = [u, own_x, two, two_x, far, flip(far, 1), side, flip(two_x, 2)]
        kept, near, inner = tiles_call(
            direct_kernel,
            [shape(f32, *segment), shape(bf16, *segment), shape(f32, 2 * width, width)],
            *table,
            pieces,
            [x_other, cross_other, same[0], cross[0]],
            4 * REACH,
            4,
        )
        side_x, far_x, side = flip(out_side_x, 2), flip(out_far, 1), flip(out_side, 2)
        two_out = (cross[1] + side_x.astype(f32)).astype(bf16)
        two_x, far = flip(two_out, 1), stride((same[2] + far_x.astype(f32)).astype(bf16), True)
        two = shift((same[1] + (two_x.astype(f32) + side.astype(f32))).astype(bf16), -2)
        inner_out = [inner]
        if step == 0:
            inner_out += call(gram_kernel, [shape(f32, width + width // 2, width)], [core, x, x_other], smem=1)
        inner = scatter(jnp.concatenate(inner_out), stages[0])
        inner, *joined = together(inner, flip(near, 1), far, two)
        (v,) = call(descend_kernel, [flat], [x, kept, *joined])
        v_other = swap_cores(v)
        (gram,) = call(gram_kernel, [shape(f32, width + width // 2, width)], [core, v, v_other], smem=1)
        inner, gram = together(inner, gram)
        inner, gram = sum_both(inner, gram, stages)
        full = (2 * width, 2 * width)
        wide = shape(f32, count, width)
        out = call(
            lambda *refs: factor_kernel(rows_total, step == 0, last, *refs),
            [wide, wide] if last else [flat, chunk],
            [core, v, v_other, x, x_other, gram, swap_cores(gram), inner, swap_cores(inner)],
            scratch=[VMEM(full, f32), VMEM(full, f32), VMEM(full, bf16), VMEM(full, bf16)]
            + [VMEM((2 * width, count), f32), VMEM(full, f32)],
            smem=1,
            flops=16 << 30,
            vmem=28,
        )
        x, u = out
    return x, u


def solution(mesh):
    in_specs = (P("patch", "vec"), P("patch", None, None), P("patch"), P("patch"), P("patch"))
    out_specs = (P("patch", "vec"), P("patch", "vec"))
    return jax.shard_map(shards, mesh=mesh, in_specs=in_specs, out_specs=out_specs, check_vma=False)
```

profile of v0, /device:TPU:0, one launch (start us, length us, event | category | flops | bytes accessed | tf_op | source)
XLA Modules:
  0.0 258.1 jit_solution(7149792292518138669)
XLA Ops:
  1.9 3.0 %collective-permute-start = (bf16[2,256,256]{2,1,0:T(8,128)(2,1)S(1)}, bf16[2,256,256]{2,1,0:T(8,128)(2,1)S(1)}, u32[]{:S(2)}, u32[]{:S(2)}) collective-permute-start(bf16[2,256,256]{2,1,0:T(8,128)(2,1)S(1)} %get-tuple-element.62.refs_0_), channel_id=1, source_target_pairs={{0,2},{2,0},{4,6},{6,4},{8,10},{10,8},{12,14},{14,12},{16,18},{18,... | collective-permute-start | bytes 786440 | tf_op jit(solution)/shard_map/ppermute | solution.py:351
  4.9 3.5 %collective-permute-start.1 = (bf16[2,256,256]{2,1,0:T(8,128)(2,1)S(1)}, bf16[2,256,256]{2,1,0:T(8,128)(2,1)S(1)}, u32[]{:S(2)}, u32[]{:S(2)}) collective-permute-start(bf16[2,256,256]{2,1,0:T(8,128)(2,1)S(1)} %get-tuple-element.62.refs_0_), channel_id=1, source_target_pairs={{0,8},{2,10},{4,12},{6,14},{8,16},{10,18},{12,20},{14,22},{16,24},... | collective-permute-start | bytes 786440 | tf_op jit(solution)/shard_map/ppermute | solution.py:356
  11.2 3.7 %collective-permute-start.3 = (bf16[2,256,256]{2,1,0:T(8,128)(2,1)S(1)}, bf16[2,256,256]{2,1,0:T(8,128)(2,1)S(1)}, u32[]{:S(2)}, u32[]{:S(2)}) collective-permute-start(bf16[2,256,256]{2,1,0:T(8,128)(2,1)S(1)} %get-tuple-element.62.refs_0_), channel_id=1, source_target_pairs={{0,4},{2,6},{8,12},{10,14},{4,16},{6,18},{16,20},{18,22},{12,24},{... | collective-permute-start | bytes 786440 | tf_op jit(solution)/shard_map/ppermute | solution.py:362
  16.4 2.5 collective-permute-start.5
  20.3 4.2 %shard_map.69 = (f32[2,256,256]{2,1,0:T(8,128)S(1)}, f32[2,256,256]{2,1,0:T(8,128)S(1)}, f32[2,256,256]{2,1,0:T(8,128)S(1)}, f32[2,256,256]{2,1,0:T(8,128)S(1)},...) custom-call(s32[4]{0:T(128)S(1)} %pad_add_fusion.meta, ...), custom_call_target="tpu_custom_call" | custom-call | flops 4294967296 | bytes 12582912 | tf_op jit(solution)/shard_map/pallas_call | solution.py:147
  28.9 2.0 collective-permute-start.17
  30.9 2.0 collective-permute-start.4
  33.6 4.9 %collective-permute-done.15 = bf16[2,256,256]{2,1,0:T(8,128)(2,1)} collective-permute-done((bf16[2,256,256]{2,1,0:T(8,128)(2,1)}, bf16[2,256,256]{2,1,0:T(8,128)(2,1)}, u32[]{:S(2)}, u32[]{:S(2)}) %collective-permute-start.15) | collective-permute-done | bytes 262176 | tf_op jit(solution)/shard_map/ppermute | solution.py:351
  42.6 3.3 %collective-permute-done.4.refs_5_ = bf16[2,256,256]{2,1,0:T(8,128)(2,1)S(1)} collective-permute-done((bf16[2,256,256]{2,1,0:T(8,128)(2,1)}, bf16[2,256,256]{2,1,0:T(8,128)(2,1)S(1)}, u32[]{:S(2)}, u32[]{:S(2)}) %collective-permute-start.4) | collective-permute-done | bytes 262176 | tf_op jit(solution)/shard_map/ppermute | solution.py:351
  45.9 2.6 %collective-permute-done.6.refs_7_ = bf16[2,256,256]{2,1,0:T(8,128)(2,1)S(1)} collective-permute-done((bf16[2,256,256]{2,1,0:T(8,128)(2,1)}, bf16[2,256,256]{2,1,0:T(8,128)(2,1)S(1)}, u32[]{:S(2)}, u32[]{:S(2)}) %collective-permute-start.6) | collective-permute-done | bytes 262176 | tf_op jit(solution)/shard_map/ppermute | solution.py:351
  53.5 4.0 %shard_map.70 = (f32[2,256,256]{2,1,0:T(8,128)S(1)}, bf16[2,256,256]{2,1,0:T(8,128)(2,1)S(1)}, f32[512,256]{1,0:T(8,128)S(1)}) custom-call(s32[4]{0:T(128)S(1)} %pad_add_fusion.meta, s32[64]{0:T(128)S(1)} %copy-done.10, s32[64]{0:T(128)S(1)} %copy-done.12, bf16[2,256,256]{2,1,0:T(8,128)(2,1)S(1)} %get-tuple-element.62.refs_0_, ...), custom_call_target="tpu_custom_call" | custom-call | flops 4294967296 | bytes 12582912 | tf_op jit(solution)/shard_map/pallas_call | solution.py:147
  58.5 3.5 %collective-permute-start.9 = (f32[224,256]{1,0:T(8,128)}, f32[224,256]{1,0:T(8,128)}, u32[]{:S(2)}, u32[]{:S(2)}) collective-permute-start(f32[224,256]{1,0:T(8,128)} %get-tuple-element.122), channel_id=1, source_target_pairs={{0,2},{2,0},{4,6},{6,4},{8,10},{10,8},{12,14},{14,12},{16,18},{18,... | collective-permute-start | bytes 688136 | tf_op jit(solution)/shard_map/ppermute | solution.py:351
  62.1 3.7 %collective-permute-done.10 = f32[224,256]{1,0:T(8,128)S(1)} collective-permute-done((f32[224,256]{1,0:T(8,128)S(1)}, f32[224,256]{1,0:T(8,128)S(1)}, u32[]{:S(2)}, u32[]{:S(2)}) %collective-permute-start.10) | collective-permute-done | bytes 229408 | tf_op jit(solution)/shard_map/ppermute | solution.py:351
  68.2 3.1 %collective-permute-done.9 = f32[224,256]{1,0:T(8,128)} collective-permute-done((f32[224,256]{1,0:T(8,128)}, f32[224,256]{1,0:T(8,128)}, u32[]{:S(2)}, u32[]{:S(2)}) %collective-permute-start.9) | collective-permute-done | bytes 229408 | tf_op jit(solution)/shard_map/ppermute | solution.py:351
  78.8 5.6 %collective-permute-start.20 = (f32[56,256]{1,0:T(8,128)S(1)}, f32[56,256]{1,0:T(8,128)S(1)}, u32[]{:S(2)}, u32[]{:S(2)}) collective-permute-start(f32[56,256]{1,0:T(8,128)S(1)} %get-tuple-element.150), channel_id=1, source_target_pairs={{0,8},{2,10},{4,12},{6,14},{8,0},{10,2},{12,4},{14,6},{16,24},{18,... | collective-permute-start | bytes 172040 | tf_op jit(solution)/shard_map/ppermute | solution.py:351
  84.4 2.8 %collective-permute-start.21 = (f32[56,256]{1,0:T(8,128)S(1)}, f32[56,256]{1,0:T(8,128)S(1)}, u32[]{:S(2)}, u32[]{:S(2)}) collective-permute-start(f32[56,256]{1,0:T(8,128)S(1)} %get-tuple-element.152), channel_id=1, source_target_pairs={{0,16},{2,18},{4,20},{6,22},{8,24},{10,26},{12,28},{14,30},{16,0},... | collective-permute-start | bytes 172040 | tf_op jit(solution)/shard_map/ppermute | solution.py:351
  88.2 2.6 %collective-permute-start.25 = (f32[96,256]{1,0:T(8,128)S(1)}, f32[96,256]{1,0:T(8,128)S(1)}, u32[]{:S(2)}, u32[]{:S(2)}) collective-permute-start(f32[96,256]{1,0:T(8,128)S(1)} %get-tuple-element.144), channel_id=1, source_target_pairs={{0,6},{2,4},{4,2},{6,0},{8,14},{10,12},{12,10},{14,8},{16,22},{18,... | collective-permute-start | bytes 294920 | tf_op jit(solution)/shard_map/ppermute | solution.py:351
  90.9 2.3 collective-permute-done.22
  94.0 3.6 %collective-permute-start.26 = (f32[56,256]{1,0:T(8,128)S(1)}, f32[56,256]{1,0:T(8,128)S(1)}, u32[]{:S(2)}, u32[]{:S(2)}) collective-permute-start(f32[56,256]{1,0:T(8,128)S(1)} %fusion.9), channel_id=1, source_target_pairs={{0,24},{2,26},{4,28},{6,30},{8,16},{10,18},{12,20},{14,22},{16,8},... | collective-permute-start | bytes 172040 | tf_op jit(solution)/shard_map/ppermute | solution.py:351
  99.7 2.9 %collective-permute-start.30 = (f32[96,256]{1,0:T(8,128)S(1)}, f32[96,256]{1,0:T(8,128)S(1)}, u32[]{:S(2)}, u32[]{:S(2)}) collective-permute-start(f32[96,256]{1,0:T(8,128)S(1)} %fusion.7), channel_id=1, source_target_pairs={{0,16},{2,18},{4,20},{6,22},{8,24},{10,26},{12,28},{14,30},{16,0},... | collective-permute-start | bytes 294920 | tf_op jit(solution)/shard_map/ppermute | solution.py:351
  106.0 2.1 collective-permute-done.30
  109.2 2.6 %collective-permute-start.35 = (f32[96,256]{1,0:T(8,128)S(1)}, f32[96,256]{1,0:T(8,128)S(1)}, u32[]{:S(2)}, u32[]{:S(2)}) collective-permute-start(f32[96,256]{1,0:T(8,128)S(1)} %add_add_fusion.1), channel_id=1, source_target_pairs={{0,6},{2,4},{4,2},{6,0},{8,14},{10,12},{12,10},{14,8},{16,22},{18,... | collective-permute-start | bytes 294920 | tf_op jit(solution)/shard_map/ppermute | solution.py:351
  112.7 2.6 collective-permute-start.32
  118.2 3.6 %collective-permute-done.32 = f32[224,256]{1,0:T(8,128)S(1)} collective-permute-done((f32[224,256]{1,0:T(8,128)S(1)}, f32[224,256]{1,0:T(8,128)S(1)}, u32[]{:S(2)}, u32[]{:S(2)}) %collective-permute-start.32) | collective-permute-done | bytes 229408 | tf_op jit(solution)/shard_map/ppermute | solution.py:351
  121.8 2.3 collective-permute-done.33
  124.8 2.5 collective-permute-done.38.refs_6_
  127.4 13.2 %shard_map.74 = (f32[256,512]{1,0:T(8,128)S(1)}, bf16[2,256,256]{2,1,0:T(8,128)(2,1)S(1)}) custom-call(s32[1]{0:T(128)} %bitcast.core.refs_0_, f32[256,512]{1,0:T(8,128)S(1)} %shard_map.72.mine.refs_1_, f32[256,512]{1,0:T(8,128)S(1)} %collective-permute-done.19.theirs.refs_2_, f32[256,512]{1,0:T(8,128)S(1)} %get-tuple-element.60.mine.x.refs_3_, ...), custom_call_target="tpu_custom_call" | custom-call | flops 17179869184 | bytes 5505028 | tf_op jit(solution)/shard_map/pallas_call | solution.py:39
  141.8 5.1 %collective-permute-start.41 = (bf16[2,256,256]{2,1,0:T(8,128)(2,1)S(1)}, bf16[2,256,256]{2,1,0:T(8,128)(2,1)S(1)}, u32[]{:S(2)}, u32[]{:S(2)}) collective-permute-start(bf16[2,256,256]{2,1,0:T(8,128)(2,1)S(1)} %get-tuple-element.91.refs_0_), channel_id=1, source_target_pairs={{0,8},{2,10},{4,12},{6,14},{8,16},{10,18},{12,20},{14,22},{16,24},... | collective-permute-start | bytes 786440 | tf_op jit(solution)/shard_map/ppermute | solution.py:356
  146.9 2.1 collective-permute-done.40.refs_1_
  149.0 3.0 %collective-permute-start.43 = (bf16[2,256,256]{2,1,0:T(8,128)(2,1)S(1)}, bf16[2,256,256]{2,1,0:T(8,128)(2,1)S(1)}, u32[]{:S(2)}, u32[]{:S(2)}) collective-permute-start(bf16[2,256,256]{2,1,0:T(8,128)(2,1)S(1)} %get-tuple-element.91.refs_0_), channel_id=1, source_target_pairs={{0,4},{2,6},{8,12},{10,14},{4,16},{6,18},{16,20},{18,22},{12,24},{... | collective-permute-start | bytes 786440 | tf_op jit(solution)/shard_map/ppermute | solution.py:362
  153.8 4.4 %collective-permute-start.45 = (bf16[2,256,256]{2,1,0:T(8,128)(2,1)S(1)}, bf16[2,256,256]{2,1,0:T(8,128)(2,1)S(1)}, u32[]{:S(2)}, u32[]{:S(2)}) collective-permute-start(bf16[2,256,256]{2,1,0:T(8,128)(2,1)S(1)} %collective-permute-done.41.refs_2_), channel_id=1, source_target_pairs={{0,4},{2,6},{4,0},{6,2},{8,12},{10,14},{12,8},{14,10},{16,20},{18,... | collective-permute-start | bytes 786440 | tf_op jit(solution)/shard_map/ppermute | solution.py:351
  158.2 3.8 %shard_map.75 = (f32[2,256,256]{2,1,0:T(8,128)S(1)}, f32[2,256,256]{2,1,0:T(8,128)S(1)}, f32[2,256,256]{2,1,0:T(8,128)S(1)}, f32[2,256,256]{2,1,0:T(8,128)S(1)},...) custom-call(s32[4]{0:T(128)S(1)} %pad_add_fusion.meta, ...), custom_call_target="tpu_custom_call" | custom-call | flops 4294967296 | bytes 12582912 | tf_op jit(solution)/shard_map/pallas_call | solution.py:147
  167.4 2.4 collective-permute-done.55
  169.8 2.4 collective-permute-start.46
  172.3 2.0 collective-permute-done.53
  177.2 2.8 %collective-permute-done.44.refs_5_ = bf16[2,256,256]{2,1,0:T(8,128)(2,1)S(1)} collective-permute-done((bf16[2,256,256]{2,1,0:T(8,128)(2,1)S(1)}, bf16[2,256,256]{2,1,0:T(8,128)(2,1)S(1)}, u32[]{:S(2)}, u32[]{:S(2)}) %collective-permute-start.44) | collective-permute-done | bytes 262176 | tf_op jit(solution)/shard_map/ppermute | solution.py:351
  179.9 4.0 %shard_map.76 = (f32[2,256,256]{2,1,0:T(8,128)S(1)}, bf16[2,256,256]{2,1,0:T(8,128)(2,1)S(1)}, f32[512,256]{1,0:T(8,128)S(1)}) custom-call(s32[4]{0:T(128)S(1)} %pad_add_fusion.meta, s32[64]{0:T(128)S(1)} %copy-done.10, s32[64]{0:T(128)S(1)} %copy-done.12, bf16[2,256,256]{2,1,0:T(8,128)(2,1)S(1)} %get-tuple-element.91.refs_0_, ...), custom_call_target="tpu_custom_call" | custom-call | flops 4294967296 | bytes 12582912 | tf_op jit(solution)/shard_map/pallas_call | solution.py:147
  187.7 2.8 %collective-permute-done.49 = f32[128,256]{1,0:T(8,128)S(1)} collective-permute-done((f32[128,256]{1,0:T(8,128)S(1)}, f32[128,256]{1,0:T(8,128)S(1)}, u32[]{:S(2)}, u32[]{:S(2)}) %collective-permute-start.49) | collective-permute-done | bytes 131104 | tf_op jit(solution)/shard_map/ppermute | solution.py:351
  191.8 4.5 %collective-permute-done.50 = f32[128,256]{1,0:T(8,128)S(1)} collective-permute-done((f32[128,256]{1,0:T(8,128)S(1)}, f32[128,256]{1,0:T(8,128)S(1)}, u32[]{:S(2)}, u32[]{:S(2)}) %collective-permute-start.50) | collective-permute-done | bytes 131104 | tf_op jit(solution)/shard_map/ppermute | solution.py:351
  197.2 5.9 %collective-permute-done.58.two = bf16[2,256,256]{2,1,0:T(8,128)(2,1)S(1)} collective-permute-done((bf16[2,256,256]{2,1,0:T(8,128)(2,1)S(1)}, bf16[2,256,256]{2,1,0:T(8,128)(2,1)S(1)}, u32[]{:S(2)}, u32[]{:S(2)}) %collective-permute-start.58) | collective-permute-done | bytes 262176 | tf_op jit(solution)/shard_map/ppermute | solution.py:356
  205.9 3.1 %collective-permute-start.60 = (f32[32,256]{1,0:T(8,128)S(1)}, f32[32,256]{1,0:T(8,128)S(1)}, u32[]{:S(2)}, u32[]{:S(2)}) collective-permute-start(f32[32,256]{1,0:T(8,128)S(1)} %get-tuple-element.157), channel_id=1, source_target_pairs={{0,8},{2,10},{4,12},{6,14},{8,0},{10,2},{12,4},{14,6},{16,24},{18,... | collective-permute-start | bytes 98312 | tf_op jit(solution)/shard_map/ppermute | solution.py:351
  212.9 2.7 %collective-permute-start.65 = (f32[96,256]{1,0:T(8,128)S(1)}, f32[96,256]{1,0:T(8,128)S(1)}, u32[]{:S(2)}, u32[]{:S(2)}) collective-permute-start(f32[96,256]{1,0:T(8,128)S(1)} %get-tuple-element.137), channel_id=1, source_target_pairs={{0,6},{2,4},{4,2},{6,0},{8,14},{10,12},{12,10},{14,8},{16,22},{18,... | collective-permute-start | bytes 294920 | tf_op jit(solution)/shard_map/ppermute | solution.py:351
  218.9 2.5 collective-permute-start.66
  223.4 2.9 %collective-permute-start.70 = (f32[96,256]{1,0:T(8,128)S(1)}, f32[96,256]{1,0:T(8,128)S(1)}, u32[]{:S(2)}, u32[]{:S(2)}) collective-permute-start(f32[96,256]{1,0:T(8,128)S(1)} %fusion.5), channel_id=1, source_target_pairs={{0,16},{2,18},{4,20},{6,22},{8,24},{10,26},{12,28},{14,30},{16,0},... | collective-permute-start | bytes 294920 | tf_op jit(solution)/shard_map/ppermute | solution.py:351
  232.9 2.3 collective-permute-start.75
  236.4 2.2 collective-permute-start.72
  244.9 2.0 collective-permute-done.78.refs_6_
  246.9 11.2 %shard_map.79 = (f32[512,256]{1,0:T(8,128)}, f32[512,256]{1,0:T(8,128)}) custom-call(s32[1]{0:T(128)} %bitcast.core.refs_0_, f32[256,512]{1,0:T(8,128)S(1)} %shard_map.77.mine.refs_1_, f32[256,512]{1,0:T(8,128)S(1)} %collective-permute-done.59.theirs.refs_2_, f32[256,512]{1,0:T(8,128)S(1)} %get-tuple-element.89.x.refs_3_, ...), custom_call_target="tpu_custom_call" | custom-call | flops 17179869184 | bytes 4980740 | tf_op jit(solution)/shard_map/pallas_call | solution.py:39
  (194 shorter events, 87.3 us)
Async XLA Ops:
  1.9 9.3 %collective-permute-start = (bf16[2,256,256]{2,1,0:T(8,128)(2,1)S(1)}, bf16[2,256,256]{2,1,0:T(8,128)(2,1)S(1)}, u32[]{:S(2)}, u32[]{:S(2)}) collective-permute-start(bf16[2,256,256]{2,1,0:T(8,128)(2,1)S(1)} %get-tuple-element.62.refs_0_), channel_id=1, source_target_pairs={{0,2},{2,0},{4,6},{6,4},{8,10},{10,8},{12,14},{14,12},{16,18},{18,... | collective-permute-start | bytes 786440 | tf_op jit(solution)/shard_map/ppermute | solution.py:351
  4.9 10.0 %collective-permute-start.1 = (bf16[2,256,256]{2,1,0:T(8,128)(2,1)S(1)}, bf16[2,256,256]{2,1,0:T(8,128)(2,1)S(1)}, u32[]{:S(2)}, u32[]{:S(2)}) collective-permute-start(bf16[2,256,256]{2,1,0:T(8,128)(2,1)S(1)} %get-tuple-element.62.refs_0_), channel_id=1, source_target_pairs={{0,8},{2,10},{4,12},{6,14},{8,16},{10,18},{12,20},{14,22},{16,24},... | collective-permute-start | bytes 786440 | tf_op jit(solution)/shard_map/ppermute | solution.py:356
  8.4 22.5 %collective-permute-start.7 = (f32[256,512]{1,0:T(8,128)S(1)}, f32[256,512]{1,0:T(8,128)S(1)}, u32[]{:S(2)}, u32[]{:S(2)}) collective-permute-start(f32[256,512]{1,0:T(8,128)S(1)} %get-tuple-element.60.mine.x.refs_3_), channel_id=1, source_target_pairs={{0,1},{1,0},{2,3},{3,2},{4,5},{5,4},{6,7},{7,6},{8,9},{9,8},{10,11... | collective-permute-start | bytes 1572872 | tf_op jit(solution)/shard_map/ppermute | solution.py:347
  11.2 16.3 %collective-permute-start.3 = (bf16[2,256,256]{2,1,0:T(8,128)(2,1)S(1)}, bf16[2,256,256]{2,1,0:T(8,128)(2,1)S(1)}, u32[]{:S(2)}, u32[]{:S(2)}) collective-permute-start(bf16[2,256,256]{2,1,0:T(8,128)(2,1)S(1)} %get-tuple-element.62.refs_0_), channel_id=1, source_target_pairs={{0,4},{2,6},{8,12},{10,14},{4,16},{6,18},{16,20},{18,22},{12,24},{... | collective-permute-start | bytes 786440 | tf_op jit(solution)/shard_map/ppermute | solution.py:362
  14.9 12.6 %collective-permute-start.2 = (bf16[2,256,256]{2,1,0:T(8,128)(2,1)S(1)}, bf16[2,256,256]{2,1,0:T(8,128)(2,1)S(1)}, u32[]{:S(2)}, u32[]{:S(2)}) collective-permute-start(bf16[2,256,256]{2,1,0:T(8,128)(2,1)S(1)} %collective-permute-done.1.refs_2_), channel_id=1, source_target_pairs={{0,2},{2,0},{4,6},{6,4},{8,10},{10,8},{12,14},{14,12},{16,18},{18,... | collective-permute-start | bytes 786440 | tf_op jit(solution)/shard_map/ppermute | solution.py:351
  16.4 11.0 %collective-permute-start.5 = (bf16[2,256,256]{2,1,0:T(8,128)(2,1)S(1)}, bf16[2,256,256]{2,1,0:T(8,128)(2,1)S(1)}, u32[]{:S(2)}, u32[]{:S(2)}) collective-permute-start(bf16[2,256,256]{2,1,0:T(8,128)(2,1)S(1)} %collective-permute-done.1.refs_2_), channel_id=1, source_target_pairs={{0,4},{2,6},{4,0},{6,2},{8,12},{10,14},{12,8},{14,10},{16,20},{18,... | collective-permute-start | bytes 786440 | tf_op jit(solution)/shard_map/ppermute | solution.py:351
  28.9 9.6 %collective-permute-start.15 = (bf16[2,256,256]{2,1,0:T(8,128)(2,1)}, bf16[2,256,256]{2,1,0:T(8,128)(2,1)}, u32[]{:S(2)}, u32[]{:S(2)}) collective-permute-start(bf16[2,256,256]{2,1,0:T(8,128)(2,1)} %get-tuple-element.75), channel_id=1, source_target_pairs={{0,4},{2,6},{4,0},{6,2},{8,12},{10,14},{12,8},{14,10},{16,20},{18,... | collective-permute-start | bytes 786440 | tf_op jit(solution)/shard_map/ppermute | solution.py:351
  28.9 12.4 %collective-permute-start.8 = (bf16[2,256,256]{2,1,0:T(8,128)(2,1)S(1)}, bf16[2,256,256]{2,1,0:T(8,128)(2,1)S(1)}, u32[]{:S(2)}, u32[]{:S(2)}) collective-permute-start(bf16[2,256,256]{2,1,0:T(8,128)(2,1)S(1)} %collective-permute-done.refs_1_), channel_id=1, source_target_pairs={{0,1},{1,0},{2,3},{3,2},{4,5},{5,4},{6,7},{7,6},{8,9},{9,8},{10,11... | collective-permute-start | bytes 786440 | tf_op jit(solution)/shard_map/ppermute | solution.py:347
  28.9 29.6 %collective-permute-start.17 = (bf16[2,256,256]{2,1,0:T(8,128)(2,1)}, bf16[2,256,256]{2,1,0:T(8,128)(2,1)S(1)}, u32[]{:S(2)}, u32[]{:S(2)}) collective-permute-start(bf16[2,256,256]{2,1,0:T(8,128)(2,1)} %copy-done.1), channel_id=1, source_target_pairs={{0,4},{2,6},{4,0},{6,2},{8,12},{10,14},{12,8},{14,10},{16,20},{18,... | collective-permute-start | bytes 786440 | tf_op jit(solution)/shard_map/ppermute | solution.py:351
  30.9 9.4 %collective-permute-start.13 = (bf16[2,256,256]{2,1,0:T(8,128)(2,1)}, bf16[2,256,256]{2,1,0:T(8,128)(2,1)S(1)}, u32[]{:S(2)}, u32[]{:S(2)}) collective-permute-start(bf16[2,256,256]{2,1,0:T(8,128)(2,1)} %copy-done.8), channel_id=1, source_target_pairs={{0,2},{2,0},{4,6},{6,4},{8,10},{10,8},{12,14},{14,12},{16,18},{18,... | collective-permute-start | bytes 786440 | tf_op jit(solution)/shard_map/ppermute | solution.py:351
  30.9 15.0 %collective-permute-start.4 = (bf16[2,256,256]{2,1,0:T(8,128)(2,1)}, bf16[2,256,256]{2,1,0:T(8,128)(2,1)S(1)}, u32[]{:S(2)}, u32[]{:S(2)}) collective-permute-start(bf16[2,256,256]{2,1,0:T(8,128)(2,1)} %copy-done.2), channel_id=1, source_target_pairs={{0,2},{2,0},{4,6},{6,4},{8,10},{10,8},{12,14},{14,12},{16,18},{18,... | collective-permute-start | bytes 786440 | tf_op jit(solution)/shard_map/ppermute | solution.py:351
  38.4 10.1 %collective-permute-start.6 = (bf16[2,256,256]{2,1,0:T(8,128)(2,1)}, bf16[2,256,256]{2,1,0:T(8,128)(2,1)S(1)}, u32[]{:S(2)}, u32[]{:S(2)}) collective-permute-start(bf16[2,256,256]{2,1,0:T(8,128)(2,1)} %copy-done.4), channel_id=1, source_target_pairs={{0,4},{2,6},{4,0},{6,2},{8,12},{10,14},{12,8},{14,10},{16,20},{18,... | collective-permute-start | bytes 786440 | tf_op jit(solution)/shard_map/ppermute | solution.py:351
  40.3 21.7 %collective-permute-start.16 = (bf16[2,256,256]{2,1,0:T(8,128)(2,1)S(1)}, bf16[2,256,256]{2,1,0:T(8,128)(2,1)S(1)}, u32[]{:S(2)}, u32[]{:S(2)}) collective-permute-start(bf16[2,256,256]{2,1,0:T(8,128)(2,1)S(1)} %add_convert_fusion.4), channel_id=1, source_target_pairs={{0,2},{2,0},{4,6},{6,4},{8,10},{10,8},{12,14},{14,12},{16,18},{18,... | collective-permute-start | bytes 786440 | tf_op jit(solution)/shard_map/ppermute | solution.py:351
  41.3 31.3 %collective-permute-start.14 = (bf16[2,256,256]{2,1,0:T(8,128)(2,1)}, bf16[2,256,256]{2,1,0:T(8,128)(2,1)S(1)}, u32[]{:S(2)}, u32[]{:S(2)}) collective-permute-start(bf16[2,256,256]{2,1,0:T(8,128)(2,1)} %add_convert_fusion.5), channel_id=1, source_target_pairs={{4,0},{6,2},{12,8},{14,10},{16,4},{18,6},{20,16},{22,18},{24,12},{... | collective-permute-start | bytes 786440 | tf_op jit(solution)/shard_map/ppermute | solution.py:362
  58.5 7.3 %collective-permute-start.10 = (f32[224,256]{1,0:T(8,128)S(1)}, f32[224,256]{1,0:T(8,128)S(1)}, u32[]{:S(2)}, u32[]{:S(2)}) collective-permute-start(f32[224,256]{1,0:T(8,128)S(1)} %get-tuple-element.124), channel_id=1, source_target_pairs={{0,4},{2,6},{4,0},{6,2},{8,12},{10,14},{12,8},{14,10},{16,20},{18,... | collective-permute-start | bytes 688136 | tf_op jit(solution)/shard_map/ppermute | solution.py:351
  58.5 9.8 %collective-permute-start.11 = (f32[224,256]{1,0:T(8,128)}, f32[224,256]{1,0:T(8,128)}, u32[]{:S(2)}, u32[]{:S(2)}) collective-permute-start(f32[224,256]{1,0:T(8,128)} %get-tuple-element.123), channel_id=1, source_target_pairs={{0,6},{2,4},{4,2},{6,0},{8,14},{10,12},{12,10},{14,8},{16,22},{18,... | collective-permute-start | bytes 688136 | tf_op jit(solution)/shard_map/ppermute | solution.py:351
  58.5 12.8 %collective-permute-start.9 = (f32[224,256]{1,0:T(8,128)}, f32[224,256]{1,0:T(8,128)}, u32[]{:S(2)}, u32[]{:S(2)}) collective-permute-start(f32[224,256]{1,0:T(8,128)} %get-tuple-element.122), channel_id=1, source_target_pairs={{0,2},{2,0},{4,6},{6,4},{8,10},{10,8},{12,14},{14,12},{16,18},{18,... | collective-permute-start | bytes 688136 | tf_op jit(solution)/shard_map/ppermute | solution.py:351
  62.0 12.1 %collective-permute-start.12 = (bf16[2,256,256]{2,1,0:T(8,128)(2,1)S(1)}, bf16[2,256,256]{2,1,0:T(8,128)(2,1)S(1)}, u32[]{:S(2)}, u32[]{:S(2)}) collective-permute-start(bf16[2,256,256]{2,1,0:T(8,128)(2,1)S(1)} %get-tuple-element.67), channel_id=1, source_target_pairs={{0,2},{2,0},{4,6},{6,4},{8,10},{10,8},{12,14},{14,12},{16,18},{18,... | collective-permute-start | bytes 786440 | tf_op jit(solution)/shard_map/ppermute | solution.py:351
  65.8 10.2 %collective-permute-start.18 = (bf16[2,256,256]{2,1,0:T(8,128)(2,1)S(1)}, bf16[2,256,256]{2,1,0:T(8,128)(2,1)S(1)}, u32[]{:S(2)}, u32[]{:S(2)}) collective-permute-start(bf16[2,256,256]{2,1,0:T(8,128)(2,1)S(1)} %add_convert_fusion.3), channel_id=1, source_target_pairs={{8,0},{10,2},{12,4},{14,6},{16,8},{18,10},{20,12},{22,14},{24,16},... | collective-permute-start | bytes 786440 | tf_op jit(solution)/shard_map/ppermute | solution.py:356
  78.8 9.4 %collective-permute-start.20 = (f32[56,256]{1,0:T(8,128)S(1)}, f32[56,256]{1,0:T(8,128)S(1)}, u32[]{:S(2)}, u32[]{:S(2)}) collective-permute-start(f32[56,256]{1,0:T(8,128)S(1)} %get-tuple-element.150), channel_id=1, source_target_pairs={{0,8},{2,10},{4,12},{6,14},{8,0},{10,2},{12,4},{14,6},{16,24},{18,... | collective-permute-start | bytes 172040 | tf_op jit(solution)/shard_map/ppermute | solution.py:351
  94.0 8.6 %collective-permute-start.26 = (f32[56,256]{1,0:T(8,128)S(1)}, f32[56,256]{1,0:T(8,128)S(1)}, u32[]{:S(2)}, u32[]{:S(2)}) collective-permute-start(f32[56,256]{1,0:T(8,128)S(1)} %fusion.9), channel_id=1, source_target_pairs={{0,24},{2,26},{4,28},{6,30},{8,16},{10,18},{12,20},{14,22},{16,8},... | collective-permute-start | bytes 172040 | tf_op jit(solution)/shard_map/ppermute | solution.py:351
  97.7 7.3 %collective-permute-start.27 = (f32[56,256]{1,0:T(8,128)S(1)}, f32[56,256]{1,0:T(8,128)S(1)}, u32[]{:S(2)}, u32[]{:S(2)}) collective-permute-start(f32[56,256]{1,0:T(8,128)S(1)} %fusion.9), channel_id=1, source_target_pairs={{0,16},{2,18},{4,20},{6,22},{8,24},{10,26},{12,28},{14,30},{16,0},... | collective-permute-start | bytes 172040 | tf_op jit(solution)/shard_map/ppermute | solution.py:351
  97.7 7.3 %collective-permute-start.28 = (f32[56,256]{1,0:T(8,128)S(1)}, f32[56,256]{1,0:T(8,128)S(1)}, u32[]{:S(2)}, u32[]{:S(2)}) collective-permute-start(f32[56,256]{1,0:T(8,128)S(1)} %fusion.9), channel_id=1, source_target_pairs={{0,8},{2,10},{4,12},{6,14},{8,0},{10,2},{12,4},{14,6},{16,24},{18,... | collective-permute-start | bytes 172040 | tf_op jit(solution)/shard_map/ppermute | solution.py:351
  98.5 7.5 %collective-permute-start.29 = (f32[96,256]{1,0:T(8,128)S(1)}, f32[96,256]{1,0:T(8,128)S(1)}, u32[]{:S(2)}, u32[]{:S(2)}) collective-permute-start(f32[96,256]{1,0:T(8,128)S(1)} %fusion.7), channel_id=1, source_target_pairs={{0,8},{2,10},{4,12},{6,14},{8,0},{10,2},{12,4},{14,6},{16,24},{18,... | collective-permute-start | bytes 294920 | tf_op jit(solution)/shard_map/ppermute | solution.py:351
  99.7 8.4 %collective-permute-start.30 = (f32[96,256]{1,0:T(8,128)S(1)}, f32[96,256]{1,0:T(8,128)S(1)}, u32[]{:S(2)}, u32[]{:S(2)}) collective-permute-start(f32[96,256]{1,0:T(8,128)S(1)} %fusion.7), channel_id=1, source_target_pairs={{0,16},{2,18},{4,20},{6,22},{8,24},{10,26},{12,28},{14,30},{16,0},... | collective-permute-start | bytes 294920 | tf_op jit(solution)/shard_map/ppermute | solution.py:351
  112.7 9.1 %collective-permute-start.32 = (f32[224,256]{1,0:T(8,128)S(1)}, f32[224,256]{1,0:T(8,128)S(1)}, u32[]{:S(2)}, u32[]{:S(2)}) collective-permute-start(f32[224,256]{1,0:T(8,128)S(1)} %pad_maximum_fusion.5), channel_id=1, source_target_pairs={{0,6},{2,4},{4,2},{6,0},{8,14},{10,12},{12,10},{14,8},{16,22},{18,... | collective-permute-start | bytes 688136 | tf_op jit(solution)/shard_map/ppermute | solution.py:351
  115.3 8.8 %collective-permute-start.33 = (f32[224,256]{1,0:T(8,128)S(1)}, f32[224,256]{1,0:T(8,128)S(1)}, u32[]{:S(2)}, u32[]{:S(2)}) collective-permute-start(f32[224,256]{1,0:T(8,128)S(1)} %pad_maximum_fusion.5), channel_id=1, source_target_pairs={{0,4},{2,6},{4,0},{6,2},{8,12},{10,14},{12,8},{14,10},{16,20},{18,... | collective-permute-start | bytes 688136 | tf_op jit(solution)/shard_map/ppermute | solution.py:351
  115.9 8.2 %collective-permute-start.34 = (f32[224,256]{1,0:T(8,128)S(1)}, f32[224,256]{1,0:T(8,128)S(1)}, u32[]{:S(2)}, u32[]{:S(2)}) collective-permute-start(f32[224,256]{1,0:T(8,128)S(1)} %pad_maximum_fusion.5), channel_id=1, source_target_pairs={{0,2},{2,0},{4,6},{6,4},{8,10},{10,8},{12,14},{14,12},{16,18},{18,... | collective-permute-start | bytes 688136 | tf_op jit(solution)/shard_map/ppermute | solution.py:351
  140.6 8.4 %collective-permute-start.40 = (bf16[2,256,256]{2,1,0:T(8,128)(2,1)S(1)}, bf16[2,256,256]{2,1,0:T(8,128)(2,1)S(1)}, u32[]{:S(2)}, u32[]{:S(2)}) collective-permute-start(bf16[2,256,256]{2,1,0:T(8,128)(2,1)S(1)} %get-tuple-element.91.refs_0_), channel_id=1, source_target_pairs={{0,2},{2,0},{4,6},{6,4},{8,10},{10,8},{12,14},{14,12},{16,18},{18,... | collective-permute-start | bytes 786440 | tf_op jit(solution)/shard_map/ppermute | solution.py:351
  141.8 10.6 %collective-permute-start.41 = (bf16[2,256,256]{2,1,0:T(8,128)(2,1)S(1)}, bf16[2,256,256]{2,1,0:T(8,128)(2,1)S(1)}, u32[]{:S(2)}, u32[]{:S(2)}) collective-permute-start(bf16[2,256,256]{2,1,0:T(8,128)(2,1)S(1)} %get-tuple-element.91.refs_0_), channel_id=1, source_target_pairs={{0,8},{2,10},{4,12},{6,14},{8,16},{10,18},{12,20},{14,22},{16,24},... | collective-permute-start | bytes 786440 | tf_op jit(solution)/shard_map/ppermute | solution.py:356
  149.0 13.0 %collective-permute-start.43 = (bf16[2,256,256]{2,1,0:T(8,128)(2,1)S(1)}, bf16[2,256,256]{2,1,0:T(8,128)(2,1)S(1)}, u32[]{:S(2)}, u32[]{:S(2)}) collective-permute-start(bf16[2,256,256]{2,1,0:T(8,128)(2,1)S(1)} %get-tuple-element.91.refs_0_), channel_id=1, source_target_pairs={{0,4},{2,6},{8,12},{10,14},{4,16},{6,18},{16,20},{18,22},{12,24},{... | collective-permute-start | bytes 786440 | tf_op jit(solution)/shard_map/ppermute | solution.py:362
  152.5 9.6 %collective-permute-start.42 = (bf16[2,256,256]{2,1,0:T(8,128)(2,1)S(1)}, bf16[2,256,256]{2,1,0:T(8,128)(2,1)S(1)}, u32[]{:S(2)}, u32[]{:S(2)}) collective-permute-start(bf16[2,256,256]{2,1,0:T(8,128)(2,1)S(1)} %collective-permute-done.41.refs_2_), channel_id=1, source_target_pairs={{0,2},{2,0},{4,6},{6,4},{8,10},{10,8},{12,14},{14,12},{16,18},{18,... | collective-permute-start | bytes 786440 | tf_op jit(solution)/shard_map/ppermute | solution.py:351
  153.8 9.6 %collective-permute-start.45 = (bf16[2,256,256]{2,1,0:T(8,128)(2,1)S(1)}, bf16[2,256,256]{2,1,0:T(8,128)(2,1)S(1)}, u32[]{:S(2)}, u32[]{:S(2)}) collective-permute-start(bf16[2,256,256]{2,1,0:T(8,128)(2,1)S(1)} %collective-permute-done.41.refs_2_), channel_id=1, source_target_pairs={{0,4},{2,6},{4,0},{6,2},{8,12},{10,14},{12,8},{14,10},{16,20},{18,... | collective-permute-start | bytes 786440 | tf_op jit(solution)/shard_map/ppermute | solution.py:351
  165.2 9.5 %collective-permute-start.47 = (f32[256,512]{1,0:T(8,128)S(1)}, f32[256,512]{1,0:T(8,128)S(1)}, u32[]{:S(2)}, u32[]{:S(2)}) collective-permute-start(f32[256,512]{1,0:T(8,128)S(1)} %get-tuple-element.89.x.refs_3_), channel_id=1, source_target_pairs={{0,1},{1,0},{2,3},{3,2},{4,5},{5,4},{6,7},{7,6},{8,9},{9,8},{10,11... | collective-permute-start | bytes 1572872 | tf_op jit(solution)/shard_map/ppermute | solution.py:347
  165.2 9.1 %collective-permute-start.53 = (bf16[2,256,256]{2,1,0:T(8,128)(2,1)S(1)}, bf16[2,256,256]{2,1,0:T(8,128)(2,1)S(1)}, u32[]{:S(2)}, u32[]{:S(2)}) collective-permute-start(bf16[2,256,256]{2,1,0:T(8,128)(2,1)S(1)} %get-tuple-element.101), channel_id=1, source_target_pairs={{0,2},{2,0},{4,6},{6,4},{8,10},{10,8},{12,14},{14,12},{16,18},{18,... | collective-permute-start | bytes 786440 | tf_op jit(solution)/shard_map/ppermute | solution.py:351
  166.3 9.5 %collective-permute-start.48 = (bf16[2,256,256]{2,1,0:T(8,128)(2,1)S(1)}, bf16[2,256,256]{2,1,0:T(8,128)(2,1)S(1)}, u32[]{:S(2)}, u32[]{:S(2)}) collective-permute-start(bf16[2,256,256]{2,1,0:T(8,128)(2,1)S(1)} %collective-permute-done.40.refs_1_), channel_id=1, source_target_pairs={{0,1},{1,0},{2,3},{3,2},{4,5},{5,4},{6,7},{7,6},{8,9},{9,8},{10,11... | collective-permute-start | bytes 786440 | tf_op jit(solution)/shard_map/ppermute | solution.py:347
  166.6 13.3 %collective-permute-start.44 = (bf16[2,256,256]{2,1,0:T(8,128)(2,1)S(1)}, bf16[2,256,256]{2,1,0:T(8,128)(2,1)S(1)}, u32[]{:S(2)}, u32[]{:S(2)}) collective-permute-start(bf16[2,256,256]{2,1,0:T(8,128)(2,1)S(1)} %collective-permute-done.43.refs_4_), channel_id=1, source_target_pairs={{0,2},{2,0},{4,6},{6,4},{8,10},{10,8},{12,14},{14,12},{16,18},{18,... | collective-permute-start | bytes 786440 | tf_op jit(solution)/shard_map/ppermute | solution.py:351
  169.8 10.1 %collective-permute-start.46 = (bf16[2,256,256]{2,1,0:T(8,128)(2,1)S(1)}, bf16[2,256,256]{2,1,0:T(8,128)(2,1)S(1)}, u32[]{:S(2)}, u32[]{:S(2)}) collective-permute-start(bf16[2,256,256]{2,1,0:T(8,128)(2,1)S(1)} %collective-permute-done.42.refs_3_), channel_id=1, source_target_pairs={{0,4},{2,6},{4,0},{6,2},{8,12},{10,14},{12,8},{14,10},{16,20},{18,... | collective-permute-start | bytes 786440 | tf_op jit(solution)/shard_map/ppermute | solution.py:351
  174.3 11.7 %collective-permute-start.57 = (bf16[2,256,256]{2,1,0:T(8,128)(2,1)S(1)}, bf16[2,256,256]{2,1,0:T(8,128)(2,1)S(1)}, u32[]{:S(2)}, u32[]{:S(2)}) collective-permute-start(bf16[2,256,256]{2,1,0:T(8,128)(2,1)S(1)} %get-tuple-element.105), channel_id=1, source_target_pairs={{0,4},{2,6},{4,0},{6,2},{8,12},{10,14},{12,8},{14,10},{16,20},{18,... | collective-permute-start | bytes 786440 | tf_op jit(solution)/shard_map/ppermute | solution.py:351
  174.6 12.9 %collective-permute-start.56 = (bf16[2,256,256]{2,1,0:T(8,128)(2,1)S(1)}, bf16[2,256,256]{2,1,0:T(8,128)(2,1)S(1)}, u32[]{:S(2)}, u32[]{:S(2)}) collective-permute-start(bf16[2,256,256]{2,1,0:T(8,128)(2,1)S(1)} %add_convert_fusion.1), channel_id=1, source_target_pairs={{0,2},{2,0},{4,6},{6,4},{8,10},{10,8},{12,14},{14,12},{16,18},{18,... | collective-permute-start | bytes 786440 | tf_op jit(solution)/shard_map/ppermute | solution.py:351
  175.9 20.5 %collective-permute-start.54 = (bf16[2,256,256]{2,1,0:T(8,128)(2,1)S(1)}, bf16[2,256,256]{2,1,0:T(8,128)(2,1)S(1)}, u32[]{:S(2)}, u32[]{:S(2)}) collective-permute-start(bf16[2,256,256]{2,1,0:T(8,128)(2,1)S(1)} %add_convert_fusion.2), channel_id=1, source_target_pairs={{4,0},{6,2},{12,8},{14,10},{16,4},{18,6},{20,16},{22,18},{24,12},{... | collective-permute-start | bytes 786440 | tf_op jit(solution)/shard_map/ppermute | solution.py:362
  184.1 12.2 %collective-permute-start.50 = (f32[128,256]{1,0:T(8,128)S(1)}, f32[128,256]{1,0:T(8,128)S(1)}, u32[]{:S(2)}, u32[]{:S(2)}) collective-permute-start(f32[128,256]{1,0:T(8,128)S(1)} %get-tuple-element.131), channel_id=1, source_target_pairs={{0,4},{2,6},{4,0},{6,2},{8,12},{10,14},{12,8},{14,10},{16,20},{18,... | collective-permute-start | bytes 393224 | tf_op jit(solution)/shard_map/ppermute | solution.py:351
  186.0 10.3 %collective-permute-start.51 = (f32[128,256]{1,0:T(8,128)S(1)}, f32[128,256]{1,0:T(8,128)S(1)}, u32[]{:S(2)}, u32[]{:S(2)}) collective-permute-start(f32[128,256]{1,0:T(8,128)S(1)} %get-tuple-element.130), channel_id=1, source_target_pairs={{0,6},{2,4},{4,2},{6,0},{8,14},{10,12},{12,10},{14,8},{16,22},{18,... | collective-permute-start | bytes 393224 | tf_op jit(solution)/shard_map/ppermute | solution.py:351
  187.5 9.7 %collective-permute-start.52 = (bf16[2,256,256]{2,1,0:T(8,128)(2,1)S(1)}, bf16[2,256,256]{2,1,0:T(8,128)(2,1)S(1)}, u32[]{:S(2)}, u32[]{:S(2)}) collective-permute-start(bf16[2,256,256]{2,1,0:T(8,128)(2,1)S(1)} %get-tuple-element.96), channel_id=1, source_target_pairs={{0,2},{2,0},{4,6},{6,4},{8,10},{10,8},{12,14},{14,12},{16,18},{18,... | collective-permute-start | bytes 786440 | tf_op jit(solution)/shard_map/ppermute | solution.py:351
  190.5 12.6 %collective-permute-start.58 = (bf16[2,256,256]{2,1,0:T(8,128)(2,1)S(1)}, bf16[2,256,256]{2,1,0:T(8,128)(2,1)S(1)}, u32[]{:S(2)}, u32[]{:S(2)}) collective-permute-start(bf16[2,256,256]{2,1,0:T(8,128)(2,1)S(1)} %add_convert_fusion), channel_id=1, source_target_pairs={{8,0},{10,2},{12,4},{14,6},{16,8},{18,10},{20,12},{22,14},{24,16},... | collective-permute-start | bytes 786440 | tf_op jit(solution)/shard_map/ppermute | solution.py:356
  205.9 7.0 %collective-permute-start.60 = (f32[32,256]{1,0:T(8,128)S(1)}, f32[32,256]{1,0:T(8,128)S(1)}, u32[]{:S(2)}, u32[]{:S(2)}) collective-permute-start(f32[32,256]{1,0:T(8,128)S(1)} %get-tuple-element.157), channel_id=1, source_target_pairs={{0,8},{2,10},{4,12},{6,14},{8,0},{10,2},{12,4},{14,6},{16,24},{18,... | collective-permute-start | bytes 98312 | tf_op jit(solution)/shard_map/ppermute | solution.py:351
  218.9 7.5 %collective-permute-start.66 = (f32[32,256]{1,0:T(8,128)S(1)}, f32[32,256]{1,0:T(8,128)S(1)}, u32[]{:S(2)}, u32[]{:S(2)}) collective-permute-start(f32[32,256]{1,0:T(8,128)S(1)} %fusion.11), channel_id=1, source_target_pairs={{0,24},{2,26},{4,28},{6,30},{8,16},{10,18},{12,20},{14,22},{16,8},... | collective-permute-start | bytes 98312 | tf_op jit(solution)/shard_map/ppermute | solution.py:351
  223.4 7.8 %collective-permute-start.70 = (f32[96,256]{1,0:T(8,128)S(1)}, f32[96,256]{1,0:T(8,128)S(1)}, u32[]{:S(2)}, u32[]{:S(2)}) collective-permute-start(f32[96,256]{1,0:T(8,128)S(1)} %fusion.5), channel_id=1, source_target_pairs={{0,16},{2,18},{4,20},{6,22},{8,24},{10,26},{12,28},{14,30},{16,0},... | collective-permute-start | bytes 294920 | tf_op jit(solution)/shard_map/ppermute | solution.py:351
  (50 other events, 271.1 us)
where the time goes:
time: 261 us; the launch traced here: 258 us
  starting transfers between devices  112 us (43%)
  waiting for transfers between devices  84.4 us (32%)
  Pallas kernels  42.8 us (16%)
  local copies, waits for them, and re-layouts  12.7 us (5%)
  other arithmetic  4.07 us (2%)
    ppermute x62, starting transfers between devices, flip(): lax.ppermute(a, 'patch', [(i, i ^ mask) for i in range(lax.axis_size('pat...  90.1 us
    ppermute x62, waiting for transfers between devices, flip(): lax.ppermute(a, 'patch', [(i, i ^ mask) for i in range(lax.axis_size('pat...  67.8 us
    pallas_call x8, Pallas kernels, call(): pl.pallas_call(kernel, out_shape=out, in_specs=[pl.BlockSpec(memory_space...  26.8 us
    pallas_call x4, Pallas kernels, tiles_call(): pl.pallas_call(kernel, in_specs=[pl.BlockSpec(memory_space=SMEM)] * 3 + [...  16 us
    unnamed x36, local copies, waits for them, and re-layouts  11.7 us
    ppermute x4, starting transfers between devices, shift(): lax.ppermute(a, 'patch', [(i - 2 * pairs, i) for i in devices if i - 2 *...  11.3 us
    ppermute x4, starting transfers between devices, stride(): lax.ppermute(a, 'patch', [(d, s) if back else (s, d) for s, d in route if...  9.24 us
    ppermute x4, waiting for transfers between devices, shift(): lax.ppermute(a, 'patch', [(i - 2 * pairs, i) for i in devices if i - 2 *...  8.33 us
  transfers between devices with their start and end apart: 80, of which 48 were waited for; matrix products, arithmetic and copies ran while one was open for 2% of the time, Pallas kernels for 6%

commit v1 on v0

--- a/solution.py
+++ b/solution.py
@@ -295,7 +295,7 @@
     out[pl.ds(0, width), pl.ds(width, width)] = below.T
 
 
-def factor_kernel(rows_total, first_step, last, core, v, v_other, x, x_other, gram, gram_other, inner, inner_other, *refs):
+def factor_kernel(rows_total, first_step, last, core, v, v_other, x, x_other, sums, sums_other, *refs):
     out, (g, w, high, low, update, rayleigh) = refs[:-6], refs[-6:]
     width, count = v.shape
     ahead = core[0] == 0
@@ -304,17 +304,23 @@
         mine, theirs = mine / rows_total, theirs / rows_total
         return jnp.where(ahead, mine, theirs), jnp.where(ahead, theirs, mine)
 
-    first, second = ordered(inner[pl.ds(0, 2 * width), :], inner_other[pl.ds(0, 2 * width), :])
+    blocks, rows, _ = sums.shape
+    cut = rows - (width + width // 2) // blocks
+
+    def joined(ref, low, high):
+        return jnp.concatenate([ref[block, pl.ds(low, high - low), :] for block in range(blocks)], axis=0)
+
+    inner, inner_other = joined(sums, 0, cut), joined(sums_other, 0, cut)
+    first, second = ordered(inner[: 2 * width], inner_other[: 2 * width])
     rayleigh[pl.ds(0, width), pl.ds(0, width)] = first[:width]
     rayleigh[pl.ds(width, width), pl.ds(width, width)] = second[:width]
     across = first[width:] + second[width:].T
     rayleigh[pl.ds(0, width), pl.ds(width, width)] = across
     rayleigh[pl.ds(width, width), pl.ds(0, width)] = across.T
-    lay_out(g, *ordered(gram[...], gram_other[...]))
+    lay_out(g, *ordered(joined(sums, cut, rows), joined(sums_other, cut, rows)))
     r = split(rayleigh[...])
     if first_step:
-        extra = pl.ds(2 * width, width + width // 2)
-        lay_out(w, *ordered(inner[extra, :], inner_other[extra, :]))
+        lay_out(w, *ordered(inner[2 * width :], inner_other[2 * width :]))
         turned = dot3(dot_nn, split(w[...]), r)
         g[...] += STEP_RATE * (turned + turned.T)
         g[...] += dot3(dot_nn, r, split(STEP_RATE**2 * turned - (2 * STEP_RATE**2) * rayleigh[...]))
@@ -400,24 +406,27 @@
     return a
 
 
-def exchange(a, stage):
+def shared(a, stage):
     radix, step = stage
-    return sum([flip(a, m * step) for m in range(1, radix)], a)
-
-
-def collect(a, stage):
+    return [a] + [flip(a, m * step) for m in range(1, radix)]
+
+
+def in_order(parts, stage):
     radix, step = stage
-    place = (lax.axis_index("patch") // step) % radix
-    return jnp.concatenate(place_order([a] + [flip(a, m * step) for m in range(1, radix)], place), axis=0)
+    return jnp.concatenate(place_order(parts, (lax.axis_index("patch") // step) % radix), axis=0)
 
 
 def sum_both(a, b, stages):
-    steps_a = [(scatter, stage) for stage in stages[1:]] + [(collect, stage) for stage in stages[::-1]]
-    steps_b = [(scatter, stage) for stage in stages[:-1]] + [(exchange, stages[-1])]
-    steps_b += [(collect, stage) for stage in stages[-2::-1]]
-    for (go_a, stage_a), (go_b, stage_b) in zip(steps_a, steps_b, strict=True):
-        a, b = together(go_a(a, stage_a), go_b(b, stage_b))
-    return a, b
+    for stage_a, stage_b in zip(stages[1:], stages[:-1], strict=True):
+        a, b = together(scatter(a, stage_a), scatter(b, stage_b))
+    cut = a.shape[0]
+    parts = shared(jnp.concatenate([a, b]), stages[-1])
+    joined = jnp.concatenate([in_order([part[:cut] for part in parts], stages[-1]), sum(part[cut:] for part in parts)])
+    blocks = 1
+    for stage in stages[-2::-1]:
+        joined = in_order(shared(joined, stage), stage)
+        blocks *= stage[0]
+    return joined.reshape(blocks, joined.shape[0] // blocks, joined.shape[1])
 
 
 def shards(vectors, blocks, block_row, block_col, block_count):
@@ -443,8 +452,9 @@
         )
         same, cross = sums[::2], sums[1::2]
         two, two_x, far, side = reach(u, own_x)
-        out_side_x, out_far, out_side = together(cross[3], cross[2], same[3], far, two_x, side)[:3]
         pieces = [u, own_x, two, two_x, far, flip(far, 1), side, flip(two_x, 2)]
+        out_side_x, out_side = together(cross[3], same[3], pieces[7])[:2]
+        out_far = together(cross[2], side, two_x)[0]
         kept, near, inner = tiles_call(
             direct_kernel,
             [shape(f32, *segment), shape(bf16, *segment), shape(f32, 2 * width, width)],
@@ -467,13 +477,13 @@
         v_other = swap_cores(v)
         (gram,) = call(gram_kernel, [shape(f32, width + width // 2, width)], [core, v, v_other], smem=1)
         inner, gram = together(inner, gram)
-        inner, gram = sum_both(inner, gram, stages)
+        sums = sum_both(inner, gram, stages)
         full = (2 * width, 2 * width)
         wide = shape(f32, count, width)
         out = call(
             lambda *refs: factor_kernel(rows_total, step == 0, last, *refs),
             [wide, wide] if last else [flat, chunk],
-            [core, v, v_other, x, x_other, gram, swap_cores(gram), inner, swap_cores(inner)],
+            [core, v, v_other, x, x_other, sums, swap_cores(sums)],
             scratch=[VMEM(full, f32), VMEM(full, f32), VMEM(full, bf16), VMEM(full, bf16)]
             + [VMEM((2 * width, count), f32), VMEM(full, f32)],
             smem=1,

time: 261 us -> 267 us (1.023)
  waiting for transfers between devices: 84.4 us -> 110 us
  Pallas kernels: 42.8 us -> 35.2 us
  starting transfers between devices: 112 us -> 106 us
  local copies, waits for them, and re-layouts: 12.7 us -> 7.17 us
    ppermute x62 -> x50, waiting for transfers between devices: 67.8 us -> 85.2 us  [flip(): lax.ppermute(a, 'patch', [(i, i ^ mask) for i in range(lax.axis_size('pat...]
    pallas_call x4, Pallas kernels: 16 us -> 8.49 us  [tiles_call(): pl.pallas_call(kernel, in_specs=[pl.BlockSpec(memory_space=SMEM)] * 3 + [...]
    ppermute x4, waiting for transfers between devices: 8.33 us -> 15.5 us  [shift(): lax.ppermute(a, 'patch', [(i - 2 * pairs, i) for i in devices if i - 2 *...]
    unnamed x36 -> x40, local copies, waits for them, and re-layouts: 11.7 us -> 6.1 us
    ppermute x62 -> x50, starting transfers between devices: 90.1 us -> 86.8 us  [flip(): lax.ppermute(a, 'patch', [(i, i ^ mask) for i in range(lax.axis_size('pat...]
    ppermute x10 -> x8, waiting for transfers between devices: 8.25 us -> 9.24 us  [swap_cores(): return lax.ppermute(a, 'vec', [(0, 1), (1, 0)])]
  transfers between devices with their start and end apart: 80 -> 66, of which waited for: 48 -> 36; matrix products, arithmetic and copies ran while one was open for 2% -> 2% of each run, Pallas kernels for 6% -> 3%
where the time goes in v1:
time: 267 us; the launch traced here: 266 us
  waiting for transfers between devices  110 us (41%)
  starting transfers between devices  106 us (40%)
  Pallas kernels  35.2 us (13%)
  local copies, waits for them, and re-layouts  7.17 us (3%)
  other arithmetic  6.03 us (2%)
    ppermute x50, starting transfers between devices, flip(): lax.ppermute(a, 'patch', [(i, i ^ mask) for i in range(lax.axis_size('pat...  86.8 us
    ppermute x50, waiting for transfers between devices, flip(): lax.ppermute(a, 'patch', [(i, i ^ mask) for i in range(lax.axis_size('pat...  85.2 us
    pallas_call x8, Pallas kernels, call(): pl.pallas_call(kernel, out_shape=out, in_specs=[pl.BlockSpec(memory_space...  26.8 us
    ppermute x4, waiting for transfers between devices, shift(): lax.ppermute(a, 'patch', [(i - 2 * pairs, i) for i in devices if i - 2 *...  15.5 us
    ppermute x4, starting transfers between devices, stride(): lax.ppermute(a, 'patch', [(d, s) if back else (s, d) for s, d in route if...  9.43 us
    ppermute x4, starting transfers between devices, shift(): lax.ppermute(a, 'patch', [(i - 2 * pairs, i) for i in devices if i - 2 *...  9.33 us
    ppermute x8, waiting for transfers between devices, swap_cores(): return lax.ppermute(a, 'vec', [(0, 1), (1, 0)])  9.24 us
    pallas_call x4, Pallas kernels, tiles_call(): pl.pallas_call(kernel, in_specs=[pl.BlockSpec(memory_space=SMEM)] * 3 + [...  8.49 us
  transfers between devices with their start and end apart: 66, of which 36 were waited for; matrix products, arithmetic and copies ran while one was open for 2% of the time, Pallas kernels for 3%

profile of v1, /device:TPU:0, one launch (start us, length us, event | category | flops | bytes accessed | tf_op | source)
XLA Modules:
  0.0 266.3 jit_solution(6318243004246591526)
XLA Ops:
  1.9 4.9 %collective-permute-start.1 = (bf16[2,256,256]{2,1,0:T(8,128)(2,1)S(1)}, bf16[2,256,256]{2,1,0:T(8,128)(2,1)S(1)}, u32[]{:S(2)}, u32[]{:S(2)}) collective-permute-start(bf16[2,256,256]{2,1,0:T(8,128)(2,1)S(1)} %get-tuple-element.54.refs_0_), channel_id=1, source_target_pairs={{0,8},{2,10},{4,12},{6,14},{8,16},{10,18},{12,20},{14,22},{16,24},... | collective-permute-start | bytes 786440 | tf_op jit(solution)/shard_map/ppermute | solution.py:362
  8.4 4.0 %collective-permute-done.1.refs_2_ = bf16[2,256,256]{2,1,0:T(8,128)(2,1)S(1)} collective-permute-done((bf16[2,256,256]{2,1,0:T(8,128)(2,1)S(1)}, bf16[2,256,256]{2,1,0:T(8,128)(2,1)S(1)}, u32[]{:S(2)}, u32[]{:S(2)}) %collective-permute-start.1) | collective-permute-done | bytes 262176 | tf_op jit(solution)/shard_map/ppermute | solution.py:362
  15.4 4.1 %collective-permute-start.3 = (bf16[2,256,256]{2,1,0:T(8,128)(2,1)S(1)}, bf16[2,256,256]{2,1,0:T(8,128)(2,1)}, u32[]{:S(2)}, u32[]{:S(2)}) collective-permute-start(bf16[2,256,256]{2,1,0:T(8,128)(2,1)S(1)} %get-tuple-element.54.refs_0_), channel_id=1, source_target_pairs={{0,4},{2,6},{8,12},{10,14},{4,16},{6,18},{16,20},{18,22},{12,24},{... | collective-permute-start | bytes 786440 | tf_op jit(solution)/shard_map/ppermute | solution.py:368
  19.6 2.0 collective-permute-start.5
  23.1 2.5 shard_map.69
  28.6 2.6 collective-permute-done.5.refs_6_
  35.5 2.6 collective-permute-start.15
  38.1 2.4 collective-permute-done.13
  44.2 3.2 %shard_map.70 = (f32[2,256,256]{2,1,0:T(8,128)S(1)}, bf16[2,256,256]{2,1,0:T(8,128)(2,1)}, f32[512,256]{1,0:T(8,128)S(1)}) custom-call(s32[4]{0:T(128)S(1)} %pad_add_fusion.meta, s32[64]{0:T(128)S(1)} %copy-done.10, s32[64]{0:T(128)S(1)} %copy-done.12, bf16[2,256,256]{2,1,0:T(8,128)(2,1)S(1)} %get-tuple-element.54.refs_0_, ...), custom_call_target="tpu_custom_call" | custom-call | flops 4294967296 | bytes 12582912 | tf_op jit(solution)/shard_map/pallas_call | solution.py:147
  47.4 4.0 %collective-permute-start.16 = (bf16[2,256,256]{2,1,0:T(8,128)(2,1)S(1)}, bf16[2,256,256]{2,1,0:T(8,128)(2,1)S(1)}, u32[]{:S(2)}, u32[]{:S(2)}) collective-permute-start(bf16[2,256,256]{2,1,0:T(8,128)(2,1)S(1)} %add_convert_fusion.4), channel_id=1, source_target_pairs={{0,2},{2,0},{4,6},{6,4},{8,10},{10,8},{12,14},{14,12},{16,18},{18,... | collective-permute-start | bytes 786440 | tf_op jit(solution)/shard_map/ppermute | solution.py:357
  52.5 4.1 %collective-permute-start.10 = (f32[224,256]{1,0:T(8,128)S(1)}, f32[224,256]{1,0:T(8,128)}, u32[]{:S(2)}, u32[]{:S(2)}) collective-permute-start(f32[224,256]{1,0:T(8,128)S(1)} %get-tuple-element.112), channel_id=1, source_target_pairs={{0,4},{2,6},{4,0},{6,2},{8,12},{10,14},{12,8},{14,10},{16,20},{18,... | collective-permute-start | bytes 688136 | tf_op jit(solution)/shard_map/ppermute | solution.py:357
  59.9 6.8 %collective-permute-done.10 = f32[224,256]{1,0:T(8,128)} collective-permute-done((f32[224,256]{1,0:T(8,128)S(1)}, f32[224,256]{1,0:T(8,128)}, u32[]{:S(2)}, u32[]{:S(2)}) %collective-permute-start.10) | collective-permute-done | bytes 229408 | tf_op jit(solution)/shard_map/ppermute | solution.py:357
  72.8 3.5 %collective-permute-done.18.two = bf16[2,256,256]{2,1,0:T(8,128)(2,1)S(1)} collective-permute-done((bf16[2,256,256]{2,1,0:T(8,128)(2,1)S(1)}, bf16[2,256,256]{2,1,0:T(8,128)(2,1)S(1)}, u32[]{:S(2)}, u32[]{:S(2)}) %collective-permute-start.18) | collective-permute-done | bytes 262176 | tf_op jit(solution)/shard_map/ppermute | solution.py:362
  79.0 3.8 %collective-permute-start.20 = (f32[56,256]{1,0:T(8,128)S(1)}, f32[56,256]{1,0:T(8,128)S(1)}, u32[]{:S(2)}, u32[]{:S(2)}) collective-permute-start(f32[56,256]{1,0:T(8,128)S(1)} %get-tuple-element.122), channel_id=1, source_target_pairs={{0,8},{2,10},{4,12},{6,14},{8,0},{10,2},{12,4},{14,6},{16,24},{18,... | collective-permute-start | bytes 172040 | tf_op jit(solution)/shard_map/ppermute | solution.py:357
  86.0 2.0 collective-permute-start.23
  88.0 3.4 %collective-permute-start.24 = (f32[96,256]{1,0:T(8,128)S(1)}, f32[96,256]{1,0:T(8,128)S(1)}, u32[]{:S(2)}, u32[]{:S(2)}) collective-permute-start(f32[96,256]{1,0:T(8,128)S(1)} %get-tuple-element.121), channel_id=1, source_target_pairs={{0,4},{2,6},{4,0},{6,2},{8,12},{10,14},{12,8},{14,10},{16,20},{18,... | collective-permute-start | bytes 294920 | tf_op jit(solution)/shard_map/ppermute | solution.py:357
  93.0 2.0 collective-permute-done.24
  96.9 2.5 collective-permute-start.26
  101.4 4.4 %collective-permute-done.26 = f32[152,256]{1,0:T(8,128)S(1)} collective-permute-done((f32[152,256]{1,0:T(8,128)S(1)}, f32[152,256]{1,0:T(8,128)S(1)}, u32[]{:S(2)}, u32[]{:S(2)}) %collective-permute-start.26) | collective-permute-done | bytes 155680 | tf_op jit(solution)/shard_map/ppermute | solution.py:357
  105.8 6.1 %collective-permute-done.27 = f32[152,256]{1,0:T(8,128)S(1)} collective-permute-done((f32[152,256]{1,0:T(8,128)S(1)}, f32[152,256]{1,0:T(8,128)S(1)}, u32[]{:S(2)}, u32[]{:S(2)}) %collective-permute-start.27) | collective-permute-done | bytes 155680 | tf_op jit(solution)/shard_map/ppermute | solution.py:357
  115.5 8.1 %collective-permute-done.29 = f32[320,256]{1,0:T(8,128)S(1)} collective-permute-done((f32[320,256]{1,0:T(8,128)S(1)}, f32[320,256]{1,0:T(8,128)S(1)}, u32[]{:S(2)}, u32[]{:S(2)}) %collective-permute-start.29) | collective-permute-done | bytes 327712 | tf_op jit(solution)/shard_map/ppermute | solution.py:357
  123.6 4.5 %collective-permute-done.30 = f32[320,256]{1,0:T(8,128)S(1)} collective-permute-done((f32[320,256]{1,0:T(8,128)S(1)}, f32[320,256]{1,0:T(8,128)S(1)}, u32[]{:S(2)}, u32[]{:S(2)}) %collective-permute-start.30) | collective-permute-done | bytes 327712 | tf_op jit(solution)/shard_map/ppermute | solution.py:357
  130.1 3.0 %collective-permute-done.32.refs_6_ = f32[4,320,256]{2,1,0:T(8,128)S(1)} collective-permute-done((f32[4,320,256]{2,1,0:T(8,128)S(1)}, f32[4,320,256]{2,1,0:T(8,128)S(1)}, u32[]{:S(2)}, u32[]{:S(2)}) %collective-permute-start.32) | collective-permute-done | bytes 1310752 | tf_op jit(solution)/shard_map/ppermute | solution.py:353
  133.1 13.2 %shard_map.74 = (f32[256,512]{1,0:T(8,128)S(1)}, bf16[2,256,256]{2,1,0:T(8,128)(2,1)S(1)}) custom-call(s32[1]{0:T(128)} %bitcast.core.refs_0_, f32[256,512]{1,0:T(8,128)S(1)} %shard_map.72.mine.refs_1_, f32[256,512]{1,0:T(8,128)S(1)} %collective-permute-done.19.theirs.refs_2_, f32[256,512]{1,0:T(8,128)S(1)} %get-tuple-element.52.mine.x.refs_3_, ...), custom_call_target="tpu_custom_call" | custom-call | flops 17179869184 | bytes 5505028 | tf_op jit(solution)/shard_map/pallas_call | solution.py:39
  148.5 5.2 %collective-permute-done.34.refs_2_ = bf16[2,256,256]{2,1,0:T(8,128)(2,1)S(1)} collective-permute-done((bf16[2,256,256]{2,1,0:T(8,128)(2,1)S(1)}, bf16[2,256,256]{2,1,0:T(8,128)(2,1)S(1)}, u32[]{:S(2)}, u32[]{:S(2)}) %collective-permute-start.34) | collective-permute-done | bytes 262176 | tf_op jit(solution)/shard_map/ppermute | solution.py:362
  154.2 2.1 collective-permute-done.33.refs_1_
  156.4 2.5 collective-permute-start.36
  158.9 4.3 %collective-permute-start.38 = (bf16[2,256,256]{2,1,0:T(8,128)(2,1)S(1)}, bf16[2,256,256]{2,1,0:T(8,128)(2,1)S(1)}, u32[]{:S(2)}, u32[]{:S(2)}) collective-permute-start(bf16[2,256,256]{2,1,0:T(8,128)(2,1)S(1)} %collective-permute-done.34.refs_2_), channel_id=1, source_target_pairs={{0,4},{2,6},{4,0},{6,2},{8,12},{10,14},{12,8},{14,10},{16,20},{18,... | collective-permute-start | bytes 786440 | tf_op jit(solution)/shard_map/ppermute | solution.py:357
  164.5 5.9 %collective-permute-done.38.refs_6_ = bf16[2,256,256]{2,1,0:T(8,128)(2,1)S(1)} collective-permute-done((bf16[2,256,256]{2,1,0:T(8,128)(2,1)S(1)}, bf16[2,256,256]{2,1,0:T(8,128)(2,1)S(1)}, u32[]{:S(2)}, u32[]{:S(2)}) %collective-permute-start.38) | collective-permute-done | bytes 262176 | tf_op jit(solution)/shard_map/ppermute | solution.py:357
  170.4 2.0 collective-permute-start.46
  172.4 2.1 collective-permute-done.39.refs_7_
  174.5 2.5 collective-permute-start.48
  179.3 4.4 %collective-permute-done.48 = bf16[2,256,256]{2,1,0:T(8,128)(2,1)S(1)} collective-permute-done((bf16[2,256,256]{2,1,0:T(8,128)(2,1)S(1)}, bf16[2,256,256]{2,1,0:T(8,128)(2,1)S(1)}, u32[]{:S(2)}, u32[]{:S(2)}) %collective-permute-start.48) | collective-permute-done | bytes 262176 | tf_op jit(solution)/shard_map/ppermute | solution.py:357
  187.9 3.6 %collective-permute-start.42 = (f32[128,256]{1,0:T(8,128)S(1)}, f32[128,256]{1,0:T(8,128)S(1)}, u32[]{:S(2)}, u32[]{:S(2)}) collective-permute-start(f32[128,256]{1,0:T(8,128)S(1)} %get-tuple-element.113), channel_id=1, source_target_pairs={{0,2},{2,0},{4,6},{6,4},{8,10},{10,8},{12,14},{14,12},{16,18},{18,... | collective-permute-start | bytes 393224 | tf_op jit(solution)/shard_map/ppermute | solution.py:357
  191.5 3.8 %collective-permute-start.43 = (f32[128,256]{1,0:T(8,128)S(1)}, f32[128,256]{1,0:T(8,128)S(1)}, u32[]{:S(2)}, u32[]{:S(2)}) collective-permute-start(f32[128,256]{1,0:T(8,128)S(1)} %get-tuple-element.115), channel_id=1, source_target_pairs={{0,4},{2,6},{4,0},{6,2},{8,12},{10,14},{12,8},{14,10},{16,20},{18,... | collective-permute-start | bytes 393224 | tf_op jit(solution)/shard_map/ppermute | solution.py:357
  198.2 2.2 collective-permute-done.43
  200.5 2.2 collective-permute-done.44
  203.0 2.9 %collective-permute-done.51.two = bf16[2,256,256]{2,1,0:T(8,128)(2,1)S(1)} collective-permute-done((bf16[2,256,256]{2,1,0:T(8,128)(2,1)S(1)}, bf16[2,256,256]{2,1,0:T(8,128)(2,1)S(1)}, u32[]{:S(2)}, u32[]{:S(2)}) %collective-permute-start.51) | collective-permute-done | bytes 262176 | tf_op jit(solution)/shard_map/ppermute | solution.py:362
  208.6 6.6 %collective-permute-start.53 = (f32[32,256]{1,0:T(8,128)S(1)}, f32[32,256]{1,0:T(8,128)S(1)}, u32[]{:S(2)}, u32[]{:S(2)}) collective-permute-start(f32[32,256]{1,0:T(8,128)S(1)} %get-tuple-element.125), channel_id=1, source_target_pairs={{0,8},{2,10},{4,12},{6,14},{8,0},{10,2},{12,4},{14,6},{16,24},{18,... | collective-permute-start | bytes 98312 | tf_op jit(solution)/shard_map/ppermute | solution.py:357
  219.6 2.8 %collective-permute-start.57 = (f32[96,256]{1,0:T(8,128)S(1)}, f32[96,256]{1,0:T(8,128)S(1)}, u32[]{:S(2)}, u32[]{:S(2)}) collective-permute-start(f32[96,256]{1,0:T(8,128)S(1)} %get-tuple-element.118), channel_id=1, source_target_pairs={{0,4},{2,6},{4,0},{6,2},{8,12},{10,14},{12,8},{14,10},{16,20},{18,... | collective-permute-start | bytes 294920 | tf_op jit(solution)/shard_map/ppermute | solution.py:357
  223.1 3.0 %collective-permute-done.57 = f32[96,256]{1,0:T(8,128)S(1)} collective-permute-done((f32[96,256]{1,0:T(8,128)S(1)}, f32[96,256]{1,0:T(8,128)S(1)}, u32[]{:S(2)}, u32[]{:S(2)}) %collective-permute-start.57) | collective-permute-done | bytes 98336 | tf_op jit(solution)/shard_map/ppermute | solution.py:357
  228.0 2.5 collective-permute-start.59
  232.4 3.9 %collective-permute-done.59 = f32[128,256]{1,0:T(8,128)S(1)} collective-permute-done((f32[128,256]{1,0:T(8,128)S(1)}, f32[128,256]{1,0:T(8,128)S(1)}, u32[]{:S(2)}, u32[]{:S(2)}) %collective-permute-start.59) | collective-permute-done | bytes 131104 | tf_op jit(solution)/shard_map/ppermute | solution.py:357
  236.3 4.5 %collective-permute-done.60 = f32[128,256]{1,0:T(8,128)S(1)} collective-permute-done((f32[128,256]{1,0:T(8,128)S(1)}, f32[128,256]{1,0:T(8,128)S(1)}, u32[]{:S(2)}, u32[]{:S(2)}) %collective-permute-start.60) | collective-permute-done | bytes 131104 | tf_op jit(solution)/shard_map/ppermute | solution.py:357
  244.5 6.0 %collective-permute-done.62 = f32[224,256]{1,0:T(8,128)S(1)} collective-permute-done((f32[224,256]{1,0:T(8,128)S(1)}, f32[224,256]{1,0:T(8,128)S(1)}, u32[]{:S(2)}, u32[]{:S(2)}) %collective-permute-start.62) | collective-permute-done | bytes 229408 | tf_op jit(solution)/shard_map/ppermute | solution.py:357
  250.4 2.0 collective-permute-done.63
  252.7 2.5 collective-permute-done.65.refs_6_
  255.1 11.2 %shard_map.79 = (f32[512,256]{1,0:T(8,128)}, f32[512,256]{1,0:T(8,128)}) custom-call(s32[1]{0:T(128)} %bitcast.core.refs_0_, f32[256,512]{1,0:T(8,128)S(1)} %shard_map.77.mine.refs_1_, f32[256,512]{1,0:T(8,128)S(1)} %collective-permute-done.52.theirs.refs_2_, f32[256,512]{1,0:T(8,128)S(1)} %get-tuple-element.77.x.refs_3_, ...), custom_call_target="tpu_custom_call" | custom-call | flops 17179869184 | bytes 4980740 | tf_op jit(solution)/shard_map/pallas_call | solution.py:39
  (172 shorter events, 74.2 us)
Async XLA Ops:
  1.9 10.5 %collective-permute-start.1 = (bf16[2,256,256]{2,1,0:T(8,128)(2,1)S(1)}, bf16[2,256,256]{2,1,0:T(8,128)(2,1)S(1)}, u32[]{:S(2)}, u32[]{:S(2)}) collective-permute-start(bf16[2,256,256]{2,1,0:T(8,128)(2,1)S(1)} %get-tuple-element.54.refs_0_), channel_id=1, source_target_pairs={{0,8},{2,10},{4,12},{6,14},{8,16},{10,18},{12,20},{14,22},{16,24},... | collective-permute-start | bytes 786440 | tf_op jit(solution)/shard_map/ppermute | solution.py:362
  6.8 8.6 %collective-permute-start = (bf16[2,256,256]{2,1,0:T(8,128)(2,1)S(1)}, bf16[2,256,256]{2,1,0:T(8,128)(2,1)}, u32[]{:S(2)}, u32[]{:S(2)}) collective-permute-start(bf16[2,256,256]{2,1,0:T(8,128)(2,1)S(1)} %get-tuple-element.54.refs_0_), channel_id=1, source_target_pairs={{0,2},{2,0},{4,6},{6,4},{8,10},{10,8},{12,14},{14,12},{16,18},{18,... | collective-permute-start | bytes 786440 | tf_op jit(solution)/shard_map/ppermute | solution.py:357
  12.4 9.2 %collective-permute-start.2 = (bf16[2,256,256]{2,1,0:T(8,128)(2,1)S(1)}, bf16[2,256,256]{2,1,0:T(8,128)(2,1)S(1)}, u32[]{:S(2)}, u32[]{:S(2)}) collective-permute-start(bf16[2,256,256]{2,1,0:T(8,128)(2,1)S(1)} %collective-permute-done.1.refs_2_), channel_id=1, source_target_pairs={{0,2},{2,0},{4,6},{6,4},{8,10},{10,8},{12,14},{14,12},{16,18},{18,... | collective-permute-start | bytes 786440 | tf_op jit(solution)/shard_map/ppermute | solution.py:357
  13.8 20.3 %collective-permute-start.7 = (f32[256,512]{1,0:T(8,128)S(1)}, f32[256,512]{1,0:T(8,128)S(1)}, u32[]{:S(2)}, u32[]{:S(2)}) collective-permute-start(f32[256,512]{1,0:T(8,128)S(1)} %get-tuple-element.52.mine.x.refs_3_), channel_id=1, source_target_pairs={{0,1},{1,0},{2,3},{3,2},{4,5},{5,4},{6,7},{7,6},{8,9},{9,8},{10,11... | collective-permute-start | bytes 1572872 | tf_op jit(solution)/shard_map/ppermute | solution.py:353
  15.4 18.1 %collective-permute-start.3 = (bf16[2,256,256]{2,1,0:T(8,128)(2,1)S(1)}, bf16[2,256,256]{2,1,0:T(8,128)(2,1)}, u32[]{:S(2)}, u32[]{:S(2)}) collective-permute-start(bf16[2,256,256]{2,1,0:T(8,128)(2,1)S(1)} %get-tuple-element.54.refs_0_), channel_id=1, source_target_pairs={{0,4},{2,6},{8,12},{10,14},{4,16},{6,18},{16,20},{18,22},{12,24},{... | collective-permute-start | bytes 786440 | tf_op jit(solution)/shard_map/ppermute | solution.py:368
  19.6 11.6 %collective-permute-start.5 = (bf16[2,256,256]{2,1,0:T(8,128)(2,1)S(1)}, bf16[2,256,256]{2,1,0:T(8,128)(2,1)S(1)}, u32[]{:S(2)}, u32[]{:S(2)}) collective-permute-start(bf16[2,256,256]{2,1,0:T(8,128)(2,1)S(1)} %collective-permute-done.1.refs_2_), channel_id=1, source_target_pairs={{0,4},{2,6},{4,0},{6,2},{8,12},{10,14},{12,8},{14,10},{16,20},{18,... | collective-permute-start | bytes 786440 | tf_op jit(solution)/shard_map/ppermute | solution.py:357
  21.5 13.9 %collective-permute-start.6 = (bf16[2,256,256]{2,1,0:T(8,128)(2,1)S(1)}, bf16[2,256,256]{2,1,0:T(8,128)(2,1)}, u32[]{:S(2)}, u32[]{:S(2)}) collective-permute-start(bf16[2,256,256]{2,1,0:T(8,128)(2,1)S(1)} %collective-permute-done.2.refs_3_), channel_id=1, source_target_pairs={{0,4},{2,6},{4,0},{6,2},{8,12},{10,14},{12,8},{14,10},{16,20},{18,... | collective-permute-start | bytes 786440 | tf_op jit(solution)/shard_map/ppermute | solution.py:357
  31.9 8.6 %collective-permute-start.13 = (bf16[2,256,256]{2,1,0:T(8,128)(2,1)}, bf16[2,256,256]{2,1,0:T(8,128)(2,1)}, u32[]{:S(2)}, u32[]{:S(2)}) collective-permute-start(bf16[2,256,256]{2,1,0:T(8,128)(2,1)} %get-tuple-element.62), channel_id=1, source_target_pairs={{0,2},{2,0},{4,6},{6,4},{8,10},{10,8},{12,14},{14,12},{16,18},{18,... | collective-permute-start | bytes 786440 | tf_op jit(solution)/shard_map/ppermute | solution.py:357
  33.5 10.1 %collective-permute-start.8 = (bf16[2,256,256]{2,1,0:T(8,128)(2,1)}, bf16[2,256,256]{2,1,0:T(8,128)(2,1)S(1)}, u32[]{:S(2)}, u32[]{:S(2)}) collective-permute-start(bf16[2,256,256]{2,1,0:T(8,128)(2,1)} %collective-permute-done.refs_1_), channel_id=1, source_target_pairs={{0,1},{1,0},{2,3},{3,2},{4,5},{5,4},{6,7},{7,6},{8,9},{9,8},{10,11... | collective-permute-start | bytes 786440 | tf_op jit(solution)/shard_map/ppermute | solution.py:353
  33.6 10.6 %collective-permute-start.4 = (bf16[2,256,256]{2,1,0:T(8,128)(2,1)}, bf16[2,256,256]{2,1,0:T(8,128)(2,1)S(1)}, u32[]{:S(2)}, u32[]{:S(2)}) collective-permute-start(bf16[2,256,256]{2,1,0:T(8,128)(2,1)} %collective-permute-done.3.refs_4_), channel_id=1, source_target_pairs={{0,2},{2,0},{4,6},{6,4},{8,10},{10,8},{12,14},{14,12},{16,18},{18,... | collective-permute-start | bytes 786440 | tf_op jit(solution)/shard_map/ppermute | solution.py:357
  35.5 11.9 %collective-permute-start.15 = (bf16[2,256,256]{2,1,0:T(8,128)(2,1)S(1)}, bf16[2,256,256]{2,1,0:T(8,128)(2,1)S(1)}, u32[]{:S(2)}, u32[]{:S(2)}) collective-permute-start(bf16[2,256,256]{2,1,0:T(8,128)(2,1)S(1)} %copy-done.8), channel_id=1, source_target_pairs={{0,4},{2,6},{4,0},{6,2},{8,12},{10,14},{12,8},{14,10},{16,20},{18,... | collective-permute-start | bytes 786440 | tf_op jit(solution)/shard_map/ppermute | solution.py:357
  38.1 18.6 %collective-permute-start.17 = (bf16[2,256,256]{2,1,0:T(8,128)(2,1)S(1)}, bf16[2,256,256]{2,1,0:T(8,128)(2,1)S(1)}, u32[]{:S(2)}, u32[]{:S(2)}) collective-permute-start(bf16[2,256,256]{2,1,0:T(8,128)(2,1)S(1)} %copy-done.4), channel_id=1, source_target_pairs={{0,4},{2,6},{4,0},{6,2},{8,12},{10,14},{12,8},{14,10},{16,20},{18,... | collective-permute-start | bytes 786440 | tf_op jit(solution)/shard_map/ppermute | solution.py:357
  42.3 29.1 %collective-permute-start.14 = (bf16[2,256,256]{2,1,0:T(8,128)(2,1)}, bf16[2,256,256]{2,1,0:T(8,128)(2,1)S(1)}, u32[]{:S(2)}, u32[]{:S(2)}) collective-permute-start(bf16[2,256,256]{2,1,0:T(8,128)(2,1)} %add_convert_fusion.5), channel_id=1, source_target_pairs={{4,0},{6,2},{12,8},{14,10},{16,4},{18,6},{20,16},{22,18},{24,12},{... | collective-permute-start | bytes 786440 | tf_op jit(solution)/shard_map/ppermute | solution.py:368
  47.4 10.7 %collective-permute-start.16 = (bf16[2,256,256]{2,1,0:T(8,128)(2,1)S(1)}, bf16[2,256,256]{2,1,0:T(8,128)(2,1)S(1)}, u32[]{:S(2)}, u32[]{:S(2)}) collective-permute-start(bf16[2,256,256]{2,1,0:T(8,128)(2,1)S(1)} %add_convert_fusion.4), channel_id=1, source_target_pairs={{0,2},{2,0},{4,6},{6,4},{8,10},{10,8},{12,14},{14,12},{16,18},{18,... | collective-permute-start | bytes 786440 | tf_op jit(solution)/shard_map/ppermute | solution.py:357
  52.5 14.2 %collective-permute-start.10 = (f32[224,256]{1,0:T(8,128)S(1)}, f32[224,256]{1,0:T(8,128)}, u32[]{:S(2)}, u32[]{:S(2)}) collective-permute-start(f32[224,256]{1,0:T(8,128)S(1)} %get-tuple-element.112), channel_id=1, source_target_pairs={{0,4},{2,6},{4,0},{6,2},{8,12},{10,14},{12,8},{14,10},{16,20},{18,... | collective-permute-start | bytes 688136 | tf_op jit(solution)/shard_map/ppermute | solution.py:357
  56.6 11.6 %collective-permute-start.11 = (f32[224,256]{1,0:T(8,128)}, f32[224,256]{1,0:T(8,128)}, u32[]{:S(2)}, u32[]{:S(2)}) collective-permute-start(f32[224,256]{1,0:T(8,128)} %get-tuple-element.111), channel_id=1, source_target_pairs={{0,6},{2,4},{4,2},{6,0},{8,14},{10,12},{12,10},{14,8},{16,22},{18,... | collective-permute-start | bytes 688136 | tf_op jit(solution)/shard_map/ppermute | solution.py:357
  56.6 13.4 %collective-permute-start.9 = (f32[224,256]{1,0:T(8,128)}, f32[224,256]{1,0:T(8,128)}, u32[]{:S(2)}, u32[]{:S(2)}) collective-permute-start(f32[224,256]{1,0:T(8,128)} %get-tuple-element.110), channel_id=1, source_target_pairs={{0,2},{2,0},{4,6},{6,4},{8,10},{10,8},{12,14},{14,12},{16,18},{18,... | collective-permute-start | bytes 688136 | tf_op jit(solution)/shard_map/ppermute | solution.py:357
  58.1 14.7 %collective-permute-start.12 = (bf16[2,256,256]{2,1,0:T(8,128)(2,1)}, bf16[2,256,256]{2,1,0:T(8,128)(2,1)S(1)}, u32[]{:S(2)}, u32[]{:S(2)}) collective-permute-start(bf16[2,256,256]{2,1,0:T(8,128)(2,1)} %get-tuple-element.59), channel_id=1, source_target_pairs={{0,2},{2,0},{4,6},{6,4},{8,10},{10,8},{12,14},{14,12},{16,18},{18,... | collective-permute-start | bytes 786440 | tf_op jit(solution)/shard_map/ppermute | solution.py:357
  66.7 9.5 %collective-permute-start.18 = (bf16[2,256,256]{2,1,0:T(8,128)(2,1)S(1)}, bf16[2,256,256]{2,1,0:T(8,128)(2,1)S(1)}, u32[]{:S(2)}, u32[]{:S(2)}) collective-permute-start(bf16[2,256,256]{2,1,0:T(8,128)(2,1)S(1)} %add_convert_fusion.3), channel_id=1, source_target_pairs={{8,0},{10,2},{12,4},{14,6},{16,8},{18,10},{20,12},{22,14},{24,16},... | collective-permute-start | bytes 786440 | tf_op jit(solution)/shard_map/ppermute | solution.py:362
  79.0 12.3 %collective-permute-start.20 = (f32[56,256]{1,0:T(8,128)S(1)}, f32[56,256]{1,0:T(8,128)S(1)}, u32[]{:S(2)}, u32[]{:S(2)}) collective-permute-start(f32[56,256]{1,0:T(8,128)S(1)} %get-tuple-element.122), channel_id=1, source_target_pairs={{0,8},{2,10},{4,12},{6,14},{8,0},{10,2},{12,4},{14,6},{16,24},{18,... | collective-permute-start | bytes 172040 | tf_op jit(solution)/shard_map/ppermute | solution.py:357
  82.9 9.3 %collective-permute-start.21 = (f32[56,256]{1,0:T(8,128)S(1)}, f32[56,256]{1,0:T(8,128)S(1)}, u32[]{:S(2)}, u32[]{:S(2)}) collective-permute-start(f32[56,256]{1,0:T(8,128)S(1)} %get-tuple-element.124), channel_id=1, source_target_pairs={{0,16},{2,18},{4,20},{6,22},{8,24},{10,26},{12,28},{14,30},{16,0},... | collective-permute-start | bytes 172040 | tf_op jit(solution)/shard_map/ppermute | solution.py:357
  96.9 8.8 %collective-permute-start.26 = (f32[152,256]{1,0:T(8,128)S(1)}, f32[152,256]{1,0:T(8,128)S(1)}, u32[]{:S(2)}, u32[]{:S(2)}) collective-permute-start(f32[152,256]{1,0:T(8,128)S(1)} %constant_dynamic-update-slice_fusion), channel_id=1, source_target_pairs={{0,24},{2,26},{4,28},{6,30},{8,16},{10,18},{12,20},{14,22},{16,8},... | collective-permute-start | bytes 466952 | tf_op jit(solution)/shard_map/ppermute | solution.py:357
  99.4 12.4 %collective-permute-start.27 = (f32[152,256]{1,0:T(8,128)S(1)}, f32[152,256]{1,0:T(8,128)S(1)}, u32[]{:S(2)}, u32[]{:S(2)}) collective-permute-start(f32[152,256]{1,0:T(8,128)S(1)} %constant_dynamic-update-slice_fusion), channel_id=1, source_target_pairs={{0,16},{2,18},{4,20},{6,22},{8,24},{10,26},{12,28},{14,30},{16,0},... | collective-permute-start | bytes 466952 | tf_op jit(solution)/shard_map/ppermute | solution.py:357
  99.4 12.4 %collective-permute-start.28 = (f32[152,256]{1,0:T(8,128)S(1)}, f32[152,256]{1,0:T(8,128)S(1)}, u32[]{:S(2)}, u32[]{:S(2)}) collective-permute-start(f32[152,256]{1,0:T(8,128)S(1)} %constant_dynamic-update-slice_fusion), channel_id=1, source_target_pairs={{0,8},{2,10},{4,12},{6,14},{8,0},{10,2},{12,4},{14,6},{16,24},{18,... | collective-permute-start | bytes 466952 | tf_op jit(solution)/shard_map/ppermute | solution.py:357
  111.9 11.6 %collective-permute-start.29 = (f32[320,256]{1,0:T(8,128)S(1)}, f32[320,256]{1,0:T(8,128)S(1)}, u32[]{:S(2)}, u32[]{:S(2)}) collective-permute-start(f32[320,256]{1,0:T(8,128)S(1)} %fusion.5), channel_id=1, source_target_pairs={{0,6},{2,4},{4,2},{6,0},{8,14},{10,12},{12,10},{14,8},{16,22},{18,... | collective-permute-start | bytes 983048 | tf_op jit(solution)/shard_map/ppermute | solution.py:357
  113.1 14.9 %collective-permute-start.30 = (f32[320,256]{1,0:T(8,128)S(1)}, f32[320,256]{1,0:T(8,128)S(1)}, u32[]{:S(2)}, u32[]{:S(2)}) collective-permute-start(f32[320,256]{1,0:T(8,128)S(1)} %fusion.5), channel_id=1, source_target_pairs={{0,4},{2,6},{4,0},{6,2},{8,12},{10,14},{12,8},{14,10},{16,20},{18,... | collective-permute-start | bytes 983048 | tf_op jit(solution)/shard_map/ppermute | solution.py:357
  114.3 14.5 %collective-permute-start.31 = (f32[320,256]{1,0:T(8,128)S(1)}, f32[320,256]{1,0:T(8,128)}, u32[]{:S(2)}, u32[]{:S(2)}) collective-permute-start(f32[320,256]{1,0:T(8,128)S(1)} %fusion.5), channel_id=1, source_target_pairs={{0,2},{2,0},{4,6},{6,4},{8,10},{10,8},{12,14},{14,12},{16,18},{18,... | collective-permute-start | bytes 983048 | tf_op jit(solution)/shard_map/ppermute | solution.py:357
  147.9 8.5 %collective-permute-start.33 = (bf16[2,256,256]{2,1,0:T(8,128)(2,1)S(1)}, bf16[2,256,256]{2,1,0:T(8,128)(2,1)S(1)}, u32[]{:S(2)}, u32[]{:S(2)}) collective-permute-start(bf16[2,256,256]{2,1,0:T(8,128)(2,1)S(1)} %get-tuple-element.79.refs_0_), channel_id=1, source_target_pairs={{0,2},{2,0},{4,6},{6,4},{8,10},{10,8},{12,14},{14,12},{16,18},{18,... | collective-permute-start | bytes 786440 | tf_op jit(solution)/shard_map/ppermute | solution.py:357
  153.7 9.4 %collective-permute-start.35 = (bf16[2,256,256]{2,1,0:T(8,128)(2,1)S(1)}, bf16[2,256,256]{2,1,0:T(8,128)(2,1)S(1)}, u32[]{:S(2)}, u32[]{:S(2)}) collective-permute-start(bf16[2,256,256]{2,1,0:T(8,128)(2,1)S(1)} %collective-permute-done.34.refs_2_), channel_id=1, source_target_pairs={{0,2},{2,0},{4,6},{6,4},{8,10},{10,8},{12,14},{14,12},{16,18},{18,... | collective-permute-start | bytes 786440 | tf_op jit(solution)/shard_map/ppermute | solution.py:357
  156.4 20.6 %collective-permute-start.36 = (bf16[2,256,256]{2,1,0:T(8,128)(2,1)S(1)}, bf16[2,256,256]{2,1,0:T(8,128)(2,1)S(1)}, u32[]{:S(2)}, u32[]{:S(2)}) collective-permute-start(bf16[2,256,256]{2,1,0:T(8,128)(2,1)S(1)} %get-tuple-element.79.refs_0_), channel_id=1, source_target_pairs={{0,4},{2,6},{8,12},{10,14},{4,16},{6,18},{16,20},{18,22},{12,24},{... | collective-permute-start | bytes 786440 | tf_op jit(solution)/shard_map/ppermute | solution.py:368
  158.9 11.5 %collective-permute-start.38 = (bf16[2,256,256]{2,1,0:T(8,128)(2,1)S(1)}, bf16[2,256,256]{2,1,0:T(8,128)(2,1)S(1)}, u32[]{:S(2)}, u32[]{:S(2)}) collective-permute-start(bf16[2,256,256]{2,1,0:T(8,128)(2,1)S(1)} %collective-permute-done.34.refs_2_), channel_id=1, source_target_pairs={{0,4},{2,6},{4,0},{6,2},{8,12},{10,14},{12,8},{14,10},{16,20},{18,... | collective-permute-start | bytes 786440 | tf_op jit(solution)/shard_map/ppermute | solution.py:357
  163.1 11.3 %collective-permute-start.39 = (bf16[2,256,256]{2,1,0:T(8,128)(2,1)S(1)}, bf16[2,256,256]{2,1,0:T(8,128)(2,1)S(1)}, u32[]{:S(2)}, u32[]{:S(2)}) collective-permute-start(bf16[2,256,256]{2,1,0:T(8,128)(2,1)S(1)} %collective-permute-done.35.refs_3_), channel_id=1, source_target_pairs={{0,4},{2,6},{4,0},{6,2},{8,12},{10,14},{12,8},{14,10},{16,20},{18,... | collective-permute-start | bytes 786440 | tf_op jit(solution)/shard_map/ppermute | solution.py:357
  172.4 12.9 %collective-permute-start.40 = (f32[256,512]{1,0:T(8,128)S(1)}, f32[256,512]{1,0:T(8,128)S(1)}, u32[]{:S(2)}, u32[]{:S(2)}) collective-permute-start(f32[256,512]{1,0:T(8,128)S(1)} %get-tuple-element.77.x.refs_3_), channel_id=1, source_target_pairs={{0,1},{1,0},{2,3},{3,2},{4,5},{5,4},{6,7},{7,6},{8,9},{9,8},{10,11... | collective-permute-start | bytes 1572872 | tf_op jit(solution)/shard_map/ppermute | solution.py:353
  174.5 9.2 %collective-permute-start.48 = (bf16[2,256,256]{2,1,0:T(8,128)(2,1)S(1)}, bf16[2,256,256]{2,1,0:T(8,128)(2,1)S(1)}, u32[]{:S(2)}, u32[]{:S(2)}) collective-permute-start(bf16[2,256,256]{2,1,0:T(8,128)(2,1)S(1)} %get-tuple-element.92), channel_id=1, source_target_pairs={{0,4},{2,6},{4,0},{6,2},{8,12},{10,14},{12,8},{14,10},{16,20},{18,... | collective-permute-start | bytes 786440 | tf_op jit(solution)/shard_map/ppermute | solution.py:357
  177.0 9.3 %collective-permute-start.41 = (bf16[2,256,256]{2,1,0:T(8,128)(2,1)S(1)}, bf16[2,256,256]{2,1,0:T(8,128)(2,1)S(1)}, u32[]{:S(2)}, u32[]{:S(2)}) collective-permute-start(bf16[2,256,256]{2,1,0:T(8,128)(2,1)S(1)} %collective-permute-done.33.refs_1_), channel_id=1, source_target_pairs={{0,1},{1,0},{2,3},{3,2},{4,5},{5,4},{6,7},{7,6},{8,9},{9,8},{10,11... | collective-permute-start | bytes 786440 | tf_op jit(solution)/shard_map/ppermute | solution.py:353
  177.0 9.3 %collective-permute-start.37 = (bf16[2,256,256]{2,1,0:T(8,128)(2,1)S(1)}, bf16[2,256,256]{2,1,0:T(8,128)(2,1)S(1)}, u32[]{:S(2)}, u32[]{:S(2)}) collective-permute-start(bf16[2,256,256]{2,1,0:T(8,128)(2,1)S(1)} %collective-permute-done.36.refs_4_), channel_id=1, source_target_pairs={{0,2},{2,0},{4,6},{6,4},{8,10},{10,8},{12,14},{14,12},{16,18},{18,... | collective-permute-start | bytes 786440 | tf_op jit(solution)/shard_map/ppermute | solution.py:357
  178.2 17.2 %collective-permute-start.50 = (bf16[2,256,256]{2,1,0:T(8,128)(2,1)S(1)}, bf16[2,256,256]{2,1,0:T(8,128)(2,1)S(1)}, u32[]{:S(2)}, u32[]{:S(2)}) collective-permute-start(bf16[2,256,256]{2,1,0:T(8,128)(2,1)S(1)} %get-tuple-element.93), channel_id=1, source_target_pairs={{0,4},{2,6},{4,0},{6,2},{8,12},{10,14},{12,8},{14,10},{16,20},{18,... | collective-permute-start | bytes 786440 | tf_op jit(solution)/shard_map/ppermute | solution.py:357
  183.7 19.0 %collective-permute-start.47 = (bf16[2,256,256]{2,1,0:T(8,128)(2,1)S(1)}, bf16[2,256,256]{2,1,0:T(8,128)(2,1)S(1)}, u32[]{:S(2)}, u32[]{:S(2)}) collective-permute-start(bf16[2,256,256]{2,1,0:T(8,128)(2,1)S(1)} %add_convert_fusion.2), channel_id=1, source_target_pairs={{4,0},{6,2},{12,8},{14,10},{16,4},{18,6},{20,16},{22,18},{24,12},{... | collective-permute-start | bytes 786440 | tf_op jit(solution)/shard_map/ppermute | solution.py:368
  185.3 10.0 %collective-permute-start.49 = (bf16[2,256,256]{2,1,0:T(8,128)(2,1)S(1)}, bf16[2,256,256]{2,1,0:T(8,128)(2,1)S(1)}, u32[]{:S(2)}, u32[]{:S(2)}) collective-permute-start(bf16[2,256,256]{2,1,0:T(8,128)(2,1)S(1)} %add_convert_fusion.1), channel_id=1, source_target_pairs={{0,2},{2,0},{4,6},{6,4},{8,10},{10,8},{12,14},{14,12},{16,18},{18,... | collective-permute-start | bytes 786440 | tf_op jit(solution)/shard_map/ppermute | solution.py:357
  187.9 9.0 %collective-permute-start.42 = (f32[128,256]{1,0:T(8,128)S(1)}, f32[128,256]{1,0:T(8,128)S(1)}, u32[]{:S(2)}, u32[]{:S(2)}) collective-permute-start(f32[128,256]{1,0:T(8,128)S(1)} %get-tuple-element.113), channel_id=1, source_target_pairs={{0,2},{2,0},{4,6},{6,4},{8,10},{10,8},{12,14},{14,12},{16,18},{18,... | collective-permute-start | bytes 393224 | tf_op jit(solution)/shard_map/ppermute | solution.py:357
  191.5 9.0 %collective-permute-start.43 = (f32[128,256]{1,0:T(8,128)S(1)}, f32[128,256]{1,0:T(8,128)S(1)}, u32[]{:S(2)}, u32[]{:S(2)}) collective-permute-start(f32[128,256]{1,0:T(8,128)S(1)} %get-tuple-element.115), channel_id=1, source_target_pairs={{0,4},{2,6},{4,0},{6,2},{8,12},{10,14},{12,8},{14,10},{16,20},{18,... | collective-permute-start | bytes 393224 | tf_op jit(solution)/shard_map/ppermute | solution.py:357
  196.9 8.9 %collective-permute-start.51 = (bf16[2,256,256]{2,1,0:T(8,128)(2,1)S(1)}, bf16[2,256,256]{2,1,0:T(8,128)(2,1)S(1)}, u32[]{:S(2)}, u32[]{:S(2)}) collective-permute-start(bf16[2,256,256]{2,1,0:T(8,128)(2,1)S(1)} %add_convert_fusion), channel_id=1, source_target_pairs={{8,0},{10,2},{12,4},{14,6},{16,8},{18,10},{20,12},{22,14},{24,16},... | collective-permute-start | bytes 786440 | tf_op jit(solution)/shard_map/ppermute | solution.py:362
  208.6 13.8 %collective-permute-start.53 = (f32[32,256]{1,0:T(8,128)S(1)}, f32[32,256]{1,0:T(8,128)S(1)}, u32[]{:S(2)}, u32[]{:S(2)}) collective-permute-start(f32[32,256]{1,0:T(8,128)S(1)} %get-tuple-element.125), channel_id=1, source_target_pairs={{0,8},{2,10},{4,12},{6,14},{8,0},{10,2},{12,4},{14,6},{16,24},{18,... | collective-permute-start | bytes 98312 | tf_op jit(solution)/shard_map/ppermute | solution.py:357
  230.5 10.3 %collective-permute-start.60 = (f32[128,256]{1,0:T(8,128)S(1)}, f32[128,256]{1,0:T(8,128)S(1)}, u32[]{:S(2)}, u32[]{:S(2)}) collective-permute-start(f32[128,256]{1,0:T(8,128)S(1)} %constant_dynamic-update-slice_fusion.2), channel_id=1, source_target_pairs={{0,16},{2,18},{4,20},{6,22},{8,24},{10,26},{12,28},{14,30},{16,0},... | collective-permute-start | bytes 393224 | tf_op jit(solution)/shard_map/ppermute | solution.py:357
  230.5 10.3 %collective-permute-start.61 = (f32[128,256]{1,0:T(8,128)S(1)}, f32[128,256]{1,0:T(8,128)S(1)}, u32[]{:S(2)}, u32[]{:S(2)}) collective-permute-start(f32[128,256]{1,0:T(8,128)S(1)} %constant_dynamic-update-slice_fusion.2), channel_id=1, source_target_pairs={{0,8},{2,10},{4,12},{6,14},{8,0},{10,2},{12,4},{14,6},{16,24},{18,... | collective-permute-start | bytes 393224 | tf_op jit(solution)/shard_map/ppermute | solution.py:357
  240.9 9.5 %collective-permute-start.62 = (f32[224,256]{1,0:T(8,128)S(1)}, f32[224,256]{1,0:T(8,128)S(1)}, u32[]{:S(2)}, u32[]{:S(2)}) collective-permute-start(f32[224,256]{1,0:T(8,128)S(1)} %fusion.4), channel_id=1, source_target_pairs={{0,6},{2,4},{4,2},{6,0},{8,14},{10,12},{12,10},{14,8},{16,22},{18,... | collective-permute-start | bytes 688136 | tf_op jit(solution)/shard_map/ppermute | solution.py:357
  241.5 10.9 %collective-permute-start.63 = (f32[224,256]{1,0:T(8,128)S(1)}, f32[224,256]{1,0:T(8,128)S(1)}, u32[]{:S(2)}, u32[]{:S(2)}) collective-permute-start(f32[224,256]{1,0:T(8,128)S(1)} %fusion.4), channel_id=1, source_target_pairs={{0,4},{2,6},{4,0},{6,2},{8,12},{10,14},{12,8},{14,10},{16,20},{18,... | collective-permute-start | bytes 688136 | tf_op jit(solution)/shard_map/ppermute | solution.py:357
  243.3 9.1 %collective-permute-start.64 = (f32[224,256]{1,0:T(8,128)S(1)}, f32[224,256]{1,0:T(8,128)S(1)}, u32[]{:S(2)}, u32[]{:S(2)}) collective-permute-start(f32[224,256]{1,0:T(8,128)S(1)} %fusion.4), channel_id=1, source_target_pairs={{0,2},{2,0},{4,6},{6,4},{8,10},{10,8},{12,14},{14,12},{16,18},{18,... | collective-permute-start | bytes 688136 | tf_op jit(solution)/shard_map/ppermute | solution.py:357
  (37 other events, 212.7 us)

commit v2 on v1

--- a/solution.py
+++ b/solution.py
@@ -97,11 +97,10 @@
         for k in range(GROUP):
             slot = group * GROUP + k
             row, col = rows[slot], cols[slot]
-            tile = tiles[slot]
-            tile = jnp.where(slot < used, tile, jnp.zeros_like(tile))
-            found.append(product(tile, place(row, meta), place(col, meta)) + (row == col,))
-        for at, part, diagonal in found:
-            total[at] += part * jnp.where(diagonal, 0.5, 1.0).astype(f32)
+            weight = jnp.where(slot < used, jnp.where(row == col, 0.5, 1.0), 0.0).astype(f32)
+            found.append(product(tiles[slot], place(row, meta), place(col, meta)) + (weight,))
+        for at, part, weight in found:
+            total[at] += part * weight
         return carry
 
     lax.fori_loop(0, groups, multiply, 0)
@@ -452,9 +451,8 @@
         )
         same, cross = sums[::2], sums[1::2]
         two, two_x, far, side = reach(u, own_x)
+        out_side_x, out_far, out_side = together(cross[3], cross[2], same[3], far, two_x, side)[:3]
         pieces = [u, own_x, two, two_x, far, flip(far, 1), side, flip(two_x, 2)]
-        out_side_x, out_side = together(cross[3], same[3], pieces[7])[:2]
-        out_far = together(cross[2], side, two_x)[0]
         kept, near, inner = tiles_call(
             direct_kernel,
             [shape(f32, *segment), shape(bf16, *segment), shape(f32, 2 * width, width)],

time: 267 us -> 252 us (0.944)
  starting transfers between devices: 106 us -> 76.3 us
  waiting for transfers between devices: 110 us -> 119 us
  Pallas kernels: 35.2 us -> 41.1 us
    ppermute x50, starting transfers between devices: 86.8 us -> 59.2 us  [flip(): lax.ppermute(a, 'patch', [(i, i ^ mask) for i in range(lax.axis_size('pat...]
    ppermute x50, waiting for transfers between devices: 85.2 us -> 98.8 us  [flip(): lax.ppermute(a, 'patch', [(i, i ^ mask) for i in range(lax.axis_size('pat...]
    ppermute x4, waiting for transfers between devices: 15.5 us -> 8.64 us  [shift(): lax.ppermute(a, 'patch', [(i - 2 * pairs, i) for i in devices if i - 2 *...]
    pallas_call x4, Pallas kernels: 8.49 us -> 14.3 us  [tiles_call(): pl.pallas_call(kernel, in_specs=[pl.BlockSpec(memory_space=SMEM)] * 3 + [...]
    ppermute x4, waiting for transfers between devices: 0.01 us -> 2.73 us  [stride(): lax.ppermute(a, 'patch', [(d, s) if back else (s, d) for s, d in route if...]
  transfers between devices with their start and end apart: 66 -> 66, of which waited for: 36 -> 40; matrix products, arithmetic and copies ran while one was open for 2% -> 2% of each run, Pallas kernels for 3% -> 6%
where the time goes in v2:
time: 252 us; the launch traced here: 253 us
  waiting for transfers between devices  119 us (47%)
  starting transfers between devices  76.3 us (30%)
  Pallas kernels  41.1 us (16%)
  local copies, waits for them, and re-layouts  7.82 us (3%)
  other arithmetic  5.96 us (2%)
    ppermute x50, waiting for transfers between devices, flip(): lax.ppermute(a, 'patch', [(i, i ^ mask) for i in range(lax.axis_size('pat...  98.8 us
    ppermute x50, starting transfers between devices, flip(): lax.ppermute(a, 'patch', [(i, i ^ mask) for i in range(lax.axis_size('pat...  59.2 us
    pallas_call x8, Pallas kernels, call(): pl.pallas_call(kernel, out_shape=out, in_specs=[pl.BlockSpec(memory_space...  26.8 us
    pallas_call x4, Pallas kernels, tiles_call(): pl.pallas_call(kernel, in_specs=[pl.BlockSpec(memory_space=SMEM)] * 3 + [...  14.3 us
    ppermute x8, waiting for transfers between devices, swap_cores(): return lax.ppermute(a, 'vec', [(0, 1), (1, 0)])  9.24 us
    ppermute x4, starting transfers between devices, stride(): lax.ppermute(a, 'patch', [(d, s) if back else (s, d) for s, d in route if...  8.86 us
    ppermute x4, waiting for transfers between devices, shift(): lax.ppermute(a, 'patch', [(i - 2 * pairs, i) for i in devices if i - 2 *...  8.64 us
    ppermute x4, starting transfers between devices, shift(): lax.ppermute(a, 'patch', [(i - 2 * pairs, i) for i in devices if i - 2 *...  7.52 us
  transfers between devices with their start and end apart: 66, of which 40 were waited for; matrix products, arithmetic and copies ran while one was open for 2% of the time, Pallas kernels for 6%

profile of v2, /device:TPU:0, one launch (start us, length us, event | category | flops | bytes accessed | tf_op | source)
XLA Modules:
  0.0 252.6 jit_solution(13095919817409300604)
XLA Ops:
  1.9 3.0 %collective-permute-start = (bf16[2,256,256]{2,1,0:T(8,128)(2,1)S(1)}, bf16[2,256,256]{2,1,0:T(8,128)(2,1)S(1)}, u32[]{:S(2)}, u32[]{:S(2)}) collective-permute-start(bf16[2,256,256]{2,1,0:T(8,128)(2,1)S(1)} %get-tuple-element.54.refs_0_), channel_id=1, source_target_pairs={{0,2},{2,0},{4,6},{6,4},{8,10},{10,8},{12,14},{14,12},{16,18},{18,... | collective-permute-start | bytes 786440 | tf_op jit(solution)/shard_map/ppermute | solution.py:356
  4.9 3.5 %collective-permute-start.1 = (bf16[2,256,256]{2,1,0:T(8,128)(2,1)S(1)}, bf16[2,256,256]{2,1,0:T(8,128)(2,1)S(1)}, u32[]{:S(2)}, u32[]{:S(2)}) collective-permute-start(bf16[2,256,256]{2,1,0:T(8,128)(2,1)S(1)} %get-tuple-element.54.refs_0_), channel_id=1, source_target_pairs={{0,8},{2,10},{4,12},{6,14},{8,16},{10,18},{12,20},{14,22},{16,24},... | collective-permute-start | bytes 786440 | tf_op jit(solution)/shard_map/ppermute | solution.py:361
  11.2 3.7 %collective-permute-start.3 = (bf16[2,256,256]{2,1,0:T(8,128)(2,1)S(1)}, bf16[2,256,256]{2,1,0:T(8,128)(2,1)S(1)}, u32[]{:S(2)}, u32[]{:S(2)}) collective-permute-start(bf16[2,256,256]{2,1,0:T(8,128)(2,1)S(1)} %get-tuple-element.54.refs_0_), channel_id=1, source_target_pairs={{0,4},{2,6},{8,12},{10,14},{4,16},{6,18},{16,20},{18,22},{12,24},{... | collective-permute-start | bytes 786440 | tf_op jit(solution)/shard_map/ppermute | solution.py:367
  16.4 2.5 collective-permute-start.5
  20.3 3.7 %shard_map.69 = (f32[2,256,256]{2,1,0:T(8,128)S(1)}, f32[2,256,256]{2,1,0:T(8,128)S(1)}, f32[2,256,256]{2,1,0:T(8,128)S(1)}, f32[2,256,256]{2,1,0:T(8,128)S(1)},...) custom-call(s32[4]{0:T(128)S(1)} %pad_add_fusion.meta, ...), custom_call_target="tpu_custom_call" | custom-call | flops 4294967296 | bytes 12582912 | tf_op jit(solution)/shard_map/pallas_call | solution.py:146
  30.5 2.0 collective-permute-start.4
  33.2 4.8 %collective-permute-done.15 = bf16[2,256,256]{2,1,0:T(8,128)(2,1)} collective-permute-done((bf16[2,256,256]{2,1,0:T(8,128)(2,1)}, bf16[2,256,256]{2,1,0:T(8,128)(2,1)}, u32[]{:S(2)}, u32[]{:S(2)}) %collective-permute-start.15) | collective-permute-done | bytes 262176 | tf_op jit(solution)/shard_map/ppermute | solution.py:356
  42.6 2.9 %collective-permute-done.4.refs_5_ = bf16[2,256,256]{2,1,0:T(8,128)(2,1)S(1)} collective-permute-done((bf16[2,256,256]{2,1,0:T(8,128)(2,1)}, bf16[2,256,256]{2,1,0:T(8,128)(2,1)S(1)}, u32[]{:S(2)}, u32[]{:S(2)}) %collective-permute-start.4) | collective-permute-done | bytes 262176 | tf_op jit(solution)/shard_map/ppermute | solution.py:356
  45.4 2.6 %collective-permute-done.6.refs_7_ = bf16[2,256,256]{2,1,0:T(8,128)(2,1)S(1)} collective-permute-done((bf16[2,256,256]{2,1,0:T(8,128)(2,1)S(1)}, bf16[2,256,256]{2,1,0:T(8,128)(2,1)S(1)}, u32[]{:S(2)}, u32[]{:S(2)}) %collective-permute-start.6) | collective-permute-done | bytes 262176 | tf_op jit(solution)/shard_map/ppermute | solution.py:356
  48.1 3.7 %shard_map.70 = (f32[2,256,256]{2,1,0:T(8,128)S(1)}, bf16[2,256,256]{2,1,0:T(8,128)(2,1)S(1)}, f32[512,256]{1,0:T(8,128)S(1)}) custom-call(s32[4]{0:T(128)S(1)} %pad_add_fusion.meta, s32[64]{0:T(128)S(1)} %copy-done.10, s32[64]{0:T(128)S(1)} %copy-done.12, bf16[2,256,256]{2,1,0:T(8,128)(2,1)S(1)} %get-tuple-element.54.refs_0_, ...), custom_call_target="tpu_custom_call" | custom-call | flops 4294967296 | bytes 12582912 | tf_op jit(solution)/shard_map/pallas_call | solution.py:146
  52.8 3.5 %collective-permute-start.9 = (f32[224,256]{1,0:T(8,128)}, f32[224,256]{1,0:T(8,128)}, u32[]{:S(2)}, u32[]{:S(2)}) collective-permute-start(f32[224,256]{1,0:T(8,128)} %get-tuple-element.110), channel_id=1, source_target_pairs={{0,2},{2,0},{4,6},{6,4},{8,10},{10,8},{12,14},{14,12},{16,18},{18,... | collective-permute-start | bytes 688136 | tf_op jit(solution)/shard_map/ppermute | solution.py:356
  56.5 6.6 %collective-permute-done.10 = f32[224,256]{1,0:T(8,128)S(1)} collective-permute-done((f32[224,256]{1,0:T(8,128)S(1)}, f32[224,256]{1,0:T(8,128)S(1)}, u32[]{:S(2)}, u32[]{:S(2)}) %collective-permute-start.10) | collective-permute-done | bytes 229408 | tf_op jit(solution)/shard_map/ppermute | solution.py:356
  64.5 2.0 collective-permute-done.9
  69.2 5.3 %collective-permute-done.18.two = bf16[2,256,256]{2,1,0:T(8,128)(2,1)S(1)} collective-permute-done((bf16[2,256,256]{2,1,0:T(8,128)(2,1)S(1)}, bf16[2,256,256]{2,1,0:T(8,128)(2,1)S(1)}, u32[]{:S(2)}, u32[]{:S(2)}) %collective-permute-start.18) | collective-permute-done | bytes 262176 | tf_op jit(solution)/shard_map/ppermute | solution.py:361
  77.3 2.1 collective-permute-start.20
  79.4 2.0 collective-permute-start.21
  82.2 2.3 collective-permute-start.24
  92.8 2.2 collective-permute-start.28
  94.9 4.4 %collective-permute-done.26 = f32[152,256]{1,0:T(8,128)S(1)} collective-permute-done((f32[152,256]{1,0:T(8,128)S(1)}, f32[152,256]{1,0:T(8,128)S(1)}, u32[]{:S(2)}, u32[]{:S(2)}) %collective-permute-start.26) | collective-permute-done | bytes 155680 | tf_op jit(solution)/shard_map/ppermute | solution.py:356
  99.3 5.9 %collective-permute-done.27 = f32[152,256]{1,0:T(8,128)S(1)} collective-permute-done((f32[152,256]{1,0:T(8,128)S(1)}, f32[152,256]{1,0:T(8,128)S(1)}, u32[]{:S(2)}, u32[]{:S(2)}) %collective-permute-start.27) | collective-permute-done | bytes 155680 | tf_op jit(solution)/shard_map/ppermute | solution.py:356
  108.9 8.1 %collective-permute-done.29 = f32[320,256]{1,0:T(8,128)S(1)} collective-permute-done((f32[320,256]{1,0:T(8,128)S(1)}, f32[320,256]{1,0:T(8,128)S(1)}, u32[]{:S(2)}, u32[]{:S(2)}) %collective-permute-start.29) | collective-permute-done | bytes 327712 | tf_op jit(solution)/shard_map/ppermute | solution.py:356
  117.0 4.1 %collective-permute-done.30 = f32[320,256]{1,0:T(8,128)S(1)} collective-permute-done((f32[320,256]{1,0:T(8,128)S(1)}, f32[320,256]{1,0:T(8,128)S(1)}, u32[]{:S(2)}, u32[]{:S(2)}) %collective-permute-start.30) | collective-permute-done | bytes 327712 | tf_op jit(solution)/shard_map/ppermute | solution.py:356
  123.8 3.0 %collective-permute-done.32.refs_6_ = f32[4,320,256]{2,1,0:T(8,128)S(1)} collective-permute-done((f32[4,320,256]{2,1,0:T(8,128)S(1)}, f32[4,320,256]{2,1,0:T(8,128)S(1)}, u32[]{:S(2)}, u32[]{:S(2)}) %collective-permute-start.32) | collective-permute-done | bytes 1310752 | tf_op jit(solution)/shard_map/ppermute | solution.py:352
  126.8 13.2 %shard_map.74 = (f32[256,512]{1,0:T(8,128)S(1)}, bf16[2,256,256]{2,1,0:T(8,128)(2,1)S(1)}) custom-call(s32[1]{0:T(128)} %bitcast.core.refs_0_, f32[256,512]{1,0:T(8,128)S(1)} %shard_map.72.mine.refs_1_, f32[256,512]{1,0:T(8,128)S(1)} %collective-permute-done.19.theirs.refs_2_, f32[256,512]{1,0:T(8,128)S(1)} %get-tuple-element.52.mine.x.refs_3_, ...), custom_call_target="tpu_custom_call" | custom-call | flops 17179869184 | bytes 5505028 | tf_op jit(solution)/shard_map/pallas_call | solution.py:39
  141.5 6.9 %collective-permute-done.33.refs_1_ = bf16[2,256,256]{2,1,0:T(8,128)(2,1)S(1)} collective-permute-done((bf16[2,256,256]{2,1,0:T(8,128)(2,1)S(1)}, bf16[2,256,256]{2,1,0:T(8,128)(2,1)S(1)}, u32[]{:S(2)}, u32[]{:S(2)}) %collective-permute-start.33) | collective-permute-done | bytes 262176 | tf_op jit(solution)/shard_map/ppermute | solution.py:356
  148.4 2.4 collective-permute-start.36
  151.7 3.1 %shard_map.75 = (f32[2,256,256]{2,1,0:T(8,128)S(1)}, f32[2,256,256]{2,1,0:T(8,128)S(1)}, f32[2,256,256]{2,1,0:T(8,128)S(1)}, f32[2,256,256]{2,1,0:T(8,128)S(1)},...) custom-call(s32[4]{0:T(128)S(1)} %pad_add_fusion.meta, ...), custom_call_target="tpu_custom_call" | custom-call | flops 4294967296 | bytes 12582912 | tf_op jit(solution)/shard_map/pallas_call | solution.py:146
  154.9 2.7 %collective-permute-done.36.refs_4_ = bf16[2,256,256]{2,1,0:T(8,128)(2,1)S(1)} collective-permute-done((bf16[2,256,256]{2,1,0:T(8,128)(2,1)S(1)}, bf16[2,256,256]{2,1,0:T(8,128)(2,1)S(1)}, u32[]{:S(2)}, u32[]{:S(2)}) %collective-permute-start.36) | collective-permute-done | bytes 262176 | tf_op jit(solution)/shard_map/ppermute | solution.py:367
  158.2 3.3 %collective-permute-done.38.refs_6_ = bf16[2,256,256]{2,1,0:T(8,128)(2,1)S(1)} collective-permute-done((bf16[2,256,256]{2,1,0:T(8,128)(2,1)S(1)}, bf16[2,256,256]{2,1,0:T(8,128)(2,1)S(1)}, u32[]{:S(2)}, u32[]{:S(2)}) %collective-permute-start.38) | collective-permute-done | bytes 262176 | tf_op jit(solution)/shard_map/ppermute | solution.py:356
  161.5 2.5 collective-permute-start.48
  166.2 2.6 %collective-permute-done.48 = bf16[2,256,256]{2,1,0:T(8,128)(2,1)S(1)} collective-permute-done((bf16[2,256,256]{2,1,0:T(8,128)(2,1)S(1)}, bf16[2,256,256]{2,1,0:T(8,128)(2,1)S(1)}, u32[]{:S(2)}, u32[]{:S(2)}) %collective-permute-start.48) | collective-permute-done | bytes 262176 | tf_op jit(solution)/shard_map/ppermute | solution.py:356
  170.6 2.5 collective-permute-done.46
  175.1 3.6 %collective-permute-done.37.refs_5_ = bf16[2,256,256]{2,1,0:T(8,128)(2,1)S(1)} collective-permute-done((bf16[2,256,256]{2,1,0:T(8,128)(2,1)S(1)}, bf16[2,256,256]{2,1,0:T(8,128)(2,1)S(1)}, u32[]{:S(2)}, u32[]{:S(2)}) %collective-permute-start.37) | collective-permute-done | bytes 262176 | tf_op jit(solution)/shard_map/ppermute | solution.py:356
  178.7 3.7 %shard_map.76 = (f32[2,256,256]{2,1,0:T(8,128)S(1)}, bf16[2,256,256]{2,1,0:T(8,128)(2,1)S(1)}, f32[512,256]{1,0:T(8,128)S(1)}) custom-call(s32[4]{0:T(128)S(1)} %pad_add_fusion.meta, s32[64]{0:T(128)S(1)} %copy-done.10, s32[64]{0:T(128)S(1)} %copy-done.12, bf16[2,256,256]{2,1,0:T(8,128)(2,1)S(1)} %get-tuple-element.79.refs_0_, ...), custom_call_target="tpu_custom_call" | custom-call | flops 4294967296 | bytes 12582912 | tf_op jit(solution)/shard_map/pallas_call | solution.py:146
  183.3 2.7 %collective-permute-start.44 = (f32[128,256]{1,0:T(8,128)S(1)}, f32[128,256]{1,0:T(8,128)S(1)}, u32[]{:S(2)}, u32[]{:S(2)}) collective-permute-start(f32[128,256]{1,0:T(8,128)S(1)} %get-tuple-element.114), channel_id=1, source_target_pairs={{0,6},{2,4},{4,2},{6,0},{8,14},{10,12},{12,10},{14,8},{16,22},{18,... | collective-permute-start | bytes 393224 | tf_op jit(solution)/shard_map/ppermute | solution.py:356
  186.2 2.8 %collective-permute-done.42 = f32[128,256]{1,0:T(8,128)S(1)} collective-permute-done((f32[128,256]{1,0:T(8,128)S(1)}, f32[128,256]{1,0:T(8,128)S(1)}, u32[]{:S(2)}, u32[]{:S(2)}) %collective-permute-start.42) | collective-permute-done | bytes 131104 | tf_op jit(solution)/shard_map/ppermute | solution.py:356
  190.2 3.2 %collective-permute-done.43 = f32[128,256]{1,0:T(8,128)S(1)} collective-permute-done((f32[128,256]{1,0:T(8,128)S(1)}, f32[128,256]{1,0:T(8,128)S(1)}, u32[]{:S(2)}, u32[]{:S(2)}) %collective-permute-start.43) | collective-permute-done | bytes 131104 | tf_op jit(solution)/shard_map/ppermute | solution.py:356
  193.5 2.2 collective-permute-done.45.near
  195.7 3.4 %collective-permute-done.51.two = bf16[2,256,256]{2,1,0:T(8,128)(2,1)S(1)} collective-permute-done((bf16[2,256,256]{2,1,0:T(8,128)(2,1)S(1)}, bf16[2,256,256]{2,1,0:T(8,128)(2,1)S(1)}, u32[]{:S(2)}, u32[]{:S(2)}) %collective-permute-start.51) | collective-permute-done | bytes 262176 | tf_op jit(solution)/shard_map/ppermute | solution.py:361
  201.8 2.1 collective-permute-start.53
  207.4 2.5 collective-permute-start.58
  213.6 3.1 %collective-permute-start.59 = (f32[128,256]{1,0:T(8,128)S(1)}, f32[128,256]{1,0:T(8,128)S(1)}, u32[]{:S(2)}, u32[]{:S(2)}) collective-permute-start(f32[128,256]{1,0:T(8,128)S(1)} %constant_dynamic-update-slice_fusion.2), channel_id=1, source_target_pairs={{0,24},{2,26},{4,28},{6,30},{8,16},{10,18},{12,20},{14,22},{16,8},... | collective-permute-start | bytes 393224 | tf_op jit(solution)/shard_map/ppermute | solution.py:356
  218.0 3.9 %collective-permute-done.59 = f32[128,256]{1,0:T(8,128)S(1)} collective-permute-done((f32[128,256]{1,0:T(8,128)S(1)}, f32[128,256]{1,0:T(8,128)S(1)}, u32[]{:S(2)}, u32[]{:S(2)}) %collective-permute-start.59) | collective-permute-done | bytes 131104 | tf_op jit(solution)/shard_map/ppermute | solution.py:356
  221.9 4.4 %collective-permute-done.60 = f32[128,256]{1,0:T(8,128)S(1)} collective-permute-done((f32[128,256]{1,0:T(8,128)S(1)}, f32[128,256]{1,0:T(8,128)S(1)}, u32[]{:S(2)}, u32[]{:S(2)}) %collective-permute-start.60) | collective-permute-done | bytes 131104 | tf_op jit(solution)/shard_map/ppermute | solution.py:356
  230.0 6.0 %collective-permute-done.62 = f32[224,256]{1,0:T(8,128)S(1)} collective-permute-done((f32[224,256]{1,0:T(8,128)S(1)}, f32[224,256]{1,0:T(8,128)S(1)}, u32[]{:S(2)}, u32[]{:S(2)}) %collective-permute-start.62) | collective-permute-done | bytes 229408 | tf_op jit(solution)/shard_map/ppermute | solution.py:356
  236.0 2.7 %collective-permute-done.63 = f32[224,256]{1,0:T(8,128)S(1)} collective-permute-done((f32[224,256]{1,0:T(8,128)S(1)}, f32[224,256]{1,0:T(8,128)S(1)}, u32[]{:S(2)}, u32[]{:S(2)}) %collective-permute-start.63) | collective-permute-done | bytes 229408 | tf_op jit(solution)/shard_map/ppermute | solution.py:356
  238.9 2.5 collective-permute-done.65.refs_6_
  241.3 11.2 %shard_map.79 = (f32[512,256]{1,0:T(8,128)}, f32[512,256]{1,0:T(8,128)}) custom-call(s32[1]{0:T(128)} %bitcast.core.refs_0_, f32[256,512]{1,0:T(8,128)S(1)} %shard_map.77.mine.refs_1_, f32[256,512]{1,0:T(8,128)S(1)} %collective-permute-done.52.theirs.refs_2_, f32[256,512]{1,0:T(8,128)S(1)} %get-tuple-element.77.x.refs_3_, ...), custom_call_target="tpu_custom_call" | custom-call | flops 17179869184 | bytes 4980740 | tf_op jit(solution)/shard_map/pallas_call | solution.py:39
  (172 shorter events, 67.7 us)
Async XLA Ops:
  1.9 9.3 %collective-permute-start = (bf16[2,256,256]{2,1,0:T(8,128)(2,1)S(1)}, bf16[2,256,256]{2,1,0:T(8,128)(2,1)S(1)}, u32[]{:S(2)}, u32[]{:S(2)}) collective-permute-start(bf16[2,256,256]{2,1,0:T(8,128)(2,1)S(1)} %get-tuple-element.54.refs_0_), channel_id=1, source_target_pairs={{0,2},{2,0},{4,6},{6,4},{8,10},{10,8},{12,14},{14,12},{16,18},{18,... | collective-permute-start | bytes 786440 | tf_op jit(solution)/shard_map/ppermute | solution.py:356
  4.9 10.0 %collective-permute-start.1 = (bf16[2,256,256]{2,1,0:T(8,128)(2,1)S(1)}, bf16[2,256,256]{2,1,0:T(8,128)(2,1)S(1)}, u32[]{:S(2)}, u32[]{:S(2)}) collective-permute-start(bf16[2,256,256]{2,1,0:T(8,128)(2,1)S(1)} %get-tuple-element.54.refs_0_), channel_id=1, source_target_pairs={{0,8},{2,10},{4,12},{6,14},{8,16},{10,18},{12,20},{14,22},{16,24},... | collective-permute-start | bytes 786440 | tf_op jit(solution)/shard_map/ppermute | solution.py:361
  8.4 22.1 %collective-permute-start.7 = (f32[256,512]{1,0:T(8,128)S(1)}, f32[256,512]{1,0:T(8,128)S(1)}, u32[]{:S(2)}, u32[]{:S(2)}) collective-permute-start(f32[256,512]{1,0:T(8,128)S(1)} %get-tuple-element.52.mine.x.refs_3_), channel_id=1, source_target_pairs={{0,1},{1,0},{2,3},{3,2},{4,5},{5,4},{6,7},{7,6},{8,9},{9,8},{10,11... | collective-permute-start | bytes 1572872 | tf_op jit(solution)/shard_map/ppermute | solution.py:352
  11.2 15.9 %collective-permute-start.3 = (bf16[2,256,256]{2,1,0:T(8,128)(2,1)S(1)}, bf16[2,256,256]{2,1,0:T(8,128)(2,1)S(1)}, u32[]{:S(2)}, u32[]{:S(2)}) collective-permute-start(bf16[2,256,256]{2,1,0:T(8,128)(2,1)S(1)} %get-tuple-element.54.refs_0_), channel_id=1, source_target_pairs={{0,4},{2,6},{8,12},{10,14},{4,16},{6,18},{16,20},{18,22},{12,24},{... | collective-permute-start | bytes 786440 | tf_op jit(solution)/shard_map/ppermute | solution.py:367
  14.9 12.2 %collective-permute-start.2 = (bf16[2,256,256]{2,1,0:T(8,128)(2,1)S(1)}, bf16[2,256,256]{2,1,0:T(8,128)(2,1)S(1)}, u32[]{:S(2)}, u32[]{:S(2)}) collective-permute-start(bf16[2,256,256]{2,1,0:T(8,128)(2,1)S(1)} %collective-permute-done.1.refs_2_), channel_id=1, source_target_pairs={{0,2},{2,0},{4,6},{6,4},{8,10},{10,8},{12,14},{14,12},{16,18},{18,... | collective-permute-start | bytes 786440 | tf_op jit(solution)/shard_map/ppermute | solution.py:356
  16.4 10.6 %collective-permute-start.5 = (bf16[2,256,256]{2,1,0:T(8,128)(2,1)S(1)}, bf16[2,256,256]{2,1,0:T(8,128)(2,1)S(1)}, u32[]{:S(2)}, u32[]{:S(2)}) collective-permute-start(bf16[2,256,256]{2,1,0:T(8,128)(2,1)S(1)} %collective-permute-done.1.refs_2_), channel_id=1, source_target_pairs={{0,4},{2,6},{4,0},{6,2},{8,12},{10,14},{12,8},{14,10},{16,20},{18,... | collective-permute-start | bytes 786440 | tf_op jit(solution)/shard_map/ppermute | solution.py:356
  28.4 9.6 %collective-permute-start.15 = (bf16[2,256,256]{2,1,0:T(8,128)(2,1)}, bf16[2,256,256]{2,1,0:T(8,128)(2,1)}, u32[]{:S(2)}, u32[]{:S(2)}) collective-permute-start(bf16[2,256,256]{2,1,0:T(8,128)(2,1)} %get-tuple-element.67), channel_id=1, source_target_pairs={{0,4},{2,6},{4,0},{6,2},{8,12},{10,14},{12,8},{14,10},{16,20},{18,... | collective-permute-start | bytes 786440 | tf_op jit(solution)/shard_map/ppermute | solution.py:356
  28.4 12.8 %collective-permute-start.8 = (bf16[2,256,256]{2,1,0:T(8,128)(2,1)S(1)}, bf16[2,256,256]{2,1,0:T(8,128)(2,1)S(1)}, u32[]{:S(2)}, u32[]{:S(2)}) collective-permute-start(bf16[2,256,256]{2,1,0:T(8,128)(2,1)S(1)} %collective-permute-done.refs_1_), channel_id=1, source_target_pairs={{0,1},{1,0},{2,3},{3,2},{4,5},{5,4},{6,7},{7,6},{8,9},{9,8},{10,11... | collective-permute-start | bytes 786440 | tf_op jit(solution)/shard_map/ppermute | solution.py:352
  28.5 24.3 %collective-permute-start.17 = (bf16[2,256,256]{2,1,0:T(8,128)(2,1)}, bf16[2,256,256]{2,1,0:T(8,128)(2,1)S(1)}, u32[]{:S(2)}, u32[]{:S(2)}) collective-permute-start(bf16[2,256,256]{2,1,0:T(8,128)(2,1)} %copy-done.1), channel_id=1, source_target_pairs={{0,4},{2,6},{4,0},{6,2},{8,12},{10,14},{12,8},{14,10},{16,20},{18,... | collective-permute-start | bytes 786440 | tf_op jit(solution)/shard_map/ppermute | solution.py:356
  30.5 9.4 %collective-permute-start.13 = (bf16[2,256,256]{2,1,0:T(8,128)(2,1)}, bf16[2,256,256]{2,1,0:T(8,128)(2,1)S(1)}, u32[]{:S(2)}, u32[]{:S(2)}) collective-permute-start(bf16[2,256,256]{2,1,0:T(8,128)(2,1)} %copy-done.8), channel_id=1, source_target_pairs={{0,2},{2,0},{4,6},{6,4},{8,10},{10,8},{12,14},{14,12},{16,18},{18,... | collective-permute-start | bytes 786440 | tf_op jit(solution)/shard_map/ppermute | solution.py:356
  30.5 15.0 %collective-permute-start.4 = (bf16[2,256,256]{2,1,0:T(8,128)(2,1)}, bf16[2,256,256]{2,1,0:T(8,128)(2,1)S(1)}, u32[]{:S(2)}, u32[]{:S(2)}) collective-permute-start(bf16[2,256,256]{2,1,0:T(8,128)(2,1)} %copy-done.2), channel_id=1, source_target_pairs={{0,2},{2,0},{4,6},{6,4},{8,10},{10,8},{12,14},{14,12},{16,18},{18,... | collective-permute-start | bytes 786440 | tf_op jit(solution)/shard_map/ppermute | solution.py:356
  38.0 10.0 %collective-permute-start.6 = (bf16[2,256,256]{2,1,0:T(8,128)(2,1)S(1)}, bf16[2,256,256]{2,1,0:T(8,128)(2,1)S(1)}, u32[]{:S(2)}, u32[]{:S(2)}) collective-permute-start(bf16[2,256,256]{2,1,0:T(8,128)(2,1)S(1)} %copy-done.5), channel_id=1, source_target_pairs={{0,4},{2,6},{4,0},{6,2},{8,12},{10,14},{12,8},{14,10},{16,20},{18,... | collective-permute-start | bytes 786440 | tf_op jit(solution)/shard_map/ppermute | solution.py:356
  39.8 16.5 %collective-permute-start.16 = (bf16[2,256,256]{2,1,0:T(8,128)(2,1)S(1)}, bf16[2,256,256]{2,1,0:T(8,128)(2,1)S(1)}, u32[]{:S(2)}, u32[]{:S(2)}) collective-permute-start(bf16[2,256,256]{2,1,0:T(8,128)(2,1)S(1)} %add_convert_fusion.4), channel_id=1, source_target_pairs={{0,2},{2,0},{4,6},{6,4},{8,10},{10,8},{12,14},{14,12},{16,18},{18,... | collective-permute-start | bytes 786440 | tf_op jit(solution)/shard_map/ppermute | solution.py:356
  41.3 26.5 %collective-permute-start.14 = (bf16[2,256,256]{2,1,0:T(8,128)(2,1)}, bf16[2,256,256]{2,1,0:T(8,128)(2,1)S(1)}, u32[]{:S(2)}, u32[]{:S(2)}) collective-permute-start(bf16[2,256,256]{2,1,0:T(8,128)(2,1)} %add_convert_fusion.5), channel_id=1, source_target_pairs={{4,0},{6,2},{12,8},{14,10},{16,4},{18,6},{20,16},{22,18},{24,12},{... | collective-permute-start | bytes 786440 | tf_op jit(solution)/shard_map/ppermute | solution.py:367
  52.8 10.3 %collective-permute-start.10 = (f32[224,256]{1,0:T(8,128)S(1)}, f32[224,256]{1,0:T(8,128)S(1)}, u32[]{:S(2)}, u32[]{:S(2)}) collective-permute-start(f32[224,256]{1,0:T(8,128)S(1)} %get-tuple-element.112), channel_id=1, source_target_pairs={{0,4},{2,6},{4,0},{6,2},{8,12},{10,14},{12,8},{14,10},{16,20},{18,... | collective-permute-start | bytes 688136 | tf_op jit(solution)/shard_map/ppermute | solution.py:356
  52.8 11.7 %collective-permute-start.11 = (f32[224,256]{1,0:T(8,128)}, f32[224,256]{1,0:T(8,128)}, u32[]{:S(2)}, u32[]{:S(2)}) collective-permute-start(f32[224,256]{1,0:T(8,128)} %get-tuple-element.111), channel_id=1, source_target_pairs={{0,6},{2,4},{4,2},{6,0},{8,14},{10,12},{12,10},{14,8},{16,22},{18,... | collective-permute-start | bytes 688136 | tf_op jit(solution)/shard_map/ppermute | solution.py:356
  52.8 13.7 %collective-permute-start.9 = (f32[224,256]{1,0:T(8,128)}, f32[224,256]{1,0:T(8,128)}, u32[]{:S(2)}, u32[]{:S(2)}) collective-permute-start(f32[224,256]{1,0:T(8,128)} %get-tuple-element.110), channel_id=1, source_target_pairs={{0,2},{2,0},{4,6},{6,4},{8,10},{10,8},{12,14},{14,12},{16,18},{18,... | collective-permute-start | bytes 688136 | tf_op jit(solution)/shard_map/ppermute | solution.py:356
  56.3 13.0 %collective-permute-start.12 = (bf16[2,256,256]{2,1,0:T(8,128)(2,1)S(1)}, bf16[2,256,256]{2,1,0:T(8,128)(2,1)S(1)}, u32[]{:S(2)}, u32[]{:S(2)}) collective-permute-start(bf16[2,256,256]{2,1,0:T(8,128)(2,1)S(1)} %get-tuple-element.59), channel_id=1, source_target_pairs={{0,2},{2,0},{4,6},{6,4},{8,10},{10,8},{12,14},{14,12},{16,18},{18,... | collective-permute-start | bytes 786440 | tf_op jit(solution)/shard_map/ppermute | solution.py:356
  63.0 11.4 %collective-permute-start.18 = (bf16[2,256,256]{2,1,0:T(8,128)(2,1)S(1)}, bf16[2,256,256]{2,1,0:T(8,128)(2,1)S(1)}, u32[]{:S(2)}, u32[]{:S(2)}) collective-permute-start(bf16[2,256,256]{2,1,0:T(8,128)(2,1)S(1)} %add_convert_fusion.3), channel_id=1, source_target_pairs={{8,0},{10,2},{12,4},{14,6},{16,8},{18,10},{20,12},{22,14},{24,16},... | collective-permute-start | bytes 786440 | tf_op jit(solution)/shard_map/ppermute | solution.py:361
  90.5 8.8 %collective-permute-start.26 = (f32[152,256]{1,0:T(8,128)S(1)}, f32[152,256]{1,0:T(8,128)S(1)}, u32[]{:S(2)}, u32[]{:S(2)}) collective-permute-start(f32[152,256]{1,0:T(8,128)S(1)} %constant_dynamic-update-slice_fusion), channel_id=1, source_target_pairs={{0,24},{2,26},{4,28},{6,30},{8,16},{10,18},{12,20},{14,22},{16,8},... | collective-permute-start | bytes 466952 | tf_op jit(solution)/shard_map/ppermute | solution.py:356
  91.9 13.3 %collective-permute-start.27 = (f32[152,256]{1,0:T(8,128)S(1)}, f32[152,256]{1,0:T(8,128)S(1)}, u32[]{:S(2)}, u32[]{:S(2)}) collective-permute-start(f32[152,256]{1,0:T(8,128)S(1)} %constant_dynamic-update-slice_fusion), channel_id=1, source_target_pairs={{0,16},{2,18},{4,20},{6,22},{8,24},{10,26},{12,28},{14,30},{16,0},... | collective-permute-start | bytes 466952 | tf_op jit(solution)/shard_map/ppermute | solution.py:356
  92.8 12.5 %collective-permute-start.28 = (f32[152,256]{1,0:T(8,128)S(1)}, f32[152,256]{1,0:T(8,128)S(1)}, u32[]{:S(2)}, u32[]{:S(2)}) collective-permute-start(f32[152,256]{1,0:T(8,128)S(1)} %constant_dynamic-update-slice_fusion), channel_id=1, source_target_pairs={{0,8},{2,10},{4,12},{6,14},{8,0},{10,2},{12,4},{14,6},{16,24},{18,... | collective-permute-start | bytes 466952 | tf_op jit(solution)/shard_map/ppermute | solution.py:356
  105.4 11.6 %collective-permute-start.29 = (f32[320,256]{1,0:T(8,128)S(1)}, f32[320,256]{1,0:T(8,128)S(1)}, u32[]{:S(2)}, u32[]{:S(2)}) collective-permute-start(f32[320,256]{1,0:T(8,128)S(1)} %fusion.5), channel_id=1, source_target_pairs={{0,6},{2,4},{4,2},{6,0},{8,14},{10,12},{12,10},{14,8},{16,22},{18,... | collective-permute-start | bytes 983048 | tf_op jit(solution)/shard_map/ppermute | solution.py:356
  106.2 14.9 %collective-permute-start.30 = (f32[320,256]{1,0:T(8,128)S(1)}, f32[320,256]{1,0:T(8,128)S(1)}, u32[]{:S(2)}, u32[]{:S(2)}) collective-permute-start(f32[320,256]{1,0:T(8,128)S(1)} %fusion.5), channel_id=1, source_target_pairs={{0,4},{2,6},{4,0},{6,2},{8,12},{10,14},{12,8},{14,10},{16,20},{18,... | collective-permute-start | bytes 983048 | tf_op jit(solution)/shard_map/ppermute | solution.py:356
  107.8 14.7 %collective-permute-start.31 = (f32[320,256]{1,0:T(8,128)S(1)}, f32[320,256]{1,0:T(8,128)}, u32[]{:S(2)}, u32[]{:S(2)}) collective-permute-start(f32[320,256]{1,0:T(8,128)S(1)} %fusion.5), channel_id=1, source_target_pairs={{0,2},{2,0},{4,6},{6,4},{8,10},{10,8},{12,14},{14,12},{16,18},{18,... | collective-permute-start | bytes 983048 | tf_op jit(solution)/shard_map/ppermute | solution.py:356
  140.0 8.4 %collective-permute-start.33 = (bf16[2,256,256]{2,1,0:T(8,128)(2,1)S(1)}, bf16[2,256,256]{2,1,0:T(8,128)(2,1)S(1)}, u32[]{:S(2)}, u32[]{:S(2)}) collective-permute-start(bf16[2,256,256]{2,1,0:T(8,128)(2,1)S(1)} %get-tuple-element.79.refs_0_), channel_id=1, source_target_pairs={{0,2},{2,0},{4,6},{6,4},{8,10},{10,8},{12,14},{14,12},{16,18},{18,... | collective-permute-start | bytes 786440 | tf_op jit(solution)/shard_map/ppermute | solution.py:356
  140.2 10.6 %collective-permute-start.34 = (bf16[2,256,256]{2,1,0:T(8,128)(2,1)S(1)}, bf16[2,256,256]{2,1,0:T(8,128)(2,1)S(1)}, u32[]{:S(2)}, u32[]{:S(2)}) collective-permute-start(bf16[2,256,256]{2,1,0:T(8,128)(2,1)S(1)} %get-tuple-element.79.refs_0_), channel_id=1, source_target_pairs={{0,8},{2,10},{4,12},{6,14},{8,16},{10,18},{12,20},{14,22},{16,24},... | collective-permute-start | bytes 786440 | tf_op jit(solution)/shard_map/ppermute | solution.py:361
  148.4 9.1 %collective-permute-start.36 = (bf16[2,256,256]{2,1,0:T(8,128)(2,1)S(1)}, bf16[2,256,256]{2,1,0:T(8,128)(2,1)S(1)}, u32[]{:S(2)}, u32[]{:S(2)}) collective-permute-start(bf16[2,256,256]{2,1,0:T(8,128)(2,1)S(1)} %get-tuple-element.79.refs_0_), channel_id=1, source_target_pairs={{0,4},{2,6},{8,12},{10,14},{4,16},{6,18},{16,20},{18,22},{12,24},{... | collective-permute-start | bytes 786440 | tf_op jit(solution)/shard_map/ppermute | solution.py:367
  151.3 10.2 %collective-permute-start.38 = (bf16[2,256,256]{2,1,0:T(8,128)(2,1)S(1)}, bf16[2,256,256]{2,1,0:T(8,128)(2,1)S(1)}, u32[]{:S(2)}, u32[]{:S(2)}) collective-permute-start(bf16[2,256,256]{2,1,0:T(8,128)(2,1)S(1)} %collective-permute-done.34.refs_2_), channel_id=1, source_target_pairs={{0,4},{2,6},{4,0},{6,2},{8,12},{10,14},{12,8},{14,10},{16,20},{18,... | collective-permute-start | bytes 786440 | tf_op jit(solution)/shard_map/ppermute | solution.py:356
  161.5 7.3 %collective-permute-start.48 = (bf16[2,256,256]{2,1,0:T(8,128)(2,1)S(1)}, bf16[2,256,256]{2,1,0:T(8,128)(2,1)S(1)}, u32[]{:S(2)}, u32[]{:S(2)}) collective-permute-start(bf16[2,256,256]{2,1,0:T(8,128)(2,1)S(1)} %get-tuple-element.92), channel_id=1, source_target_pairs={{0,4},{2,6},{4,0},{6,2},{8,12},{10,14},{12,8},{14,10},{16,20},{18,... | collective-permute-start | bytes 786440 | tf_op jit(solution)/shard_map/ppermute | solution.py:356
  164.0 9.2 %collective-permute-start.40 = (f32[256,512]{1,0:T(8,128)S(1)}, f32[256,512]{1,0:T(8,128)S(1)}, u32[]{:S(2)}, u32[]{:S(2)}) collective-permute-start(f32[256,512]{1,0:T(8,128)S(1)} %get-tuple-element.77.x.refs_3_), channel_id=1, source_target_pairs={{0,1},{1,0},{2,3},{3,2},{4,5},{5,4},{6,7},{7,6},{8,9},{9,8},{10,11... | collective-permute-start | bytes 1572872 | tf_op jit(solution)/shard_map/ppermute | solution.py:352
  164.0 9.1 %collective-permute-start.46 = (bf16[2,256,256]{2,1,0:T(8,128)(2,1)S(1)}, bf16[2,256,256]{2,1,0:T(8,128)(2,1)S(1)}, u32[]{:S(2)}, u32[]{:S(2)}) collective-permute-start(bf16[2,256,256]{2,1,0:T(8,128)(2,1)S(1)} %get-tuple-element.89), channel_id=1, source_target_pairs={{0,2},{2,0},{4,6},{6,4},{8,10},{10,8},{12,14},{14,12},{16,18},{18,... | collective-permute-start | bytes 786440 | tf_op jit(solution)/shard_map/ppermute | solution.py:356
  164.3 9.2 %collective-permute-start.41 = (bf16[2,256,256]{2,1,0:T(8,128)(2,1)S(1)}, bf16[2,256,256]{2,1,0:T(8,128)(2,1)S(1)}, u32[]{:S(2)}, u32[]{:S(2)}) collective-permute-start(bf16[2,256,256]{2,1,0:T(8,128)(2,1)S(1)} %collective-permute-done.33.refs_1_), channel_id=1, source_target_pairs={{0,1},{1,0},{2,3},{3,2},{4,5},{5,4},{6,7},{7,6},{8,9},{9,8},{10,11... | collective-permute-start | bytes 786440 | tf_op jit(solution)/shard_map/ppermute | solution.py:352
  164.5 14.1 %collective-permute-start.37 = (bf16[2,256,256]{2,1,0:T(8,128)(2,1)S(1)}, bf16[2,256,256]{2,1,0:T(8,128)(2,1)S(1)}, u32[]{:S(2)}, u32[]{:S(2)}) collective-permute-start(bf16[2,256,256]{2,1,0:T(8,128)(2,1)S(1)} %collective-permute-done.36.refs_4_), channel_id=1, source_target_pairs={{0,2},{2,0},{4,6},{6,4},{8,10},{10,8},{12,14},{14,12},{16,18},{18,... | collective-permute-start | bytes 786440 | tf_op jit(solution)/shard_map/ppermute | solution.py:356
  168.8 9.9 %collective-permute-start.39 = (bf16[2,256,256]{2,1,0:T(8,128)(2,1)S(1)}, bf16[2,256,256]{2,1,0:T(8,128)(2,1)S(1)}, u32[]{:S(2)}, u32[]{:S(2)}) collective-permute-start(bf16[2,256,256]{2,1,0:T(8,128)(2,1)S(1)} %collective-permute-done.35.refs_3_), channel_id=1, source_target_pairs={{0,4},{2,6},{4,0},{6,2},{8,12},{10,14},{12,8},{14,10},{16,20},{18,... | collective-permute-start | bytes 786440 | tf_op jit(solution)/shard_map/ppermute | solution.py:356
  173.1 10.2 %collective-permute-start.50 = (bf16[2,256,256]{2,1,0:T(8,128)(2,1)S(1)}, bf16[2,256,256]{2,1,0:T(8,128)(2,1)S(1)}, u32[]{:S(2)}, u32[]{:S(2)}) collective-permute-start(bf16[2,256,256]{2,1,0:T(8,128)(2,1)S(1)} %get-tuple-element.93), channel_id=1, source_target_pairs={{0,4},{2,6},{4,0},{6,2},{8,12},{10,14},{12,8},{14,10},{16,20},{18,... | collective-permute-start | bytes 786440 | tf_op jit(solution)/shard_map/ppermute | solution.py:356
  173.1 12.9 %collective-permute-start.49 = (bf16[2,256,256]{2,1,0:T(8,128)(2,1)S(1)}, bf16[2,256,256]{2,1,0:T(8,128)(2,1)S(1)}, u32[]{:S(2)}, u32[]{:S(2)}) collective-permute-start(bf16[2,256,256]{2,1,0:T(8,128)(2,1)S(1)} %add_convert_fusion.1), channel_id=1, source_target_pairs={{0,2},{2,0},{4,6},{6,4},{8,10},{10,8},{12,14},{14,12},{16,18},{18,... | collective-permute-start | bytes 786440 | tf_op jit(solution)/shard_map/ppermute | solution.py:356
  173.6 19.9 %collective-permute-start.47 = (bf16[2,256,256]{2,1,0:T(8,128)(2,1)S(1)}, bf16[2,256,256]{2,1,0:T(8,128)(2,1)S(1)}, u32[]{:S(2)}, u32[]{:S(2)}) collective-permute-start(bf16[2,256,256]{2,1,0:T(8,128)(2,1)S(1)} %add_convert_fusion.2), channel_id=1, source_target_pairs={{4,0},{6,2},{12,8},{14,10},{16,4},{18,6},{20,16},{22,18},{24,12},{... | collective-permute-start | bytes 786440 | tf_op jit(solution)/shard_map/ppermute | solution.py:367
  182.5 10.9 %collective-permute-start.43 = (f32[128,256]{1,0:T(8,128)S(1)}, f32[128,256]{1,0:T(8,128)S(1)}, u32[]{:S(2)}, u32[]{:S(2)}) collective-permute-start(f32[128,256]{1,0:T(8,128)S(1)} %get-tuple-element.115), channel_id=1, source_target_pairs={{0,4},{2,6},{4,0},{6,2},{8,12},{10,14},{12,8},{14,10},{16,20},{18,... | collective-permute-start | bytes 393224 | tf_op jit(solution)/shard_map/ppermute | solution.py:356
  183.3 10.2 %collective-permute-start.44 = (f32[128,256]{1,0:T(8,128)S(1)}, f32[128,256]{1,0:T(8,128)S(1)}, u32[]{:S(2)}, u32[]{:S(2)}) collective-permute-start(f32[128,256]{1,0:T(8,128)S(1)} %get-tuple-element.114), channel_id=1, source_target_pairs={{0,6},{2,4},{4,2},{6,0},{8,14},{10,12},{12,10},{14,8},{16,22},{18,... | collective-permute-start | bytes 393224 | tf_op jit(solution)/shard_map/ppermute | solution.py:356
  186.0 9.7 %collective-permute-start.45 = (bf16[2,256,256]{2,1,0:T(8,128)(2,1)S(1)}, bf16[2,256,256]{2,1,0:T(8,128)(2,1)S(1)}, u32[]{:S(2)}, u32[]{:S(2)}) collective-permute-start(bf16[2,256,256]{2,1,0:T(8,128)(2,1)S(1)} %get-tuple-element.84), channel_id=1, source_target_pairs={{0,2},{2,0},{4,6},{6,4},{8,10},{10,8},{12,14},{14,12},{16,18},{18,... | collective-permute-start | bytes 786440 | tf_op jit(solution)/shard_map/ppermute | solution.py:356
  188.9 10.1 %collective-permute-start.51 = (bf16[2,256,256]{2,1,0:T(8,128)(2,1)S(1)}, bf16[2,256,256]{2,1,0:T(8,128)(2,1)S(1)}, u32[]{:S(2)}, u32[]{:S(2)}) collective-permute-start(bf16[2,256,256]{2,1,0:T(8,128)(2,1)S(1)} %add_convert_fusion), channel_id=1, source_target_pairs={{8,0},{10,2},{12,4},{14,6},{16,8},{18,10},{20,12},{22,14},{24,16},... | collective-permute-start | bytes 786440 | tf_op jit(solution)/shard_map/ppermute | solution.py:361
  213.6 8.3 %collective-permute-start.59 = (f32[128,256]{1,0:T(8,128)S(1)}, f32[128,256]{1,0:T(8,128)S(1)}, u32[]{:S(2)}, u32[]{:S(2)}) collective-permute-start(f32[128,256]{1,0:T(8,128)S(1)} %constant_dynamic-update-slice_fusion.2), channel_id=1, source_target_pairs={{0,24},{2,26},{4,28},{6,30},{8,16},{10,18},{12,20},{14,22},{16,8},... | collective-permute-start | bytes 393224 | tf_op jit(solution)/shard_map/ppermute | solution.py:356
  216.7 9.7 %collective-permute-start.60 = (f32[128,256]{1,0:T(8,128)S(1)}, f32[128,256]{1,0:T(8,128)S(1)}, u32[]{:S(2)}, u32[]{:S(2)}) collective-permute-start(f32[128,256]{1,0:T(8,128)S(1)} %constant_dynamic-update-slice_fusion.2), channel_id=1, source_target_pairs={{0,16},{2,18},{4,20},{6,22},{8,24},{10,26},{12,28},{14,30},{16,0},... | collective-permute-start | bytes 393224 | tf_op jit(solution)/shard_map/ppermute | solution.py:356
  216.7 9.7 %collective-permute-start.61 = (f32[128,256]{1,0:T(8,128)S(1)}, f32[128,256]{1,0:T(8,128)S(1)}, u32[]{:S(2)}, u32[]{:S(2)}) collective-permute-start(f32[128,256]{1,0:T(8,128)S(1)} %constant_dynamic-update-slice_fusion.2), channel_id=1, source_target_pairs={{0,8},{2,10},{4,12},{6,14},{8,0},{10,2},{12,4},{14,6},{16,24},{18,... | collective-permute-start | bytes 393224 | tf_op jit(solution)/shard_map/ppermute | solution.py:356
  226.5 9.5 %collective-permute-start.62 = (f32[224,256]{1,0:T(8,128)S(1)}, f32[224,256]{1,0:T(8,128)S(1)}, u32[]{:S(2)}, u32[]{:S(2)}) collective-permute-start(f32[224,256]{1,0:T(8,128)S(1)} %fusion.4), channel_id=1, source_target_pairs={{0,6},{2,4},{4,2},{6,0},{8,14},{10,12},{12,10},{14,8},{16,22},{18,... | collective-permute-start | bytes 688136 | tf_op jit(solution)/shard_map/ppermute | solution.py:356
  228.1 10.5 %collective-permute-start.63 = (f32[224,256]{1,0:T(8,128)S(1)}, f32[224,256]{1,0:T(8,128)S(1)}, u32[]{:S(2)}, u32[]{:S(2)}) collective-permute-start(f32[224,256]{1,0:T(8,128)S(1)} %fusion.4), channel_id=1, source_target_pairs={{0,4},{2,6},{4,0},{6,2},{8,12},{10,14},{12,8},{14,10},{16,20},{18,... | collective-permute-start | bytes 688136 | tf_op jit(solution)/shard_map/ppermute | solution.py:356
  228.8 9.8 %collective-permute-start.64 = (f32[224,256]{1,0:T(8,128)S(1)}, f32[224,256]{1,0:T(8,128)S(1)}, u32[]{:S(2)}, u32[]{:S(2)}) collective-permute-start(f32[224,256]{1,0:T(8,128)S(1)} %fusion.4), channel_id=1, source_target_pairs={{0,2},{2,0},{4,6},{6,4},{8,10},{10,8},{12,14},{14,12},{16,18},{18,... | collective-permute-start | bytes 688136 | tf_op jit(solution)/shard_map/ppermute | solution.py:356
  (37 other events, 219.1 us)

commit v3 on v2

--- a/solution.py
+++ b/solution.py
@@ -13,6 +13,7 @@
 f32, bf16 = jnp.float32, jnp.bfloat16
 SEGMENT_KINDS = (f32, f32, f32, f32, f32, bf16, bf16, bf16)
 TILES_VMEM = 48
+SCALARS = 4
 VMEM, SMEM = pltpu.VMEM, pltpu.SMEM
 
 
@@ -51,6 +52,26 @@
     return jax.ShapeDtypeStruct(dims, dtype)
 
 
+def fold(a):
+    half, quarter = a.shape[0] // 2, a.shape[0] // 4
+    below = a[half:, :half]
+    return jnp.concatenate(
+        [
+            jnp.concatenate([a[:half, :half], a[half:, half:]], axis=1),
+            jnp.concatenate([below[:quarter], below[quarter:]], axis=1),
+        ],
+        axis=0,
+    )
+
+
+def unfold(a):
+    half = a.shape[1] // 2
+    below = jnp.concatenate([a[half:, :half], a[half:, half:]], axis=0)
+    return jnp.concatenate(
+        [jnp.concatenate([a[:half, :half], below.T], axis=1), jnp.concatenate([below, a[:half, half:]], axis=1)], axis=0
+    )
+
+
 def pack_kernel(vectors, columns, chunk):
     size = chunk.shape[2]
     for t in range(chunk.shape[0]):
@@ -71,7 +92,7 @@
     return [pltpu.make_async_copy(piece, window.at[pl.ds(2 * s, 2)], sems.at[s]) for s, piece in enumerate(pieces)]
 
 
-def each_tile(meta, rows, cols, blocks, tiles, sems, ready, product, total):
+def each_tile(meta, blocks, tiles, sems, ready, product, total):
     used = meta[0]
     groups = (used + GROUP - 1) // GROUP
 
@@ -96,7 +117,7 @@
         found = []
         for k in range(GROUP):
             slot = group * GROUP + k
-            row, col = rows[slot], cols[slot]
+            row, col = meta[SCALARS + slot], meta[SCALARS + blocks.shape[0] + slot]
             weight = jnp.where(slot < used, jnp.where(row == col, 0.5, 1.0), 0.0).astype(f32)
             found.append(product(tiles[slot], place(row, meta), place(col, meta)) + (weight,))
         for at, part, weight in found:
@@ -106,19 +127,19 @@
     lax.fori_loop(0, groups, multiply, 0)
 
 
-def mirror_kernel(meta, rows, cols, *refs):
+def mirror_kernel(meta, *refs):
     pieces, blocks, out = refs[:2], refs[2], refs[3:-5]
     window, total, tiles, piece_sems, tile_sems = refs[-5:]
 
     def product(tile, row, col):
         return col, dot_nn(window[row], tile)
 
-    each_tile(meta, rows, cols, blocks, tiles, tile_sems, gather(pieces, window, piece_sems), product, total)
+    each_tile(meta, blocks, tiles, tile_sems, gather(pieces, window, piece_sems), product, total)
     for s, segment in enumerate(out):
         segment[...] = total[pl.ds(2 * s, 2)].astype(segment.dtype)
 
 
-def direct_kernel(meta, rows, cols, *refs):
+def direct_kernel(meta, *refs):
     pieces, blocks = refs[: 2 * REACH], refs[2 * REACH]
     x_other, cross_other, kept, near, kept_out, near_out, inner = refs[2 * REACH + 1 : -5]
     window, total, tiles, piece_sems, tile_sems = refs[-5:]
@@ -126,7 +147,7 @@
     def product(tile, row, col):
         return row, dot_nt(window[col], tile)
 
-    each_tile(meta, rows, cols, blocks, tiles, tile_sems, gather(pieces, window, piece_sems), product, total)
+    each_tile(meta, blocks, tiles, tile_sems, gather(pieces, window, piece_sems), product, total)
     kept_out[...] = kept[...] + total[pl.ds(0, 2)]
     near_out[...] = (near[...] + total[pl.ds(2, 2)]).astype(bf16)
     size = inner.shape[1]
@@ -137,15 +158,15 @@
         there = x_other[:, pl.ds(s * size, size)].astype(bf16) if s < 2 else cross_other[s - 2]
         own += dot_nt(mine, window[s])
         other += dot_nt(mine, there)
-    inner[pl.ds(0, size), :] = own + own.T
-    inner[pl.ds(size, size), :] = other
-
-
-def tiles_call(kernel, out, meta, blocks, rows, cols, pieces, more, window, total):
+    inner[pl.ds(0, 3 * size // 4), :] = fold(own + own.T)
+    inner[pl.ds(3 * size // 4, size), :] = other
+
+
+def tiles_call(kernel, out, meta, blocks, pieces, more, window, total):
     size, width = blocks.shape[1], pieces[0].shape[1]
     return pl.pallas_call(
         kernel,
-        in_specs=[pl.BlockSpec(memory_space=SMEM)] * 3
+        in_specs=[pl.BlockSpec(memory_space=SMEM)]
         + [pl.BlockSpec(memory_space=pl.ANY)] * len(pieces)
         + [pl.BlockSpec(memory_space=pltpu.HBM)]
         + [pl.BlockSpec(memory_space=VMEM)] * len(more),
@@ -160,7 +181,7 @@
         out_shape=out,
         compiler_params=pltpu.CompilerParams(vmem_limit_bytes=TILES_VMEM << 20),
         cost_estimate=pl.CostEstimate(flops=4 << 30, bytes_accessed=12 << 20, transcendentals=0),
-    )(meta, rows, cols, *pieces, blocks, *more)
+    )(meta, *pieces, blocks, *more)
 
 
 def descend_kernel(x, kept, near, far, two, out):
@@ -175,11 +196,11 @@
     width = mine.shape[0]
     half = width // 2
     own, other = split(mine[...]), split(theirs[...])
-    out[pl.ds(0, width), :] = dot3(dot_nt, own, own)
+    out[pl.ds(0, 3 * width // 4), :] = fold(dot3(dot_nt, own, own))
     ahead = core[0] == 0
     high = jnp.where(ahead, theirs[pl.ds(0, half), :], mine[pl.ds(half, half), :])
     low = [jnp.where(ahead, a, b) for a, b in zip(own, other)]
-    out[pl.ds(width, half), :] = dot3(dot_nt, split(high), low)
+    out[pl.ds(3 * width // 4, half), :] = dot3(dot_nt, split(high), low)
 
 
 def inverse_factor(g, w, high, low):
@@ -287,9 +308,10 @@
 
 def lay_out(out, first, second):
     width = first.shape[1]
-    out[pl.ds(0, width), pl.ds(0, width)] = first[:width]
-    out[pl.ds(width, width), pl.ds(width, width)] = second[:width]
-    below = jnp.concatenate([first[width:], second[width:]], axis=0)
+    folded = 3 * width // 4
+    out[pl.ds(0, width), pl.ds(0, width)] = unfold(first[:folded])
+    out[pl.ds(width, width), pl.ds(width, width)] = unfold(second[:folded])
+    below = jnp.concatenate([first[folded:], second[folded:]], axis=0)
     out[pl.ds(width, width), pl.ds(0, width)] = below
     out[pl.ds(0, width), pl.ds(width, width)] = below.T
 
@@ -304,22 +326,24 @@
         return jnp.where(ahead, mine, theirs), jnp.where(ahead, theirs, mine)
 
     blocks, rows, _ = sums.shape
-    cut = rows - (width + width // 2) // blocks
+    cut = rows - 5 * width // 4 // blocks
+    folded, extra = 3 * width // 4, 7 * width // 4
 
     def joined(ref, low, high):
         return jnp.concatenate([ref[block, pl.ds(low, high - low), :] for block in range(blocks)], axis=0)
 
     inner, inner_other = joined(sums, 0, cut), joined(sums_other, 0, cut)
-    first, second = ordered(inner[: 2 * width], inner_other[: 2 * width])
-    rayleigh[pl.ds(0, width), pl.ds(0, width)] = first[:width]
-    rayleigh[pl.ds(width, width), pl.ds(width, width)] = second[:width]
-    across = first[width:] + second[width:].T
+    first, second = ordered(inner[:extra], inner_other[:extra])
+    rayleigh[pl.ds(0, width), pl.ds(0, width)] = unfold(first[:folded])
+    rayleigh[pl.ds(width, width), pl.ds(width, width)] = unfold(second[:folded])
+    across = first[folded:] + second[folded:].T
     rayleigh[pl.ds(0, width), pl.ds(width, width)] = across
     rayleigh[pl.ds(width, width), pl.ds(0, width)] = across.T
     lay_out(g, *ordered(joined(sums, cut, rows), joined(sums_other, cut, rows)))
     r = split(rayleigh[...])
     if first_step:
-        lay_out(w, *ordered(inner[2 * width :], inner_other[2 * width :]))
+        end = extra + 5 * width // 4
+        lay_out(w, *ordered(inner[extra:end], inner_other[extra:end]))
         turned = dot3(dot_nn, split(w[...]), r)
         g[...] += STEP_RATE * (turned + turned.T)
         g[...] += dot3(dot_nn, r, split(STEP_RATE**2 * turned - (2 * STEP_RATE**2) * rayleigh[...]))
@@ -435,6 +459,7 @@
     position = lax.axis_index("patch")
     odd = position % 2
     meta = jnp.stack([block_count[0], 2 * (position - odd) - 4 * (REACH - 1), odd, position // 2 % 2]).astype(jnp.int32)
+    meta = jnp.concatenate([meta, block_row, block_col])
     core = lax.axis_index("vec").astype(jnp.int32).reshape(1)
     stages = stages_of()
     flat, chunk = shape(f32, width, count), shape(bf16, count // size, width, size)
@@ -444,7 +469,7 @@
         own_x = flip(u, 1)
         x_other = swap_cores(x)
         cross_other = swap_cores(own_x)
-        table = (meta, blocks, block_row, block_col)
+        table = (meta, blocks)
         segment = (2, width, size)
         sums = tiles_call(
             mirror_kernel, [shape(kind, *segment) for kind in SEGMENT_KINDS], *table, [u, own_x], [], 4, 4 * REACH
@@ -455,7 +480,7 @@
         pieces = [u, own_x, two, two_x, far, flip(far, 1), side, flip(two_x, 2)]
         kept, near, inner = tiles_call(
             direct_kernel,
-            [shape(f32, *segment), shape(bf16, *segment), shape(f32, 2 * width, width)],
+            [shape(f32, *segment), shape(bf16, *segment), shape(f32, 7 * width // 4, width)],
             *table,
             pieces,
             [x_other, cross_other, same[0], cross[0]],
@@ -468,12 +493,14 @@
         two = shift((same[1] + (two_x.astype(f32) + side.astype(f32))).astype(bf16), -2)
         inner_out = [inner]
         if step == 0:
-            inner_out += call(gram_kernel, [shape(f32, width + width // 2, width)], [core, x, x_other], smem=1)
-        inner = scatter(jnp.concatenate(inner_out), stages[0])
+            inner_out += call(gram_kernel, [shape(f32, 5 * width // 4, width)], [core, x, x_other], smem=1)
+        inner = jnp.concatenate(inner_out)
+        inner = jnp.pad(inner, ((0, -inner.shape[0] % lax.axis_size("patch")), (0, 0)))
+        inner = scatter(inner, stages[0])
         inner, *joined = together(inner, flip(near, 1), far, two)
         (v,) = call(descend_kernel, [flat], [x, kept, *joined])
         v_other = swap_cores(v)
-        (gram,) = call(gram_kernel, [shape(f32, width + width // 2, width)], [core, v, v_other], smem=1)
+        (gram,) = call(gram_kernel, [shape(f32, 5 * width // 4, width)], [core, v, v_other], smem=1)
         inner, gram = together(inner, gram)
         sums = sum_both(inner, gram, stages)
         full = (2 * width, 2 * width)

time: 252 us -> 244 us (0.968)
  waiting for transfers between devices: 119 us -> 106 us
  starting transfers between devices: 76.3 us -> 83.7 us
    ppermute x50, waiting for transfers between devices: 98.8 us -> 81.9 us  [flip(): lax.ppermute(a, 'patch', [(i, i ^ mask) for i in range(lax.axis_size('pat...]
    ppermute x50, starting transfers between devices: 59.2 us -> 66 us  [flip(): lax.ppermute(a, 'patch', [(i, i ^ mask) for i in range(lax.axis_size('pat...]
    ppermute x4, waiting for transfers between devices: 8.64 us -> 12.6 us  [shift(): lax.ppermute(a, 'patch', [(i - 2 * pairs, i) for i in devices if i - 2 *...]
    unnamed x40 -> x31, local copies, waits for them, and re-layouts: 6.78 us -> 5.47 us
  transfers between devices with their start and end apart: 66 -> 66, of which waited for: 40 -> 36; matrix products, arithmetic and copies ran while one was open for 2% -> 2% of each run, Pallas kernels for 6% -> 6%
where the time goes in v3:
time: 244 us
  waiting for transfers between devices  106 us (43%)
  starting transfers between devices  83.7 us (34%)
  Pallas kernels  41 us (17%)
  local copies, waits for them, and re-layouts  7.48 us (3%)
  other arithmetic  4.63 us (2%)
    ppermute x50, waiting for transfers between devices, flip(): lax.ppermute(a, 'patch', [(i, i ^ mask) for i in range(lax.axis_size('pat...  81.9 us
    ppermute x50, starting transfers between devices, flip(): lax.ppermute(a, 'patch', [(i, i ^ mask) for i in range(lax.axis_size('pat...  66 us
    pallas_call x8, Pallas kernels, call(): pl.pallas_call(kernel, out_shape=out, in_specs=[pl.BlockSpec(memory_space...  26.8 us
    pallas_call x4, Pallas kernels, tiles_call(): pl.pallas_call(kernel, in_specs=[pl.BlockSpec(memory_space=SMEM)] + [pl.B...  14.2 us
    ppermute x4, waiting for transfers between devices, shift(): lax.ppermute(a, 'patch', [(i - 2 * pairs, i) for i in devices if i - 2 *...  12.6 us
    ppermute x4, starting transfers between devices, stride(): lax.ppermute(a, 'patch', [(d, s) if back else (s, d) for s, d in route if...  9.61 us
    ppermute x8, waiting for transfers between devices, swap_cores(): return lax.ppermute(a, 'vec', [(0, 1), (1, 0)])  8.77 us
    ppermute x4, starting transfers between devices, shift(): lax.ppermute(a, 'patch', [(i - 2 * pairs, i) for i in devices if i - 2 *...  7.52 us
  transfers between devices with their start and end apart: 66, of which 36 were waited for; matrix products, arithmetic and copies ran while one was open for 2% of the time, Pallas kernels for 6%

profile of v3, /device:TPU:0, one launch (start us, length us, event | category | flops | bytes accessed | tf_op | source)
XLA Modules:
  0.0 244.3 jit_solution(6879908543660283994)
XLA Ops:
  1.9 3.0 %collective-permute-start = (bf16[2,256,256]{2,1,0:T(8,128)(2,1)S(1)}, bf16[2,256,256]{2,1,0:T(8,128)(2,1)S(1)}, u32[]{:S(2)}, u32[]{:S(2)}) collective-permute-start(bf16[2,256,256]{2,1,0:T(8,128)(2,1)S(1)} %get-tuple-element.54.refs_0_), channel_id=1, source_target_pairs={{0,2},{2,0},{4,6},{6,4},{8,10},{10,8},{12,14},{14,12},{16,18},{18,... | collective-permute-start | bytes 786440 | tf_op jit(solution)/shard_map/ppermute | solution.py:380
  4.9 3.5 %collective-permute-start.1 = (bf16[2,256,256]{2,1,0:T(8,128)(2,1)S(1)}, bf16[2,256,256]{2,1,0:T(8,128)(2,1)S(1)}, u32[]{:S(2)}, u32[]{:S(2)}) collective-permute-start(bf16[2,256,256]{2,1,0:T(8,128)(2,1)S(1)} %get-tuple-element.54.refs_0_), channel_id=1, source_target_pairs={{0,8},{2,10},{4,12},{6,14},{8,16},{10,18},{12,20},{14,22},{16,24},... | collective-permute-start | bytes 786440 | tf_op jit(solution)/shard_map/ppermute | solution.py:385
  11.2 3.7 %collective-permute-start.3 = (bf16[2,256,256]{2,1,0:T(8,128)(2,1)S(1)}, bf16[2,256,256]{2,1,0:T(8,128)(2,1)S(1)}, u32[]{:S(2)}, u32[]{:S(2)}) collective-permute-start(bf16[2,256,256]{2,1,0:T(8,128)(2,1)S(1)} %get-tuple-element.54.refs_0_), channel_id=1, source_target_pairs={{0,4},{2,6},{8,12},{10,14},{4,16},{6,18},{16,20},{18,22},{12,24},{... | collective-permute-start | bytes 786440 | tf_op jit(solution)/shard_map/ppermute | solution.py:391
  16.4 2.5 %collective-permute-start.5 = (bf16[2,256,256]{2,1,0:T(8,128)(2,1)S(1)}, bf16[2,256,256]{2,1,0:T(8,128)(2,1)S(1)}, u32[]{:S(2)}, u32[]{:S(2)}) collective-permute-start(bf16[2,256,256]{2,1,0:T(8,128)(2,1)S(1)} %collective-permute-done.1.refs_2_), channel_id=1, source_target_pairs={{0,4},{2,6},{4,0},{6,2},{8,12},{10,14},{12,8},{14,10},{16,20},{18,... | collective-permute-start | bytes 786440 | tf_op jit(solution)/shard_map/ppermute | solution.py:380
  19.0 3.7 %shard_map.69 = (f32[2,256,256]{2,1,0:T(8,128)S(1)}, f32[2,256,256]{2,1,0:T(8,128)S(1)}, f32[2,256,256]{2,1,0:T(8,128)S(1)}, f32[2,256,256]{2,1,0:T(8,128)S(1)},...) custom-call(s32[132]{0:T(256)S(1)} %concatenate.24.meta, ...), custom_call_target="tpu_custom_call" | custom-call | flops 4294967296 | bytes 12582912 | tf_op jit(solution)/shard_map/pallas_call | solution.py:167
  31.9 4.1 %collective-permute-done.15 = bf16[2,256,256]{2,1,0:T(8,128)(2,1)} collective-permute-done((bf16[2,256,256]{2,1,0:T(8,128)(2,1)}, bf16[2,256,256]{2,1,0:T(8,128)(2,1)}, u32[]{:S(2)}, u32[]{:S(2)}) %collective-permute-start.15) | collective-permute-done | bytes 262176 | tf_op jit(solution)/shard_map/ppermute | solution.py:380
  44.1 2.2 collective-permute-done.6.refs_7_
  46.4 3.7 %shard_map.70 = (f32[2,256,256]{2,1,0:T(8,128)S(1)}, bf16[2,256,256]{2,1,0:T(8,128)(2,1)S(1)}, f32[448,256]{1,0:T(8,128)S(1)}) custom-call(s32[132]{0:T(256)S(1)} %concatenate.24.meta, bf16[2,256,256]{2,1,0:T(8,128)(2,1)S(1)} %get-tuple-element.54.refs_0_, bf16[2,256,256]{2,1,0:T(8,128)(2,1)S(1)} %collective-permute-done.refs_1_, ...), custom_call_target="tpu_custom_call" | custom-call | flops 4294967296 | bytes 12582912 | tf_op jit(solution)/shard_map/pallas_call | solution.py:167
  51.6 2.9 %collective-permute-start.9 = (f32[192,256]{1,0:T(8,128)}, f32[192,256]{1,0:T(8,128)}, u32[]{:S(2)}, u32[]{:S(2)}) collective-permute-start(f32[192,256]{1,0:T(8,128)} %get-tuple-element.110), channel_id=1, source_target_pairs={{0,2},{2,0},{4,6},{6,4},{8,10},{10,8},{12,14},{14,12},{16,18},{18,... | collective-permute-start | bytes 589832 | tf_op jit(solution)/shard_map/ppermute | solution.py:380
  54.7 6.0 %collective-permute-done.10 = f32[192,256]{1,0:T(8,128)} collective-permute-done((f32[192,256]{1,0:T(8,128)S(1)}, f32[192,256]{1,0:T(8,128)}, u32[]{:S(2)}, u32[]{:S(2)}) %collective-permute-start.10) | collective-permute-done | bytes 196640 | tf_op jit(solution)/shard_map/ppermute | solution.py:380
  65.7 8.4 %collective-permute-done.18.two = bf16[2,256,256]{2,1,0:T(8,128)(2,1)S(1)} collective-permute-done((bf16[2,256,256]{2,1,0:T(8,128)(2,1)S(1)}, bf16[2,256,256]{2,1,0:T(8,128)(2,1)S(1)}, u32[]{:S(2)}, u32[]{:S(2)}) %collective-permute-start.18) | collective-permute-done | bytes 262176 | tf_op jit(solution)/shard_map/ppermute | solution.py:385
  76.9 2.6 %collective-permute-start.20 = (f32[48,256]{1,0:T(8,128)S(1)}, f32[48,256]{1,0:T(8,128)S(1)}, u32[]{:S(2)}, u32[]{:S(2)}) collective-permute-start(f32[48,256]{1,0:T(8,128)S(1)} %get-tuple-element.126), channel_id=1, source_target_pairs={{0,8},{2,10},{4,12},{6,14},{8,0},{10,2},{12,4},{14,6},{16,24},{18,... | collective-permute-start | bytes 147464 | tf_op jit(solution)/shard_map/ppermute | solution.py:380
  79.5 2.4 collective-permute-start.22
  81.9 2.4 collective-permute-start.23
  84.3 3.0 %collective-permute-start.24 = (f32[80,256]{1,0:T(8,128)S(1)}, f32[80,256]{1,0:T(8,128)S(1)}, u32[]{:S(2)}, u32[]{:S(2)}) collective-permute-start(f32[80,256]{1,0:T(8,128)S(1)} %get-tuple-element.125), channel_id=1, source_target_pairs={{0,4},{2,6},{4,0},{6,2},{8,12},{10,14},{12,8},{14,10},{16,20},{18,... | collective-permute-start | bytes 245768 | tf_op jit(solution)/shard_map/ppermute | solution.py:380
  87.3 3.2 %collective-permute-done.24 = f32[80,256]{1,0:T(8,128)S(1)} collective-permute-done((f32[80,256]{1,0:T(8,128)S(1)}, f32[80,256]{1,0:T(8,128)S(1)}, u32[]{:S(2)}, u32[]{:S(2)}) %collective-permute-start.24) | collective-permute-done | bytes 81952 | tf_op jit(solution)/shard_map/ppermute | solution.py:380
  95.0 2.1 collective-permute-start.28
  97.1 3.5 %collective-permute-done.26 = f32[128,256]{1,0:T(8,128)S(1)} collective-permute-done((f32[128,256]{1,0:T(8,128)S(1)}, f32[128,256]{1,0:T(8,128)S(1)}, u32[]{:S(2)}, u32[]{:S(2)}) %collective-permute-start.26) | collective-permute-done | bytes 131104 | tf_op jit(solution)/shard_map/ppermute | solution.py:380
  100.6 4.1 %collective-permute-done.27 = f32[128,256]{1,0:T(8,128)S(1)} collective-permute-done((f32[128,256]{1,0:T(8,128)S(1)}, f32[128,256]{1,0:T(8,128)S(1)}, u32[]{:S(2)}, u32[]{:S(2)}) %collective-permute-start.27) | collective-permute-done | bytes 131104 | tf_op jit(solution)/shard_map/ppermute | solution.py:380
  108.4 7.0 %collective-permute-done.29 = f32[272,256]{1,0:T(8,128)S(1)} collective-permute-done((f32[272,256]{1,0:T(8,128)S(1)}, f32[272,256]{1,0:T(8,128)S(1)}, u32[]{:S(2)}, u32[]{:S(2)}) %collective-permute-start.29) | collective-permute-done | bytes 278560 | tf_op jit(solution)/shard_map/ppermute | solution.py:380
  115.4 2.6 %collective-permute-done.30 = f32[272,256]{1,0:T(8,128)S(1)} collective-permute-done((f32[272,256]{1,0:T(8,128)S(1)}, f32[272,256]{1,0:T(8,128)S(1)}, u32[]{:S(2)}, u32[]{:S(2)}) %collective-permute-start.30) | collective-permute-done | bytes 278560 | tf_op jit(solution)/shard_map/ppermute | solution.py:380
  118.3 2.7 %collective-permute-done.32.refs_6_ = f32[4,272,256]{2,1,0:T(8,128)S(1)} collective-permute-done((f32[4,272,256]{2,1,0:T(8,128)S(1)}, f32[4,272,256]{2,1,0:T(8,128)S(1)}, u32[]{:S(2)}, u32[]{:S(2)}) %collective-permute-start.32) | collective-permute-done | bytes 1114144 | tf_op jit(solution)/shard_map/ppermute | solution.py:376
  121.0 13.2 %shard_map.74 = (f32[256,512]{1,0:T(8,128)S(1)}, bf16[2,256,256]{2,1,0:T(8,128)(2,1)S(1)}) custom-call(s32[1]{0:T(128)} %bitcast.core.refs_0_, f32[256,512]{1,0:T(8,128)S(1)} %shard_map.72.mine.refs_1_, f32[256,512]{1,0:T(8,128)S(1)} %collective-permute-done.19.theirs.refs_2_, f32[256,512]{1,0:T(8,128)S(1)} %get-tuple-element.52.mine.x.refs_3_, ...), custom_call_target="tpu_custom_call" | custom-call | flops 17179869184 | bytes 5111812 | tf_op jit(solution)/shard_map/pallas_call | solution.py:40
  136.8 5.8 %collective-permute-done.33.refs_1_ = bf16[2,256,256]{2,1,0:T(8,128)(2,1)S(1)} collective-permute-done((bf16[2,256,256]{2,1,0:T(8,128)(2,1)S(1)}, bf16[2,256,256]{2,1,0:T(8,128)(2,1)S(1)}, u32[]{:S(2)}, u32[]{:S(2)}) %collective-permute-start.33) | collective-permute-done | bytes 262176 | tf_op jit(solution)/shard_map/ppermute | solution.py:380
  142.6 3.1 %collective-permute-start.36 = (bf16[2,256,256]{2,1,0:T(8,128)(2,1)S(1)}, bf16[2,256,256]{2,1,0:T(8,128)(2,1)S(1)}, u32[]{:S(2)}, u32[]{:S(2)}) collective-permute-start(bf16[2,256,256]{2,1,0:T(8,128)(2,1)S(1)} %get-tuple-element.79.refs_0_), channel_id=1, source_target_pairs={{0,4},{2,6},{8,12},{10,14},{4,16},{6,18},{16,20},{18,22},{12,24},{... | collective-permute-start | bytes 786440 | tf_op jit(solution)/shard_map/ppermute | solution.py:391
  147.1 3.1 %shard_map.75 = (f32[2,256,256]{2,1,0:T(8,128)S(1)}, f32[2,256,256]{2,1,0:T(8,128)S(1)}, f32[2,256,256]{2,1,0:T(8,128)S(1)}, f32[2,256,256]{2,1,0:T(8,128)S(1)},...) custom-call(s32[132]{0:T(256)S(1)} %concatenate.24.meta, ...), custom_call_target="tpu_custom_call" | custom-call | flops 4294967296 | bytes 12582912 | tf_op jit(solution)/shard_map/pallas_call | solution.py:167
  150.2 2.3 collective-permute-done.36.refs_4_
  153.1 3.3 %collective-permute-done.38.refs_6_ = bf16[2,256,256]{2,1,0:T(8,128)(2,1)S(1)} collective-permute-done((bf16[2,256,256]{2,1,0:T(8,128)(2,1)S(1)}, bf16[2,256,256]{2,1,0:T(8,128)(2,1)S(1)}, u32[]{:S(2)}, u32[]{:S(2)}) %collective-permute-start.38) | collective-permute-done | bytes 262176 | tf_op jit(solution)/shard_map/ppermute | solution.py:380
  156.4 2.5 %collective-permute-start.48 = (bf16[2,256,256]{2,1,0:T(8,128)(2,1)S(1)}, bf16[2,256,256]{2,1,0:T(8,128)(2,1)S(1)}, u32[]{:S(2)}, u32[]{:S(2)}) collective-permute-start(bf16[2,256,256]{2,1,0:T(8,128)(2,1)S(1)} %get-tuple-element.92), channel_id=1, source_target_pairs={{0,4},{2,6},{4,0},{6,2},{8,12},{10,14},{12,8},{14,10},{16,20},{18,... | collective-permute-start | bytes 786440 | tf_op jit(solution)/shard_map/ppermute | solution.py:380
  161.1 2.6 %collective-permute-done.48 = bf16[2,256,256]{2,1,0:T(8,128)(2,1)S(1)} collective-permute-done((bf16[2,256,256]{2,1,0:T(8,128)(2,1)S(1)}, bf16[2,256,256]{2,1,0:T(8,128)(2,1)S(1)}, u32[]{:S(2)}, u32[]{:S(2)}) %collective-permute-start.48) | collective-permute-done | bytes 262176 | tf_op jit(solution)/shard_map/ppermute | solution.py:380
  165.5 2.4 %collective-permute-done.46 = bf16[2,256,256]{2,1,0:T(8,128)(2,1)S(1)} collective-permute-done((bf16[2,256,256]{2,1,0:T(8,128)(2,1)S(1)}, bf16[2,256,256]{2,1,0:T(8,128)(2,1)S(1)}, u32[]{:S(2)}, u32[]{:S(2)}) %collective-permute-start.46) | collective-permute-done | bytes 262176 | tf_op jit(solution)/shard_map/ppermute | solution.py:380
  170.5 3.1 %collective-permute-done.37.refs_5_ = bf16[2,256,256]{2,1,0:T(8,128)(2,1)S(1)} collective-permute-done((bf16[2,256,256]{2,1,0:T(8,128)(2,1)S(1)}, bf16[2,256,256]{2,1,0:T(8,128)(2,1)S(1)}, u32[]{:S(2)}, u32[]{:S(2)}) %collective-permute-start.37) | collective-permute-done | bytes 262176 | tf_op jit(solution)/shard_map/ppermute | solution.py:380
  173.6 3.7 %shard_map.76 = (f32[2,256,256]{2,1,0:T(8,128)S(1)}, bf16[2,256,256]{2,1,0:T(8,128)(2,1)S(1)}, f32[448,256]{1,0:T(8,128)S(1)}) custom-call(s32[132]{0:T(256)S(1)} %concatenate.24.meta, bf16[2,256,256]{2,1,0:T(8,128)(2,1)S(1)} %get-tuple-element.79.refs_0_, bf16[2,256,256]{2,1,0:T(8,128)(2,1)S(1)} %collective-permute-done.33.refs_1_, ...), custom_call_target="tpu_custom_call" | custom-call | flops 4294967296 | bytes 12582912 | tf_op jit(solution)/shard_map/pallas_call | solution.py:167
  178.2 2.7 %collective-permute-start.44 = (f32[112,256]{1,0:T(8,128)S(1)}, f32[112,256]{1,0:T(8,128)S(1)}, u32[]{:S(2)}, u32[]{:S(2)}) collective-permute-start(f32[112,256]{1,0:T(8,128)S(1)} %get-tuple-element.114), channel_id=1, source_target_pairs={{0,6},{2,4},{4,2},{6,0},{8,14},{10,12},{12,10},{14,8},{16,22},{18,... | collective-permute-start | bytes 344072 | tf_op jit(solution)/shard_map/ppermute | solution.py:380
  181.1 2.3 collective-permute-done.42
  184.6 3.8 %collective-permute-done.43 = f32[112,256]{1,0:T(8,128)S(1)} collective-permute-done((f32[112,256]{1,0:T(8,128)S(1)}, f32[112,256]{1,0:T(8,128)S(1)}, u32[]{:S(2)}, u32[]{:S(2)}) %collective-permute-start.43) | collective-permute-done | bytes 114720 | tf_op jit(solution)/shard_map/ppermute | solution.py:380
  189.9 4.2 %collective-permute-done.51.two = bf16[2,256,256]{2,1,0:T(8,128)(2,1)S(1)} collective-permute-done((bf16[2,256,256]{2,1,0:T(8,128)(2,1)S(1)}, bf16[2,256,256]{2,1,0:T(8,128)(2,1)S(1)}, u32[]{:S(2)}, u32[]{:S(2)}) %collective-permute-start.51) | collective-permute-done | bytes 262176 | tf_op jit(solution)/shard_map/ppermute | solution.py:385
  196.9 2.1 collective-permute-start.53
  199.1 2.4 collective-permute-start.55
  202.5 2.6 %collective-permute-start.58 = (f32[80,256]{1,0:T(8,128)S(1)}, f32[80,256]{1,0:T(8,128)S(1)}, u32[]{:S(2)}, u32[]{:S(2)}) collective-permute-start(f32[80,256]{1,0:T(8,128)S(1)} %get-tuple-element.121), channel_id=1, source_target_pairs={{0,6},{2,4},{4,2},{6,0},{8,14},{10,12},{12,10},{14,8},{16,22},{18,... | collective-permute-start | bytes 245768 | tf_op jit(solution)/shard_map/ppermute | solution.py:380
  208.1 2.7 %collective-permute-start.59 = (f32[108,256]{1,0:T(8,128)S(1)}, f32[108,256]{1,0:T(8,128)S(1)}, u32[]{:S(2)}, u32[]{:S(2)}) collective-permute-start(f32[108,256]{1,0:T(8,128)S(1)} %pad_maximum_fusion.3), channel_id=1, source_target_pairs={{0,24},{2,26},{4,28},{6,30},{8,16},{10,18},{12,20},{14,22},{16,8},... | collective-permute-start | bytes 331784 | tf_op jit(solution)/shard_map/ppermute | solution.py:380
  212.6 3.3 %collective-permute-done.59 = f32[108,256]{1,0:T(8,128)S(1)} collective-permute-done((f32[108,256]{1,0:T(8,128)S(1)}, f32[108,256]{1,0:T(8,128)S(1)}, u32[]{:S(2)}, u32[]{:S(2)}) %collective-permute-start.59) | collective-permute-done | bytes 110624 | tf_op jit(solution)/shard_map/ppermute | solution.py:380
  215.9 3.4 %collective-permute-done.60 = f32[108,256]{1,0:T(8,128)S(1)} collective-permute-done((f32[108,256]{1,0:T(8,128)S(1)}, f32[108,256]{1,0:T(8,128)S(1)}, u32[]{:S(2)}, u32[]{:S(2)}) %collective-permute-start.60) | collective-permute-done | bytes 110624 | tf_op jit(solution)/shard_map/ppermute | solution.py:380
  219.6 2.4 collective-permute-start.62
  223.2 5.2 %collective-permute-done.62 = f32[192,256]{1,0:T(8,128)S(1)} collective-permute-done((f32[192,256]{1,0:T(8,128)S(1)}, f32[192,256]{1,0:T(8,128)S(1)}, u32[]{:S(2)}, u32[]{:S(2)}) %collective-permute-start.62) | collective-permute-done | bytes 196640 | tf_op jit(solution)/shard_map/ppermute | solution.py:380
  228.4 2.1 collective-permute-done.63
  230.9 2.3 collective-permute-done.65.refs_6_
  233.2 11.2 %shard_map.79 = (f32[512,256]{1,0:T(8,128)}, f32[512,256]{1,0:T(8,128)}) custom-call(s32[1]{0:T(128)} %bitcast.core.refs_0_, f32[256,512]{1,0:T(8,128)S(1)} %shard_map.77.mine.refs_1_, f32[256,512]{1,0:T(8,128)S(1)} %collective-permute-done.52.theirs.refs_2_, f32[256,512]{1,0:T(8,128)S(1)} %get-tuple-element.77.x.refs_3_, ...), custom_call_target="tpu_custom_call" | custom-call | flops 17179869184 | bytes 4718596 | tf_op jit(solution)/shard_map/pallas_call | solution.py:40
  (162 shorter events, 65.3 us)
Async XLA Ops:
  1.9 9.3 %collective-permute-start = (bf16[2,256,256]{2,1,0:T(8,128)(2,1)S(1)}, bf16[2,256,256]{2,1,0:T(8,128)(2,1)S(1)}, u32[]{:S(2)}, u32[]{:S(2)}) collective-permute-start(bf16[2,256,256]{2,1,0:T(8,128)(2,1)S(1)} %get-tuple-element.54.refs_0_), channel_id=1, source_target_pairs={{0,2},{2,0},{4,6},{6,4},{8,10},{10,8},{12,14},{14,12},{16,18},{18,... | collective-permute-start | bytes 786440 | tf_op jit(solution)/shard_map/ppermute | solution.py:380
  4.9 10.0 %collective-permute-start.1 = (bf16[2,256,256]{2,1,0:T(8,128)(2,1)S(1)}, bf16[2,256,256]{2,1,0:T(8,128)(2,1)S(1)}, u32[]{:S(2)}, u32[]{:S(2)}) collective-permute-start(bf16[2,256,256]{2,1,0:T(8,128)(2,1)S(1)} %get-tuple-element.54.refs_0_), channel_id=1, source_target_pairs={{0,8},{2,10},{4,12},{6,14},{8,16},{10,18},{12,20},{14,22},{16,24},... | collective-permute-start | bytes 786440 | tf_op jit(solution)/shard_map/ppermute | solution.py:385
  8.4 21.6 %collective-permute-start.7 = (f32[256,512]{1,0:T(8,128)S(1)}, f32[256,512]{1,0:T(8,128)S(1)}, u32[]{:S(2)}, u32[]{:S(2)}) collective-permute-start(f32[256,512]{1,0:T(8,128)S(1)} %get-tuple-element.52.mine.x.refs_3_), channel_id=1, source_target_pairs={{0,1},{1,0},{2,3},{3,2},{4,5},{5,4},{6,7},{7,6},{8,9},{9,8},{10,11... | collective-permute-start | bytes 1572872 | tf_op jit(solution)/shard_map/ppermute | solution.py:376
  11.2 14.5 %collective-permute-start.3 = (bf16[2,256,256]{2,1,0:T(8,128)(2,1)S(1)}, bf16[2,256,256]{2,1,0:T(8,128)(2,1)S(1)}, u32[]{:S(2)}, u32[]{:S(2)}) collective-permute-start(bf16[2,256,256]{2,1,0:T(8,128)(2,1)S(1)} %get-tuple-element.54.refs_0_), channel_id=1, source_target_pairs={{0,4},{2,6},{8,12},{10,14},{4,16},{6,18},{16,20},{18,22},{12,24},{... | collective-permute-start | bytes 786440 | tf_op jit(solution)/shard_map/ppermute | solution.py:391
  14.9 10.8 %collective-permute-start.2 = (bf16[2,256,256]{2,1,0:T(8,128)(2,1)S(1)}, bf16[2,256,256]{2,1,0:T(8,128)(2,1)S(1)}, u32[]{:S(2)}, u32[]{:S(2)}) collective-permute-start(bf16[2,256,256]{2,1,0:T(8,128)(2,1)S(1)} %collective-permute-done.1.refs_2_), channel_id=1, source_target_pairs={{0,2},{2,0},{4,6},{6,4},{8,10},{10,8},{12,14},{14,12},{16,18},{18,... | collective-permute-start | bytes 786440 | tf_op jit(solution)/shard_map/ppermute | solution.py:380
  16.4 9.3 %collective-permute-start.5 = (bf16[2,256,256]{2,1,0:T(8,128)(2,1)S(1)}, bf16[2,256,256]{2,1,0:T(8,128)(2,1)S(1)}, u32[]{:S(2)}, u32[]{:S(2)}) collective-permute-start(bf16[2,256,256]{2,1,0:T(8,128)(2,1)S(1)} %collective-permute-done.1.refs_2_), channel_id=1, source_target_pairs={{0,4},{2,6},{4,0},{6,2},{8,12},{10,14},{12,8},{14,10},{16,20},{18,... | collective-permute-start | bytes 786440 | tf_op jit(solution)/shard_map/ppermute | solution.py:380
  27.1 8.8 %collective-permute-start.15 = (bf16[2,256,256]{2,1,0:T(8,128)(2,1)}, bf16[2,256,256]{2,1,0:T(8,128)(2,1)}, u32[]{:S(2)}, u32[]{:S(2)}) collective-permute-start(bf16[2,256,256]{2,1,0:T(8,128)(2,1)} %get-tuple-element.67), channel_id=1, source_target_pairs={{0,4},{2,6},{4,0},{6,2},{8,12},{10,14},{12,8},{14,10},{16,20},{18,... | collective-permute-start | bytes 786440 | tf_op jit(solution)/shard_map/ppermute | solution.py:380
  28.3 12.9 %collective-permute-start.8 = (bf16[2,256,256]{2,1,0:T(8,128)(2,1)S(1)}, bf16[2,256,256]{2,1,0:T(8,128)(2,1)S(1)}, u32[]{:S(2)}, u32[]{:S(2)}) collective-permute-start(bf16[2,256,256]{2,1,0:T(8,128)(2,1)S(1)} %collective-permute-done.refs_1_), channel_id=1, source_target_pairs={{0,1},{1,0},{2,3},{3,2},{4,5},{5,4},{6,7},{7,6},{8,9},{9,8},{10,11... | collective-permute-start | bytes 786440 | tf_op jit(solution)/shard_map/ppermute | solution.py:376
  28.4 23.3 %collective-permute-start.17 = (bf16[2,256,256]{2,1,0:T(8,128)(2,1)}, bf16[2,256,256]{2,1,0:T(8,128)(2,1)S(1)}, u32[]{:S(2)}, u32[]{:S(2)}) collective-permute-start(bf16[2,256,256]{2,1,0:T(8,128)(2,1)} %copy-done.1), channel_id=1, source_target_pairs={{0,4},{2,6},{4,0},{6,2},{8,12},{10,14},{12,8},{14,10},{16,20},{18,... | collective-permute-start | bytes 786440 | tf_op jit(solution)/shard_map/ppermute | solution.py:380
  29.2 9.4 %collective-permute-start.13 = (bf16[2,256,256]{2,1,0:T(8,128)(2,1)}, bf16[2,256,256]{2,1,0:T(8,128)(2,1)S(1)}, u32[]{:S(2)}, u32[]{:S(2)}) collective-permute-start(bf16[2,256,256]{2,1,0:T(8,128)(2,1)} %copy-done.8), channel_id=1, source_target_pairs={{0,2},{2,0},{4,6},{6,4},{8,10},{10,8},{12,14},{14,12},{16,18},{18,... | collective-permute-start | bytes 786440 | tf_op jit(solution)/shard_map/ppermute | solution.py:380
  30.0 14.1 %collective-permute-start.4 = (bf16[2,256,256]{2,1,0:T(8,128)(2,1)}, bf16[2,256,256]{2,1,0:T(8,128)(2,1)S(1)}, u32[]{:S(2)}, u32[]{:S(2)}) collective-permute-start(bf16[2,256,256]{2,1,0:T(8,128)(2,1)} %copy-done.2), channel_id=1, source_target_pairs={{0,2},{2,0},{4,6},{6,4},{8,10},{10,8},{12,14},{14,12},{16,18},{18,... | collective-permute-start | bytes 786440 | tf_op jit(solution)/shard_map/ppermute | solution.py:380
  35.9 10.4 %collective-permute-start.6 = (bf16[2,256,256]{2,1,0:T(8,128)(2,1)S(1)}, bf16[2,256,256]{2,1,0:T(8,128)(2,1)S(1)}, u32[]{:S(2)}, u32[]{:S(2)}) collective-permute-start(bf16[2,256,256]{2,1,0:T(8,128)(2,1)S(1)} %copy-done.5), channel_id=1, source_target_pairs={{0,4},{2,6},{4,0},{6,2},{8,12},{10,14},{12,8},{14,10},{16,20},{18,... | collective-permute-start | bytes 786440 | tf_op jit(solution)/shard_map/ppermute | solution.py:380
  38.6 15.9 %collective-permute-start.16 = (bf16[2,256,256]{2,1,0:T(8,128)(2,1)S(1)}, bf16[2,256,256]{2,1,0:T(8,128)(2,1)S(1)}, u32[]{:S(2)}, u32[]{:S(2)}) collective-permute-start(bf16[2,256,256]{2,1,0:T(8,128)(2,1)S(1)} %add_convert_fusion.4), channel_id=1, source_target_pairs={{0,2},{2,0},{4,6},{6,4},{8,10},{10,8},{12,14},{14,12},{16,18},{18,... | collective-permute-start | bytes 786440 | tf_op jit(solution)/shard_map/ppermute | solution.py:380
  41.3 23.6 %collective-permute-start.14 = (bf16[2,256,256]{2,1,0:T(8,128)(2,1)}, bf16[2,256,256]{2,1,0:T(8,128)(2,1)S(1)}, u32[]{:S(2)}, u32[]{:S(2)}) collective-permute-start(bf16[2,256,256]{2,1,0:T(8,128)(2,1)} %add_convert_fusion.5), channel_id=1, source_target_pairs={{4,0},{6,2},{12,8},{14,10},{16,4},{18,6},{20,16},{22,18},{24,12},{... | collective-permute-start | bytes 786440 | tf_op jit(solution)/shard_map/ppermute | solution.py:391
  51.0 9.6 %collective-permute-start.10 = (f32[192,256]{1,0:T(8,128)S(1)}, f32[192,256]{1,0:T(8,128)}, u32[]{:S(2)}, u32[]{:S(2)}) collective-permute-start(f32[192,256]{1,0:T(8,128)S(1)} %get-tuple-element.112), channel_id=1, source_target_pairs={{0,4},{2,6},{4,0},{6,2},{8,12},{10,14},{12,8},{14,10},{16,20},{18,... | collective-permute-start | bytes 589832 | tf_op jit(solution)/shard_map/ppermute | solution.py:380
  51.0 11.1 %collective-permute-start.11 = (f32[192,256]{1,0:T(8,128)}, f32[192,256]{1,0:T(8,128)}, u32[]{:S(2)}, u32[]{:S(2)}) collective-permute-start(f32[192,256]{1,0:T(8,128)} %get-tuple-element.111), channel_id=1, source_target_pairs={{0,6},{2,4},{4,2},{6,0},{8,14},{10,12},{12,10},{14,8},{16,22},{18,... | collective-permute-start | bytes 589832 | tf_op jit(solution)/shard_map/ppermute | solution.py:380
  51.6 11.3 %collective-permute-start.9 = (f32[192,256]{1,0:T(8,128)}, f32[192,256]{1,0:T(8,128)}, u32[]{:S(2)}, u32[]{:S(2)}) collective-permute-start(f32[192,256]{1,0:T(8,128)} %get-tuple-element.110), channel_id=1, source_target_pairs={{0,2},{2,0},{4,6},{6,4},{8,10},{10,8},{12,14},{14,12},{16,18},{18,... | collective-permute-start | bytes 589832 | tf_op jit(solution)/shard_map/ppermute | solution.py:380
  54.5 11.2 %collective-permute-start.12 = (bf16[2,256,256]{2,1,0:T(8,128)(2,1)S(1)}, bf16[2,256,256]{2,1,0:T(8,128)(2,1)S(1)}, u32[]{:S(2)}, u32[]{:S(2)}) collective-permute-start(bf16[2,256,256]{2,1,0:T(8,128)(2,1)S(1)} %get-tuple-element.59), channel_id=1, source_target_pairs={{0,2},{2,0},{4,6},{6,4},{8,10},{10,8},{12,14},{14,12},{16,18},{18,... | collective-permute-start | bytes 786440 | tf_op jit(solution)/shard_map/ppermute | solution.py:380
  60.6 13.4 %collective-permute-start.18 = (bf16[2,256,256]{2,1,0:T(8,128)(2,1)S(1)}, bf16[2,256,256]{2,1,0:T(8,128)(2,1)S(1)}, u32[]{:S(2)}, u32[]{:S(2)}) collective-permute-start(bf16[2,256,256]{2,1,0:T(8,128)(2,1)S(1)} %add_convert_fusion.3), channel_id=1, source_target_pairs={{8,0},{10,2},{12,4},{14,6},{16,8},{18,10},{20,12},{22,14},{24,16},... | collective-permute-start | bytes 786440 | tf_op jit(solution)/shard_map/ppermute | solution.py:385
  76.9 10.4 %collective-permute-start.20 = (f32[48,256]{1,0:T(8,128)S(1)}, f32[48,256]{1,0:T(8,128)S(1)}, u32[]{:S(2)}, u32[]{:S(2)}) collective-permute-start(f32[48,256]{1,0:T(8,128)S(1)} %get-tuple-element.126), channel_id=1, source_target_pairs={{0,8},{2,10},{4,12},{6,14},{8,0},{10,2},{12,4},{14,6},{16,24},{18,... | collective-permute-start | bytes 147464 | tf_op jit(solution)/shard_map/ppermute | solution.py:380
  79.4 7.8 %collective-permute-start.21 = (f32[48,256]{1,0:T(8,128)S(1)}, f32[48,256]{1,0:T(8,128)S(1)}, u32[]{:S(2)}, u32[]{:S(2)}) collective-permute-start(f32[48,256]{1,0:T(8,128)S(1)} %get-tuple-element.128), channel_id=1, source_target_pairs={{0,16},{2,18},{4,20},{6,22},{8,24},{10,26},{12,28},{14,30},{16,0},... | collective-permute-start | bytes 147464 | tf_op jit(solution)/shard_map/ppermute | solution.py:380
  92.6 7.9 %collective-permute-start.26 = (f32[128,256]{1,0:T(8,128)S(1)}, f32[128,256]{1,0:T(8,128)S(1)}, u32[]{:S(2)}, u32[]{:S(2)}) collective-permute-start(f32[128,256]{1,0:T(8,128)S(1)} %constant_dynamic-update-slice_fusion), channel_id=1, source_target_pairs={{0,24},{2,26},{4,28},{6,30},{8,16},{10,18},{12,20},{14,22},{16,8},... | collective-permute-start | bytes 393224 | tf_op jit(solution)/shard_map/ppermute | solution.py:380
  93.9 10.8 %collective-permute-start.27 = (f32[128,256]{1,0:T(8,128)S(1)}, f32[128,256]{1,0:T(8,128)S(1)}, u32[]{:S(2)}, u32[]{:S(2)}) collective-permute-start(f32[128,256]{1,0:T(8,128)S(1)} %constant_dynamic-update-slice_fusion), channel_id=1, source_target_pairs={{0,16},{2,18},{4,20},{6,22},{8,24},{10,26},{12,28},{14,30},{16,0},... | collective-permute-start | bytes 393224 | tf_op jit(solution)/shard_map/ppermute | solution.py:380
  95.0 9.7 %collective-permute-start.28 = (f32[128,256]{1,0:T(8,128)S(1)}, f32[128,256]{1,0:T(8,128)S(1)}, u32[]{:S(2)}, u32[]{:S(2)}) collective-permute-start(f32[128,256]{1,0:T(8,128)S(1)} %constant_dynamic-update-slice_fusion), channel_id=1, source_target_pairs={{0,8},{2,10},{4,12},{6,14},{8,0},{10,2},{12,4},{14,6},{16,24},{18,... | collective-permute-start | bytes 393224 | tf_op jit(solution)/shard_map/ppermute | solution.py:380
  104.8 10.6 %collective-permute-start.29 = (f32[272,256]{1,0:T(8,128)S(1)}, f32[272,256]{1,0:T(8,128)S(1)}, u32[]{:S(2)}, u32[]{:S(2)}) collective-permute-start(f32[272,256]{1,0:T(8,128)S(1)} %fusion.4), channel_id=1, source_target_pairs={{0,6},{2,4},{4,2},{6,0},{8,14},{10,12},{12,10},{14,8},{16,22},{18,... | collective-permute-start | bytes 835592 | tf_op jit(solution)/shard_map/ppermute | solution.py:380
  105.3 12.6 %collective-permute-start.30 = (f32[272,256]{1,0:T(8,128)S(1)}, f32[272,256]{1,0:T(8,128)S(1)}, u32[]{:S(2)}, u32[]{:S(2)}) collective-permute-start(f32[272,256]{1,0:T(8,128)S(1)} %fusion.4), channel_id=1, source_target_pairs={{0,4},{2,6},{4,0},{6,2},{8,12},{10,14},{12,8},{14,10},{16,20},{18,... | collective-permute-start | bytes 835592 | tf_op jit(solution)/shard_map/ppermute | solution.py:380
  107.1 10.9 %collective-permute-start.31 = (f32[272,256]{1,0:T(8,128)S(1)}, f32[272,256]{1,0:T(8,128)S(1)}, u32[]{:S(2)}, u32[]{:S(2)}) collective-permute-start(f32[272,256]{1,0:T(8,128)S(1)} %fusion.4), channel_id=1, source_target_pairs={{0,2},{2,0},{4,6},{6,4},{8,10},{10,8},{12,14},{14,12},{16,18},{18,... | collective-permute-start | bytes 835592 | tf_op jit(solution)/shard_map/ppermute | solution.py:380
  134.2 8.4 %collective-permute-start.33 = (bf16[2,256,256]{2,1,0:T(8,128)(2,1)S(1)}, bf16[2,256,256]{2,1,0:T(8,128)(2,1)S(1)}, u32[]{:S(2)}, u32[]{:S(2)}) collective-permute-start(bf16[2,256,256]{2,1,0:T(8,128)(2,1)S(1)} %get-tuple-element.79.refs_0_), channel_id=1, source_target_pairs={{0,2},{2,0},{4,6},{6,4},{8,10},{10,8},{12,14},{14,12},{16,18},{18,... | collective-permute-start | bytes 786440 | tf_op jit(solution)/shard_map/ppermute | solution.py:380
  135.5 10.3 %collective-permute-start.34 = (bf16[2,256,256]{2,1,0:T(8,128)(2,1)S(1)}, bf16[2,256,256]{2,1,0:T(8,128)(2,1)S(1)}, u32[]{:S(2)}, u32[]{:S(2)}) collective-permute-start(bf16[2,256,256]{2,1,0:T(8,128)(2,1)S(1)} %get-tuple-element.79.refs_0_), channel_id=1, source_target_pairs={{0,8},{2,10},{4,12},{6,14},{8,16},{10,18},{12,20},{14,22},{16,24},... | collective-permute-start | bytes 786440 | tf_op jit(solution)/shard_map/ppermute | solution.py:385
  142.6 9.9 %collective-permute-start.36 = (bf16[2,256,256]{2,1,0:T(8,128)(2,1)S(1)}, bf16[2,256,256]{2,1,0:T(8,128)(2,1)S(1)}, u32[]{:S(2)}, u32[]{:S(2)}) collective-permute-start(bf16[2,256,256]{2,1,0:T(8,128)(2,1)S(1)} %get-tuple-element.79.refs_0_), channel_id=1, source_target_pairs={{0,4},{2,6},{8,12},{10,14},{4,16},{6,18},{16,20},{18,22},{12,24},{... | collective-permute-start | bytes 786440 | tf_op jit(solution)/shard_map/ppermute | solution.py:391
  146.7 9.7 %collective-permute-start.38 = (bf16[2,256,256]{2,1,0:T(8,128)(2,1)S(1)}, bf16[2,256,256]{2,1,0:T(8,128)(2,1)S(1)}, u32[]{:S(2)}, u32[]{:S(2)}) collective-permute-start(bf16[2,256,256]{2,1,0:T(8,128)(2,1)S(1)} %collective-permute-done.34.refs_2_), channel_id=1, source_target_pairs={{0,4},{2,6},{4,0},{6,2},{8,12},{10,14},{12,8},{14,10},{16,20},{18,... | collective-permute-start | bytes 786440 | tf_op jit(solution)/shard_map/ppermute | solution.py:380
  158.9 9.2 %collective-permute-start.40 = (f32[256,512]{1,0:T(8,128)S(1)}, f32[256,512]{1,0:T(8,128)S(1)}, u32[]{:S(2)}, u32[]{:S(2)}) collective-permute-start(f32[256,512]{1,0:T(8,128)S(1)} %get-tuple-element.77.x.refs_3_), channel_id=1, source_target_pairs={{0,1},{1,0},{2,3},{3,2},{4,5},{5,4},{6,7},{7,6},{8,9},{9,8},{10,11... | collective-permute-start | bytes 1572872 | tf_op jit(solution)/shard_map/ppermute | solution.py:376
  158.9 9.1 %collective-permute-start.46 = (bf16[2,256,256]{2,1,0:T(8,128)(2,1)S(1)}, bf16[2,256,256]{2,1,0:T(8,128)(2,1)S(1)}, u32[]{:S(2)}, u32[]{:S(2)}) collective-permute-start(bf16[2,256,256]{2,1,0:T(8,128)(2,1)S(1)} %get-tuple-element.89), channel_id=1, source_target_pairs={{0,2},{2,0},{4,6},{6,4},{8,10},{10,8},{12,14},{14,12},{16,18},{18,... | collective-permute-start | bytes 786440 | tf_op jit(solution)/shard_map/ppermute | solution.py:380
  159.7 9.2 %collective-permute-start.41 = (bf16[2,256,256]{2,1,0:T(8,128)(2,1)S(1)}, bf16[2,256,256]{2,1,0:T(8,128)(2,1)S(1)}, u32[]{:S(2)}, u32[]{:S(2)}) collective-permute-start(bf16[2,256,256]{2,1,0:T(8,128)(2,1)S(1)} %collective-permute-done.33.refs_1_), channel_id=1, source_target_pairs={{0,1},{1,0},{2,3},{3,2},{4,5},{5,4},{6,7},{7,6},{8,9},{9,8},{10,11... | collective-permute-start | bytes 786440 | tf_op jit(solution)/shard_map/ppermute | solution.py:376
  159.9 13.7 %collective-permute-start.37 = (bf16[2,256,256]{2,1,0:T(8,128)(2,1)S(1)}, bf16[2,256,256]{2,1,0:T(8,128)(2,1)S(1)}, u32[]{:S(2)}, u32[]{:S(2)}) collective-permute-start(bf16[2,256,256]{2,1,0:T(8,128)(2,1)S(1)} %collective-permute-done.36.refs_4_), channel_id=1, source_target_pairs={{0,2},{2,0},{4,6},{6,4},{8,10},{10,8},{12,14},{14,12},{16,18},{18,... | collective-permute-start | bytes 786440 | tf_op jit(solution)/shard_map/ppermute | solution.py:380
  163.7 9.9 %collective-permute-start.39 = (bf16[2,256,256]{2,1,0:T(8,128)(2,1)S(1)}, bf16[2,256,256]{2,1,0:T(8,128)(2,1)S(1)}, u32[]{:S(2)}, u32[]{:S(2)}) collective-permute-start(bf16[2,256,256]{2,1,0:T(8,128)(2,1)S(1)} %collective-permute-done.35.refs_3_), channel_id=1, source_target_pairs={{0,4},{2,6},{4,0},{6,2},{8,12},{10,14},{12,8},{14,10},{16,20},{18,... | collective-permute-start | bytes 786440 | tf_op jit(solution)/shard_map/ppermute | solution.py:380
  168.0 10.2 %collective-permute-start.50 = (bf16[2,256,256]{2,1,0:T(8,128)(2,1)S(1)}, bf16[2,256,256]{2,1,0:T(8,128)(2,1)S(1)}, u32[]{:S(2)}, u32[]{:S(2)}) collective-permute-start(bf16[2,256,256]{2,1,0:T(8,128)(2,1)S(1)} %get-tuple-element.93), channel_id=1, source_target_pairs={{0,4},{2,6},{4,0},{6,2},{8,12},{10,14},{12,8},{14,10},{16,20},{18,... | collective-permute-start | bytes 786440 | tf_op jit(solution)/shard_map/ppermute | solution.py:380
  168.1 12.8 %collective-permute-start.49 = (bf16[2,256,256]{2,1,0:T(8,128)(2,1)S(1)}, bf16[2,256,256]{2,1,0:T(8,128)(2,1)S(1)}, u32[]{:S(2)}, u32[]{:S(2)}) collective-permute-start(bf16[2,256,256]{2,1,0:T(8,128)(2,1)S(1)} %add_convert_fusion.1), channel_id=1, source_target_pairs={{0,2},{2,0},{4,6},{6,4},{8,10},{10,8},{12,14},{14,12},{16,18},{18,... | collective-permute-start | bytes 786440 | tf_op jit(solution)/shard_map/ppermute | solution.py:380
  169.0 19.5 %collective-permute-start.47 = (bf16[2,256,256]{2,1,0:T(8,128)(2,1)S(1)}, bf16[2,256,256]{2,1,0:T(8,128)(2,1)S(1)}, u32[]{:S(2)}, u32[]{:S(2)}) collective-permute-start(bf16[2,256,256]{2,1,0:T(8,128)(2,1)S(1)} %add_convert_fusion.2), channel_id=1, source_target_pairs={{4,0},{6,2},{12,8},{14,10},{16,4},{18,6},{20,16},{22,18},{24,12},{... | collective-permute-start | bytes 786440 | tf_op jit(solution)/shard_map/ppermute | solution.py:391
  177.4 11.0 %collective-permute-start.43 = (f32[112,256]{1,0:T(8,128)S(1)}, f32[112,256]{1,0:T(8,128)S(1)}, u32[]{:S(2)}, u32[]{:S(2)}) collective-permute-start(f32[112,256]{1,0:T(8,128)S(1)} %get-tuple-element.115), channel_id=1, source_target_pairs={{0,4},{2,6},{4,0},{6,2},{8,12},{10,14},{12,8},{14,10},{16,20},{18,... | collective-permute-start | bytes 344072 | tf_op jit(solution)/shard_map/ppermute | solution.py:380
  178.2 10.2 %collective-permute-start.44 = (f32[112,256]{1,0:T(8,128)S(1)}, f32[112,256]{1,0:T(8,128)S(1)}, u32[]{:S(2)}, u32[]{:S(2)}) collective-permute-start(f32[112,256]{1,0:T(8,128)S(1)} %get-tuple-element.114), channel_id=1, source_target_pairs={{0,6},{2,4},{4,2},{6,0},{8,14},{10,12},{12,10},{14,8},{16,22},{18,... | collective-permute-start | bytes 344072 | tf_op jit(solution)/shard_map/ppermute | solution.py:380
  180.9 9.0 %collective-permute-start.45 = (bf16[2,256,256]{2,1,0:T(8,128)(2,1)S(1)}, bf16[2,256,256]{2,1,0:T(8,128)(2,1)S(1)}, u32[]{:S(2)}, u32[]{:S(2)}) collective-permute-start(bf16[2,256,256]{2,1,0:T(8,128)(2,1)S(1)} %get-tuple-element.84), channel_id=1, source_target_pairs={{0,2},{2,0},{4,6},{6,4},{8,10},{10,8},{12,14},{14,12},{16,18},{18,... | collective-permute-start | bytes 786440 | tf_op jit(solution)/shard_map/ppermute | solution.py:380
  183.3 10.8 %collective-permute-start.51 = (bf16[2,256,256]{2,1,0:T(8,128)(2,1)S(1)}, bf16[2,256,256]{2,1,0:T(8,128)(2,1)S(1)}, u32[]{:S(2)}, u32[]{:S(2)}) collective-permute-start(bf16[2,256,256]{2,1,0:T(8,128)(2,1)S(1)} %add_convert_fusion), channel_id=1, source_target_pairs={{8,0},{10,2},{12,4},{14,6},{16,8},{18,10},{20,12},{22,14},{24,16},... | collective-permute-start | bytes 786440 | tf_op jit(solution)/shard_map/ppermute | solution.py:385
  210.8 8.4 %collective-permute-start.60 = (f32[108,256]{1,0:T(8,128)S(1)}, f32[108,256]{1,0:T(8,128)S(1)}, u32[]{:S(2)}, u32[]{:S(2)}) collective-permute-start(f32[108,256]{1,0:T(8,128)S(1)} %pad_maximum_fusion.3), channel_id=1, source_target_pairs={{0,16},{2,18},{4,20},{6,22},{8,24},{10,26},{12,28},{14,30},{16,0},... | collective-permute-start | bytes 331784 | tf_op jit(solution)/shard_map/ppermute | solution.py:380
  210.8 8.4 %collective-permute-start.61 = (f32[108,256]{1,0:T(8,128)S(1)}, f32[108,256]{1,0:T(8,128)S(1)}, u32[]{:S(2)}, u32[]{:S(2)}) collective-permute-start(f32[108,256]{1,0:T(8,128)S(1)} %pad_maximum_fusion.3), channel_id=1, source_target_pairs={{0,8},{2,10},{4,12},{6,14},{8,0},{10,2},{12,4},{14,6},{16,24},{18,... | collective-permute-start | bytes 331784 | tf_op jit(solution)/shard_map/ppermute | solution.py:380
  219.6 8.8 %collective-permute-start.62 = (f32[192,256]{1,0:T(8,128)S(1)}, f32[192,256]{1,0:T(8,128)S(1)}, u32[]{:S(2)}, u32[]{:S(2)}) collective-permute-start(f32[192,256]{1,0:T(8,128)S(1)} %concatenate.30), channel_id=1, source_target_pairs={{0,6},{2,4},{4,2},{6,0},{8,14},{10,12},{12,10},{14,8},{16,22},{18,... | collective-permute-start | bytes 589832 | tf_op jit(solution)/shard_map/ppermute | solution.py:380
  222.0 8.5 %collective-permute-start.63 = (f32[192,256]{1,0:T(8,128)S(1)}, f32[192,256]{1,0:T(8,128)S(1)}, u32[]{:S(2)}, u32[]{:S(2)}) collective-permute-start(f32[192,256]{1,0:T(8,128)S(1)} %concatenate.30), channel_id=1, source_target_pairs={{0,4},{2,6},{4,0},{6,2},{8,12},{10,14},{12,8},{14,10},{16,20},{18,... | collective-permute-start | bytes 589832 | tf_op jit(solution)/shard_map/ppermute | solution.py:380
  222.0 8.6 %collective-permute-start.64 = (f32[192,256]{1,0:T(8,128)S(1)}, f32[192,256]{1,0:T(8,128)S(1)}, u32[]{:S(2)}, u32[]{:S(2)}) collective-permute-start(f32[192,256]{1,0:T(8,128)S(1)} %concatenate.30), channel_id=1, source_target_pairs={{0,2},{2,0},{4,6},{6,4},{8,10},{10,8},{12,14},{14,12},{16,18},{18,... | collective-permute-start | bytes 589832 | tf_op jit(solution)/shard_map/ppermute | solution.py:380
  (33 other events, 175.8 us)

commit v4 on v3

--- a/solution.py
+++ b/solution.py
@@ -489,13 +489,16 @@
         )
         side_x, far_x, side = flip(out_side_x, 2), flip(out_far, 1), flip(out_side, 2)
         two_out = (cross[1] + side_x.astype(f32)).astype(bf16)
-        two_x, far = flip(two_out, 1), stride((same[2] + far_x.astype(f32)).astype(bf16), True)
-        two = shift((same[1] + (two_x.astype(f32) + side.astype(f32))).astype(bf16), -2)
+        far_sum = (same[2] + far_x.astype(f32)).astype(bf16)
+        two_x, far = flip(two_out, 1), stride(far_sum, True)
+        two_sum = (same[1] + (two_x.astype(f32) + side.astype(f32))).astype(bf16)
+        two = shift(two_sum, -2)
         inner_out = [inner]
         if step == 0:
             inner_out += call(gram_kernel, [shape(f32, 5 * width // 4, width)], [core, x, x_other], smem=1)
         inner = jnp.concatenate(inner_out)
         inner = jnp.pad(inner, ((0, -inner.shape[0] % lax.axis_size("patch")), (0, 0)))
+        inner = together(inner, two_sum, far_sum)[0]
         inner = scatter(inner, stages[0])
         inner, *joined = together(inner, flip(near, 1), far, two)
         (v,) = call(descend_kernel, [flat], [x, kept, *joined])

time: 244 us -> 250 us (1.025)
  starting transfers between devices: 83.7 us -> 93.9 us
  waiting for transfers between devices: 106 us -> 99.2 us
    ppermute x50, starting transfers between devices: 66 us -> 77 us  [flip(): lax.ppermute(a, 'patch', [(i, i ^ mask) for i in range(lax.axis_size('pat...]
    ppermute x50, waiting for transfers between devices: 81.9 us -> 74.6 us  [flip(): lax.ppermute(a, 'patch', [(i, i ^ mask) for i in range(lax.axis_size('pat...]
    ppermute x4, waiting for transfers between devices: 2.28 us -> 8.19 us  [stride(): lax.ppermute(a, 'patch', [(d, s) if back else (s, d) for s, d in route if...]
    ppermute x4, waiting for transfers between devices: 12.6 us -> 7.63 us  [shift(): lax.ppermute(a, 'patch', [(i - 2 * pairs, i) for i in devices if i - 2 *...]
    unnamed x31 -> x33, local copies, waits for them, and re-layouts: 5.47 us -> 6.19 us
  transfers between devices with their start and end apart: 66 -> 66, of which waited for: 36 -> 38; matrix products, arithmetic and copies ran while one was open for 2% -> 2% of each run, Pallas kernels for 6% -> 6%
where the time goes in v4:
time: 250 us
  waiting for transfers between devices  99.2 us (40%)
  starting transfers between devices  93.9 us (38%)
  Pallas kernels  43.3 us (17%)
  local copies, waits for them, and re-layouts  8.06 us (3%)
  other arithmetic  3.95 us (2%)
    ppermute x50, starting transfers between devices, flip(): lax.ppermute(a, 'patch', [(i, i ^ mask) for i in range(lax.axis_size('pat...  77 us
    ppermute x50, waiting for transfers between devices, flip(): lax.ppermute(a, 'patch', [(i, i ^ mask) for i in range(lax.axis_size('pat...  74.6 us
    pallas_call x8, Pallas kernels, call(): pl.pallas_call(kernel, out_shape=out, in_specs=[pl.BlockSpec(memory_space...  28.5 us
    pallas_call x4, Pallas kernels, tiles_call(): pl.pallas_call(kernel, in_specs=[pl.BlockSpec(memory_space=SMEM)] + [pl.B...  14.9 us
    ppermute x4, starting transfers between devices, stride(): lax.ppermute(a, 'patch', [(d, s) if back else (s, d) for s, d in route if...  8.96 us
    ppermute x8, waiting for transfers between devices, swap_cores(): return lax.ppermute(a, 'vec', [(0, 1), (1, 0)])  8.77 us
    ppermute x4, waiting for transfers between devices, stride(): lax.ppermute(a, 'patch', [(d, s) if back else (s, d) for s, d in route if...  8.19 us
    ppermute x4, waiting for transfers between devices, shift(): lax.ppermute(a, 'patch', [(i - 2 * pairs, i) for i in devices if i - 2 *...  7.63 us
  transfers between devices with their start and end apart: 66, of which 38 were waited for; matrix products, arithmetic and copies ran while one was open for 2% of the time, Pallas kernels for 6%

profile of v4, /device:TPU:0, one launch (start us, length us, event | category | flops | bytes accessed | tf_op | source)
XLA Modules:
  0.0 250.4 jit_solution(151503054097780050)
XLA Ops:
  1.9 3.0 %collective-permute-start = (bf16[2,256,256]{2,1,0:T(8,128)(2,1)S(1)}, bf16[2,256,256]{2,1,0:T(8,128)(2,1)S(1)}, u32[]{:S(2)}, u32[]{:S(2)}) collective-permute-start(bf16[2,256,256]{2,1,0:T(8,128)(2,1)S(1)} %get-tuple-element.56.refs_0_), channel_id=1, source_target_pairs={{0,2},{2,0},{4,6},{6,4},{8,10},{10,8},{12,14},{14,12},{16,18},{18,... | collective-permute-start | bytes 786440 | tf_op jit(solution)/shard_map/ppermute | solution.py:380
  4.9 3.5 %collective-permute-start.1 = (bf16[2,256,256]{2,1,0:T(8,128)(2,1)S(1)}, bf16[2,256,256]{2,1,0:T(8,128)(2,1)S(1)}, u32[]{:S(2)}, u32[]{:S(2)}) collective-permute-start(bf16[2,256,256]{2,1,0:T(8,128)(2,1)S(1)} %get-tuple-element.56.refs_0_), channel_id=1, source_target_pairs={{0,8},{2,10},{4,12},{6,14},{8,16},{10,18},{12,20},{14,22},{16,24},... | collective-permute-start | bytes 786440 | tf_op jit(solution)/shard_map/ppermute | solution.py:385
  11.2 3.7 %collective-permute-start.3 = (bf16[2,256,256]{2,1,0:T(8,128)(2,1)S(1)}, bf16[2,256,256]{2,1,0:T(8,128)(2,1)S(1)}, u32[]{:S(2)}, u32[]{:S(2)}) collective-permute-start(bf16[2,256,256]{2,1,0:T(8,128)(2,1)S(1)} %get-tuple-element.56.refs_0_), channel_id=1, source_target_pairs={{0,4},{2,6},{8,12},{10,14},{4,16},{6,18},{16,20},{18,22},{12,24},{... | collective-permute-start | bytes 786440 | tf_op jit(solution)/shard_map/ppermute | solution.py:391
  16.4 2.5 %collective-permute-start.5 = (bf16[2,256,256]{2,1,0:T(8,128)(2,1)S(1)}, bf16[2,256,256]{2,1,0:T(8,128)(2,1)S(1)}, u32[]{:S(2)}, u32[]{:S(2)}) collective-permute-start(bf16[2,256,256]{2,1,0:T(8,128)(2,1)S(1)} %collective-permute-done.1.refs_2_), channel_id=1, source_target_pairs={{0,4},{2,6},{4,0},{6,2},{8,12},{10,14},{12,8},{14,10},{16,20},{18,... | collective-permute-start | bytes 786440 | tf_op jit(solution)/shard_map/ppermute | solution.py:380
  19.0 3.7 %shard_map.69 = (f32[2,256,256]{2,1,0:T(8,128)S(1)}, f32[2,256,256]{2,1,0:T(8,128)S(1)}, f32[2,256,256]{2,1,0:T(8,128)S(1)}, f32[2,256,256]{2,1,0:T(8,128)S(1)},...) custom-call(s32[132]{0:T(256)S(1)} %concatenate.24.meta, ...), custom_call_target="tpu_custom_call" | custom-call | flops 4294967296 | bytes 12582912 | tf_op jit(solution)/shard_map/pallas_call | solution.py:167
  31.9 2.5 %collective-permute-done.9 = bf16[2,256,256]{2,1,0:T(8,128)(2,1)} collective-permute-done((bf16[2,256,256]{2,1,0:T(8,128)(2,1)}, bf16[2,256,256]{2,1,0:T(8,128)(2,1)}, u32[]{:S(2)}, u32[]{:S(2)}) %collective-permute-start.9) | collective-permute-done | bytes 262176 | tf_op jit(solution)/shard_map/ppermute | solution.py:380
  37.0 2.1 collective-permute-start.10
  39.1 4.2 %collective-permute-done.4.refs_5_ = bf16[2,256,256]{2,1,0:T(8,128)(2,1)S(1)} collective-permute-done((bf16[2,256,256]{2,1,0:T(8,128)(2,1)}, bf16[2,256,256]{2,1,0:T(8,128)(2,1)S(1)}, u32[]{:S(2)}, u32[]{:S(2)}) %collective-permute-start.4) | collective-permute-done | bytes 262176 | tf_op jit(solution)/shard_map/ppermute | solution.py:380
  43.4 4.3 %shard_map.70 = (f32[2,256,256]{2,1,0:T(8,128)S(1)}, bf16[2,256,256]{2,1,0:T(8,128)(2,1)}, f32[448,256]{1,0:T(8,128)S(1)}) custom-call(s32[132]{0:T(256)S(1)} %concatenate.24.meta, bf16[2,256,256]{2,1,0:T(8,128)(2,1)S(1)} %get-tuple-element.56.refs_0_, bf16[2,256,256]{2,1,0:T(8,128)(2,1)S(1)} %collective-permute-done.refs_1_, ...), custom_call_target="tpu_custom_call" | custom-call | flops 4294967296 | bytes 12582912 | tf_op jit(solution)/shard_map/pallas_call | solution.py:167
  50.9 2.0 collective-permute-start.15
  58.8 4.4 %collective-permute-done.14 = f32[192,256]{1,0:T(8,128)S(1)} collective-permute-done((f32[192,256]{1,0:T(8,128)}, f32[192,256]{1,0:T(8,128)S(1)}, u32[]{:S(2)}, u32[]{:S(2)}) %collective-permute-start.14) | collective-permute-done | bytes 196640 | tf_op jit(solution)/shard_map/ppermute | solution.py:380
  65.0 2.2 collective-permute-done.17.far
  69.0 1.8 collective-permute-done.19.theirs.refs_2_
  71.5 9.0 %collective-permute-start.20 = (f32[48,256]{1,0:T(8,128)S(1)}, f32[48,256]{1,0:T(8,128)S(1)}, u32[]{:S(2)}, u32[]{:S(2)}) collective-permute-start(f32[48,256]{1,0:T(8,128)S(1)} %get-tuple-element.130), channel_id=1, source_target_pairs={{0,8},{2,10},{4,12},{6,14},{8,0},{10,2},{12,4},{14,6},{16,24},{18,... | collective-permute-start | bytes 147464 | tf_op jit(solution)/shard_map/ppermute | solution.py:380
  80.5 2.4 collective-permute-start.22
  83.4 3.1 %collective-permute-start.25 = (f32[80,256]{1,0:T(8,128)S(1)}, f32[80,256]{1,0:T(8,128)S(1)}, u32[]{:S(2)}, u32[]{:S(2)}) collective-permute-start(f32[80,256]{1,0:T(8,128)S(1)} %get-tuple-element.128), channel_id=1, source_target_pairs={{0,6},{2,4},{4,2},{6,0},{8,14},{10,12},{12,10},{14,8},{16,22},{18,... | collective-permute-start | bytes 245768 | tf_op jit(solution)/shard_map/ppermute | solution.py:380
  91.7 1.8 collective-permute-start.28
  93.5 3.8 %collective-permute-done.26 = f32[128,256]{1,0:T(8,128)S(1)} collective-permute-done((f32[128,256]{1,0:T(8,128)S(1)}, f32[128,256]{1,0:T(8,128)S(1)}, u32[]{:S(2)}, u32[]{:S(2)}) %collective-permute-start.26) | collective-permute-done | bytes 131104 | tf_op jit(solution)/shard_map/ppermute | solution.py:380
  97.4 4.3 %collective-permute-done.27 = f32[128,256]{1,0:T(8,128)S(1)} collective-permute-done((f32[128,256]{1,0:T(8,128)S(1)}, f32[128,256]{1,0:T(8,128)S(1)}, u32[]{:S(2)}, u32[]{:S(2)}) %collective-permute-start.27) | collective-permute-done | bytes 131104 | tf_op jit(solution)/shard_map/ppermute | solution.py:380
  101.8 2.5 collective-permute-start.29
  105.4 7.0 %collective-permute-done.29 = f32[272,256]{1,0:T(8,128)S(1)} collective-permute-done((f32[272,256]{1,0:T(8,128)S(1)}, f32[272,256]{1,0:T(8,128)S(1)}, u32[]{:S(2)}, u32[]{:S(2)}) %collective-permute-start.29) | collective-permute-done | bytes 278560 | tf_op jit(solution)/shard_map/ppermute | solution.py:380
  112.4 3.3 %collective-permute-done.30 = f32[272,256]{1,0:T(8,128)S(1)} collective-permute-done((f32[272,256]{1,0:T(8,128)S(1)}, f32[272,256]{1,0:T(8,128)S(1)}, u32[]{:S(2)}, u32[]{:S(2)}) %collective-permute-start.30) | collective-permute-done | bytes 278560 | tf_op jit(solution)/shard_map/ppermute | solution.py:380
  116.6 2.7 %collective-permute-done.32.refs_6_ = f32[4,272,256]{2,1,0:T(8,128)S(1)} collective-permute-done((f32[4,272,256]{2,1,0:T(8,128)S(1)}, f32[4,272,256]{2,1,0:T(8,128)S(1)}, u32[]{:S(2)}, u32[]{:S(2)}) %collective-permute-start.32) | collective-permute-done | bytes 1114144 | tf_op jit(solution)/shard_map/ppermute | solution.py:376
  119.3 14.9 %shard_map.74 = (f32[256,512]{1,0:T(8,128)S(1)}, bf16[2,256,256]{2,1,0:T(8,128)(2,1)S(1)}) custom-call(s32[1]{0:T(128)} %bitcast.core.refs_0_, f32[256,512]{1,0:T(8,128)S(1)} %shard_map.72.mine.refs_1_, f32[256,512]{1,0:T(8,128)S(1)} %collective-permute-done.19.theirs.refs_2_, f32[256,512]{1,0:T(8,128)S(1)} %get-tuple-element.54.mine.x.refs_3_, ...), custom_call_target="tpu_custom_call" | custom-call | flops 17179869184 | bytes 5111812 | tf_op jit(solution)/shard_map/pallas_call | solution.py:40
  136.5 6.1 %collective-permute-done.33.refs_1_ = bf16[2,256,256]{2,1,0:T(8,128)(2,1)S(1)} collective-permute-done((bf16[2,256,256]{2,1,0:T(8,128)(2,1)S(1)}, bf16[2,256,256]{2,1,0:T(8,128)(2,1)S(1)}, u32[]{:S(2)}, u32[]{:S(2)}) %collective-permute-start.33) | collective-permute-done | bytes 262176 | tf_op jit(solution)/shard_map/ppermute | solution.py:380
  142.6 2.7 %collective-permute-start.36 = (bf16[2,256,256]{2,1,0:T(8,128)(2,1)S(1)}, bf16[2,256,256]{2,1,0:T(8,128)(2,1)S(1)}, u32[]{:S(2)}, u32[]{:S(2)}) collective-permute-start(bf16[2,256,256]{2,1,0:T(8,128)(2,1)S(1)} %get-tuple-element.82.refs_0_), channel_id=1, source_target_pairs={{0,4},{2,6},{8,12},{10,14},{4,16},{6,18},{16,20},{18,22},{12,24},{... | collective-permute-start | bytes 786440 | tf_op jit(solution)/shard_map/ppermute | solution.py:391
  146.7 3.1 %shard_map.75 = (f32[2,256,256]{2,1,0:T(8,128)S(1)}, f32[2,256,256]{2,1,0:T(8,128)S(1)}, f32[2,256,256]{2,1,0:T(8,128)S(1)}, f32[2,256,256]{2,1,0:T(8,128)S(1)},...) custom-call(s32[132]{0:T(256)S(1)} %concatenate.24.meta, ...), custom_call_target="tpu_custom_call" | custom-call | flops 4294967296 | bytes 12582912 | tf_op jit(solution)/shard_map/pallas_call | solution.py:167
  149.9 2.2 collective-permute-done.36.refs_4_
  152.7 3.3 %collective-permute-done.38.refs_6_ = bf16[2,256,256]{2,1,0:T(8,128)(2,1)S(1)} collective-permute-done((bf16[2,256,256]{2,1,0:T(8,128)(2,1)S(1)}, bf16[2,256,256]{2,1,0:T(8,128)(2,1)S(1)}, u32[]{:S(2)}, u32[]{:S(2)}) %collective-permute-start.38) | collective-permute-done | bytes 262176 | tf_op jit(solution)/shard_map/ppermute | solution.py:380
  156.0 2.5 collective-permute-start.42
  159.6 5.3 %collective-permute-done.42 = bf16[2,256,256]{2,1,0:T(8,128)(2,1)S(1)} collective-permute-done((bf16[2,256,256]{2,1,0:T(8,128)(2,1)S(1)}, bf16[2,256,256]{2,1,0:T(8,128)(2,1)S(1)}, u32[]{:S(2)}, u32[]{:S(2)}) %collective-permute-start.42) | collective-permute-done | bytes 262176 | tf_op jit(solution)/shard_map/ppermute | solution.py:380
  166.4 2.5 %collective-permute-start.44 = (bf16[2,256,256]{2,1,0:T(8,128)(2,1)S(1)}, bf16[2,256,256]{2,1,0:T(8,128)(2,1)S(1)}, u32[]{:S(2)}, u32[]{:S(2)}) collective-permute-start(bf16[2,256,256]{2,1,0:T(8,128)(2,1)S(1)} %get-tuple-element.93), channel_id=1, source_target_pairs={{0,4},{2,6},{4,0},{6,2},{8,12},{10,14},{12,8},{14,10},{16,20},{18,... | collective-permute-start | bytes 786440 | tf_op jit(solution)/shard_map/ppermute | solution.py:380
  170.6 3.7 %shard_map.76 = (f32[2,256,256]{2,1,0:T(8,128)S(1)}, bf16[2,256,256]{2,1,0:T(8,128)(2,1)S(1)}, f32[448,256]{1,0:T(8,128)S(1)}) custom-call(s32[132]{0:T(256)S(1)} %concatenate.24.meta, bf16[2,256,256]{2,1,0:T(8,128)(2,1)S(1)} %get-tuple-element.82.refs_0_, bf16[2,256,256]{2,1,0:T(8,128)(2,1)S(1)} %collective-permute-done.33.refs_1_, ...), custom_call_target="tpu_custom_call" | custom-call | flops 4294967296 | bytes 12582912 | tf_op jit(solution)/shard_map/pallas_call | solution.py:167
  174.5 3.9 %collective-permute-done.43 = bf16[2,256,256]{2,1,0:T(8,128)(2,1)S(1)} collective-permute-done((bf16[2,256,256]{2,1,0:T(8,128)(2,1)S(1)}, bf16[2,256,256]{2,1,0:T(8,128)(2,1)S(1)}, u32[]{:S(2)}, u32[]{:S(2)}) %collective-permute-start.43) | collective-permute-done | bytes 262176 | tf_op jit(solution)/shard_map/ppermute | solution.py:380
  187.6 3.8 %collective-permute-done.50.far = bf16[2,256,256]{2,1,0:T(8,128)(2,1)S(1)} collective-permute-done((bf16[2,256,256]{2,1,0:T(8,128)(2,1)S(1)}, bf16[2,256,256]{2,1,0:T(8,128)(2,1)S(1)}, u32[]{:S(2)}, u32[]{:S(2)}) %collective-permute-start.50) | collective-permute-done | bytes 262176 | tf_op jit(solution)/shard_map/ppermute | solution.py:391
  191.4 6.1 %collective-permute-done.51.two = bf16[2,256,256]{2,1,0:T(8,128)(2,1)S(1)} collective-permute-done((bf16[2,256,256]{2,1,0:T(8,128)(2,1)S(1)}, bf16[2,256,256]{2,1,0:T(8,128)(2,1)S(1)}, u32[]{:S(2)}, u32[]{:S(2)}) %collective-permute-start.51) | collective-permute-done | bytes 262176 | tf_op jit(solution)/shard_map/ppermute | solution.py:385
  197.7 1.9 collective-permute-done.52.theirs.refs_2_
  200.3 4.8 %collective-permute-start.53 = (f32[28,256]{1,0:T(8,128)S(1)}, f32[28,256]{1,0:T(8,128)S(1)}, u32[]{:S(2)}, u32[]{:S(2)}) collective-permute-start(f32[28,256]{1,0:T(8,128)S(1)} %get-tuple-element.133), channel_id=1, source_target_pairs={{0,8},{2,10},{4,12},{6,14},{8,0},{10,2},{12,4},{14,6},{16,24},{18,... | collective-permute-start | bytes 86024 | tf_op jit(solution)/shard_map/ppermute | solution.py:380
  205.1 2.4 collective-permute-start.55
  208.5 2.6 %collective-permute-start.58 = (f32[80,256]{1,0:T(8,128)S(1)}, f32[80,256]{1,0:T(8,128)S(1)}, u32[]{:S(2)}, u32[]{:S(2)}) collective-permute-start(f32[80,256]{1,0:T(8,128)S(1)} %get-tuple-element.125), channel_id=1, source_target_pairs={{0,6},{2,4},{4,2},{6,0},{8,14},{10,12},{12,10},{14,8},{16,22},{18,... | collective-permute-start | bytes 245768 | tf_op jit(solution)/shard_map/ppermute | solution.py:380
  216.5 2.0 collective-permute-start.61
  218.4 3.1 %collective-permute-done.59 = f32[108,256]{1,0:T(8,128)S(1)} collective-permute-done((f32[108,256]{1,0:T(8,128)S(1)}, f32[108,256]{1,0:T(8,128)S(1)}, u32[]{:S(2)}, u32[]{:S(2)}) %collective-permute-start.59) | collective-permute-done | bytes 110624 | tf_op jit(solution)/shard_map/ppermute | solution.py:380
  221.5 3.6 %collective-permute-done.60 = f32[108,256]{1,0:T(8,128)S(1)} collective-permute-done((f32[108,256]{1,0:T(8,128)S(1)}, f32[108,256]{1,0:T(8,128)S(1)}, u32[]{:S(2)}, u32[]{:S(2)}) %collective-permute-start.60) | collective-permute-done | bytes 110624 | tf_op jit(solution)/shard_map/ppermute | solution.py:380
  225.5 2.6 %collective-permute-start.62 = (f32[192,256]{1,0:T(8,128)S(1)}, f32[192,256]{1,0:T(8,128)S(1)}, u32[]{:S(2)}, u32[]{:S(2)}) collective-permute-start(f32[192,256]{1,0:T(8,128)S(1)} %concatenate.30), channel_id=1, source_target_pairs={{0,6},{2,4},{4,2},{6,0},{8,14},{10,12},{12,10},{14,8},{16,22},{18,... | collective-permute-start | bytes 589832 | tf_op jit(solution)/shard_map/ppermute | solution.py:380
  229.2 5.0 %collective-permute-done.62 = f32[192,256]{1,0:T(8,128)S(1)} collective-permute-done((f32[192,256]{1,0:T(8,128)S(1)}, f32[192,256]{1,0:T(8,128)S(1)}, u32[]{:S(2)}, u32[]{:S(2)}) %collective-permute-start.62) | collective-permute-done | bytes 196640 | tf_op jit(solution)/shard_map/ppermute | solution.py:380
  234.1 1.8 collective-permute-done.63
  236.9 2.3 collective-permute-done.65.refs_6_
  239.2 11.2 %shard_map.79 = (f32[512,256]{1,0:T(8,128)}, f32[512,256]{1,0:T(8,128)}) custom-call(s32[1]{0:T(128)} %bitcast.core.refs_0_, f32[256,512]{1,0:T(8,128)S(1)} %shard_map.77.mine.refs_1_, f32[256,512]{1,0:T(8,128)S(1)} %collective-permute-done.52.theirs.refs_2_, f32[256,512]{1,0:T(8,128)S(1)} %get-tuple-element.80.x.refs_3_, ...), custom_call_target="tpu_custom_call" | custom-call | flops 17179869184 | bytes 4718596 | tf_op jit(solution)/shard_map/pallas_call | solution.py:40
  (164 shorter events, 65.2 us)
Async XLA Ops:
  1.9 9.3 %collective-permute-start = (bf16[2,256,256]{2,1,0:T(8,128)(2,1)S(1)}, bf16[2,256,256]{2,1,0:T(8,128)(2,1)S(1)}, u32[]{:S(2)}, u32[]{:S(2)}) collective-permute-start(bf16[2,256,256]{2,1,0:T(8,128)(2,1)S(1)} %get-tuple-element.56.refs_0_), channel_id=1, source_target_pairs={{0,2},{2,0},{4,6},{6,4},{8,10},{10,8},{12,14},{14,12},{16,18},{18,... | collective-permute-start | bytes 786440 | tf_op jit(solution)/shard_map/ppermute | solution.py:380
  4.9 10.0 %collective-permute-start.1 = (bf16[2,256,256]{2,1,0:T(8,128)(2,1)S(1)}, bf16[2,256,256]{2,1,0:T(8,128)(2,1)S(1)}, u32[]{:S(2)}, u32[]{:S(2)}) collective-permute-start(bf16[2,256,256]{2,1,0:T(8,128)(2,1)S(1)} %get-tuple-element.56.refs_0_), channel_id=1, source_target_pairs={{0,8},{2,10},{4,12},{6,14},{8,16},{10,18},{12,20},{14,22},{16,24},... | collective-permute-start | bytes 786440 | tf_op jit(solution)/shard_map/ppermute | solution.py:385
  8.4 22.0 %collective-permute-start.7 = (f32[256,512]{1,0:T(8,128)S(1)}, f32[256,512]{1,0:T(8,128)S(1)}, u32[]{:S(2)}, u32[]{:S(2)}) collective-permute-start(f32[256,512]{1,0:T(8,128)S(1)} %get-tuple-element.54.mine.x.refs_3_), channel_id=1, source_target_pairs={{0,1},{1,0},{2,3},{3,2},{4,5},{5,4},{6,7},{7,6},{8,9},{9,8},{10,11... | collective-permute-start | bytes 1572872 | tf_op jit(solution)/shard_map/ppermute | solution.py:376
  11.2 14.6 %collective-permute-start.3 = (bf16[2,256,256]{2,1,0:T(8,128)(2,1)S(1)}, bf16[2,256,256]{2,1,0:T(8,128)(2,1)S(1)}, u32[]{:S(2)}, u32[]{:S(2)}) collective-permute-start(bf16[2,256,256]{2,1,0:T(8,128)(2,1)S(1)} %get-tuple-element.56.refs_0_), channel_id=1, source_target_pairs={{0,4},{2,6},{8,12},{10,14},{4,16},{6,18},{16,20},{18,22},{12,24},{... | collective-permute-start | bytes 786440 | tf_op jit(solution)/shard_map/ppermute | solution.py:391
  14.9 10.9 %collective-permute-start.2 = (bf16[2,256,256]{2,1,0:T(8,128)(2,1)S(1)}, bf16[2,256,256]{2,1,0:T(8,128)(2,1)S(1)}, u32[]{:S(2)}, u32[]{:S(2)}) collective-permute-start(bf16[2,256,256]{2,1,0:T(8,128)(2,1)S(1)} %collective-permute-done.1.refs_2_), channel_id=1, source_target_pairs={{0,2},{2,0},{4,6},{6,4},{8,10},{10,8},{12,14},{14,12},{16,18},{18,... | collective-permute-start | bytes 786440 | tf_op jit(solution)/shard_map/ppermute | solution.py:380
  16.4 9.3 %collective-permute-start.5 = (bf16[2,256,256]{2,1,0:T(8,128)(2,1)S(1)}, bf16[2,256,256]{2,1,0:T(8,128)(2,1)S(1)}, u32[]{:S(2)}, u32[]{:S(2)}) collective-permute-start(bf16[2,256,256]{2,1,0:T(8,128)(2,1)S(1)} %collective-permute-done.1.refs_2_), channel_id=1, source_target_pairs={{0,4},{2,6},{4,0},{6,2},{8,12},{10,14},{12,8},{14,10},{16,20},{18,... | collective-permute-start | bytes 786440 | tf_op jit(solution)/shard_map/ppermute | solution.py:380
  28.4 8.6 %collective-permute-start.8 = (bf16[2,256,256]{2,1,0:T(8,128)(2,1)S(1)}, bf16[2,256,256]{2,1,0:T(8,128)(2,1)S(1)}, u32[]{:S(2)}, u32[]{:S(2)}) collective-permute-start(bf16[2,256,256]{2,1,0:T(8,128)(2,1)S(1)} %collective-permute-done.refs_1_), channel_id=1, source_target_pairs={{0,1},{1,0},{2,3},{3,2},{4,5},{5,4},{6,7},{7,6},{8,9},{9,8},{10,11... | collective-permute-start | bytes 786440 | tf_op jit(solution)/shard_map/ppermute | solution.py:376
  28.4 19.4 %collective-permute-start.12 = (bf16[2,256,256]{2,1,0:T(8,128)(2,1)}, bf16[2,256,256]{2,1,0:T(8,128)(2,1)S(1)}, u32[]{:S(2)}, u32[]{:S(2)}) collective-permute-start(bf16[2,256,256]{2,1,0:T(8,128)(2,1)} %copy-done.5), channel_id=1, source_target_pairs={{0,2},{2,0},{4,6},{6,4},{8,10},{10,8},{12,14},{14,12},{16,18},{18,... | collective-permute-start | bytes 786440 | tf_op jit(solution)/shard_map/ppermute | solution.py:380
  29.9 13.4 %collective-permute-start.4 = (bf16[2,256,256]{2,1,0:T(8,128)(2,1)}, bf16[2,256,256]{2,1,0:T(8,128)(2,1)S(1)}, u32[]{:S(2)}, u32[]{:S(2)}) collective-permute-start(bf16[2,256,256]{2,1,0:T(8,128)(2,1)} %copy-done.1), channel_id=1, source_target_pairs={{0,2},{2,0},{4,6},{6,4},{8,10},{10,8},{12,14},{14,12},{16,18},{18,... | collective-permute-start | bytes 786440 | tf_op jit(solution)/shard_map/ppermute | solution.py:380
  30.4 12.9 %collective-permute-start.6 = (bf16[2,256,256]{2,1,0:T(8,128)(2,1)}, bf16[2,256,256]{2,1,0:T(8,128)(2,1)S(1)}, u32[]{:S(2)}, u32[]{:S(2)}) collective-permute-start(bf16[2,256,256]{2,1,0:T(8,128)(2,1)} %copy-done.6), channel_id=1, source_target_pairs={{0,4},{2,6},{4,0},{6,2},{8,12},{10,14},{12,8},{14,10},{16,20},{18,... | collective-permute-start | bytes 786440 | tf_op jit(solution)/shard_map/ppermute | solution.py:380
  34.4 14.2 %collective-permute-start.11 = (bf16[2,256,256]{2,1,0:T(8,128)(2,1)S(1)}, bf16[2,256,256]{2,1,0:T(8,128)(2,1)S(1)}, u32[]{:S(2)}, u32[]{:S(2)}) collective-permute-start(bf16[2,256,256]{2,1,0:T(8,128)(2,1)S(1)} %copy-done.4), channel_id=1, source_target_pairs={{0,4},{2,6},{4,0},{6,2},{8,12},{10,14},{12,8},{14,10},{16,20},{18,... | collective-permute-start | bytes 786440 | tf_op jit(solution)/shard_map/ppermute | solution.py:380
  37.0 11.7 %collective-permute-start.10 = (bf16[2,256,256]{2,1,0:T(8,128)(2,1)S(1)}, bf16[2,256,256]{2,1,0:T(8,128)(2,1)S(1)}, u32[]{:S(2)}, u32[]{:S(2)}) collective-permute-start(bf16[2,256,256]{2,1,0:T(8,128)(2,1)S(1)} %add_convert_fusion.5), channel_id=1, source_target_pairs={{0,2},{2,0},{4,6},{6,4},{8,10},{10,8},{12,14},{14,12},{16,18},{18,... | collective-permute-start | bytes 786440 | tf_op jit(solution)/shard_map/ppermute | solution.py:380
  49.5 7.8 %collective-permute-start.13 = (f32[192,256]{1,0:T(8,128)S(1)}, f32[192,256]{1,0:T(8,128)S(1)}, u32[]{:S(2)}, u32[]{:S(2)}) collective-permute-start(f32[192,256]{1,0:T(8,128)S(1)} %get-tuple-element.114), channel_id=1, source_target_pairs={{0,2},{2,0},{4,6},{6,4},{8,10},{10,8},{12,14},{14,12},{16,18},{18,... | collective-permute-start | bytes 589832 | tf_op jit(solution)/shard_map/ppermute | solution.py:380
  50.9 12.3 %collective-permute-start.14 = (f32[192,256]{1,0:T(8,128)}, f32[192,256]{1,0:T(8,128)S(1)}, u32[]{:S(2)}, u32[]{:S(2)}) collective-permute-start(f32[192,256]{1,0:T(8,128)} %get-tuple-element.116), channel_id=1, source_target_pairs={{0,4},{2,6},{4,0},{6,2},{8,12},{10,14},{12,8},{14,10},{16,20},{18,... | collective-permute-start | bytes 589832 | tf_op jit(solution)/shard_map/ppermute | solution.py:380
  50.9 12.9 %collective-permute-start.15 = (f32[192,256]{1,0:T(8,128)S(1)}, f32[192,256]{1,0:T(8,128)}, u32[]{:S(2)}, u32[]{:S(2)}) collective-permute-start(f32[192,256]{1,0:T(8,128)S(1)} %get-tuple-element.115), channel_id=1, source_target_pairs={{0,6},{2,4},{4,2},{6,0},{8,14},{10,12},{12,10},{14,8},{16,22},{18,... | collective-permute-start | bytes 589832 | tf_op jit(solution)/shard_map/ppermute | solution.py:380
  52.9 14.2 %collective-permute-start.17 = (bf16[2,256,256]{2,1,0:T(8,128)(2,1)}, bf16[2,256,256]{2,1,0:T(8,128)(2,1)S(1)}, u32[]{:S(2)}, u32[]{:S(2)}) collective-permute-start(bf16[2,256,256]{2,1,0:T(8,128)(2,1)} %add_convert_fusion.3), channel_id=1, source_target_pairs={{4,0},{6,2},{12,8},{14,10},{16,4},{18,6},{20,16},{22,18},{24,12},{... | collective-permute-start | bytes 786440 | tf_op jit(solution)/shard_map/ppermute | solution.py:391
  54.2 12.9 %collective-permute-start.16 = (bf16[2,256,256]{2,1,0:T(8,128)(2,1)}, bf16[2,256,256]{2,1,0:T(8,128)(2,1)S(1)}, u32[]{:S(2)}, u32[]{:S(2)}) collective-permute-start(bf16[2,256,256]{2,1,0:T(8,128)(2,1)} %get-tuple-element.71), channel_id=1, source_target_pairs={{0,2},{2,0},{4,6},{6,4},{8,10},{10,8},{12,14},{14,12},{16,18},{18,... | collective-permute-start | bytes 786440 | tf_op jit(solution)/shard_map/ppermute | solution.py:380
  57.3 11.4 %collective-permute-start.18 = (bf16[2,256,256]{2,1,0:T(8,128)(2,1)S(1)}, bf16[2,256,256]{2,1,0:T(8,128)(2,1)S(1)}, u32[]{:S(2)}, u32[]{:S(2)}) collective-permute-start(bf16[2,256,256]{2,1,0:T(8,128)(2,1)S(1)} %add_convert_fusion.4), channel_id=1, source_target_pairs={{8,0},{10,2},{12,4},{14,6},{16,8},{18,10},{20,12},{22,14},{24,16},... | collective-permute-start | bytes 786440 | tf_op jit(solution)/shard_map/ppermute | solution.py:385
  71.5 11.9 %collective-permute-start.20 = (f32[48,256]{1,0:T(8,128)S(1)}, f32[48,256]{1,0:T(8,128)S(1)}, u32[]{:S(2)}, u32[]{:S(2)}) collective-permute-start(f32[48,256]{1,0:T(8,128)S(1)} %get-tuple-element.130), channel_id=1, source_target_pairs={{0,8},{2,10},{4,12},{6,14},{8,0},{10,2},{12,4},{14,6},{16,24},{18,... | collective-permute-start | bytes 147464 | tf_op jit(solution)/shard_map/ppermute | solution.py:380
  89.1 8.3 %collective-permute-start.26 = (f32[128,256]{1,0:T(8,128)S(1)}, f32[128,256]{1,0:T(8,128)S(1)}, u32[]{:S(2)}, u32[]{:S(2)}) collective-permute-start(f32[128,256]{1,0:T(8,128)S(1)} %constant_dynamic-update-slice_fusion), channel_id=1, source_target_pairs={{0,24},{2,26},{4,28},{6,30},{8,16},{10,18},{12,20},{14,22},{16,8},... | collective-permute-start | bytes 393224 | tf_op jit(solution)/shard_map/ppermute | solution.py:380
  90.5 11.1 %collective-permute-start.27 = (f32[128,256]{1,0:T(8,128)S(1)}, f32[128,256]{1,0:T(8,128)S(1)}, u32[]{:S(2)}, u32[]{:S(2)}) collective-permute-start(f32[128,256]{1,0:T(8,128)S(1)} %constant_dynamic-update-slice_fusion), channel_id=1, source_target_pairs={{0,16},{2,18},{4,20},{6,22},{8,24},{10,26},{12,28},{14,30},{16,0},... | collective-permute-start | bytes 393224 | tf_op jit(solution)/shard_map/ppermute | solution.py:380
  91.7 9.9 %collective-permute-start.28 = (f32[128,256]{1,0:T(8,128)S(1)}, f32[128,256]{1,0:T(8,128)S(1)}, u32[]{:S(2)}, u32[]{:S(2)}) collective-permute-start(f32[128,256]{1,0:T(8,128)S(1)} %constant_dynamic-update-slice_fusion), channel_id=1, source_target_pairs={{0,8},{2,10},{4,12},{6,14},{8,0},{10,2},{12,4},{14,6},{16,24},{18,... | collective-permute-start | bytes 393224 | tf_op jit(solution)/shard_map/ppermute | solution.py:380
  101.8 10.6 %collective-permute-start.29 = (f32[272,256]{1,0:T(8,128)S(1)}, f32[272,256]{1,0:T(8,128)S(1)}, u32[]{:S(2)}, u32[]{:S(2)}) collective-permute-start(f32[272,256]{1,0:T(8,128)S(1)} %fusion.4), channel_id=1, source_target_pairs={{0,6},{2,4},{4,2},{6,0},{8,14},{10,12},{12,10},{14,8},{16,22},{18,... | collective-permute-start | bytes 835592 | tf_op jit(solution)/shard_map/ppermute | solution.py:380
  104.2 11.4 %collective-permute-start.30 = (f32[272,256]{1,0:T(8,128)S(1)}, f32[272,256]{1,0:T(8,128)S(1)}, u32[]{:S(2)}, u32[]{:S(2)}) collective-permute-start(f32[272,256]{1,0:T(8,128)S(1)} %fusion.4), channel_id=1, source_target_pairs={{0,4},{2,6},{4,0},{6,2},{8,12},{10,14},{12,8},{14,10},{16,20},{18,... | collective-permute-start | bytes 835592 | tf_op jit(solution)/shard_map/ppermute | solution.py:380
  104.5 11.8 %collective-permute-start.31 = (f32[272,256]{1,0:T(8,128)S(1)}, f32[272,256]{1,0:T(8,128)S(1)}, u32[]{:S(2)}, u32[]{:S(2)}) collective-permute-start(f32[272,256]{1,0:T(8,128)S(1)} %fusion.4), channel_id=1, source_target_pairs={{0,2},{2,0},{4,6},{6,4},{8,10},{10,8},{12,14},{14,12},{16,18},{18,... | collective-permute-start | bytes 835592 | tf_op jit(solution)/shard_map/ppermute | solution.py:380
  134.2 8.4 %collective-permute-start.33 = (bf16[2,256,256]{2,1,0:T(8,128)(2,1)S(1)}, bf16[2,256,256]{2,1,0:T(8,128)(2,1)S(1)}, u32[]{:S(2)}, u32[]{:S(2)}) collective-permute-start(bf16[2,256,256]{2,1,0:T(8,128)(2,1)S(1)} %get-tuple-element.82.refs_0_), channel_id=1, source_target_pairs={{0,2},{2,0},{4,6},{6,4},{8,10},{10,8},{12,14},{14,12},{16,18},{18,... | collective-permute-start | bytes 786440 | tf_op jit(solution)/shard_map/ppermute | solution.py:380
  135.1 10.2 %collective-permute-start.34 = (bf16[2,256,256]{2,1,0:T(8,128)(2,1)S(1)}, bf16[2,256,256]{2,1,0:T(8,128)(2,1)S(1)}, u32[]{:S(2)}, u32[]{:S(2)}) collective-permute-start(bf16[2,256,256]{2,1,0:T(8,128)(2,1)S(1)} %get-tuple-element.82.refs_0_), channel_id=1, source_target_pairs={{0,8},{2,10},{4,12},{6,14},{8,16},{10,18},{12,20},{14,22},{16,24},... | collective-permute-start | bytes 786440 | tf_op jit(solution)/shard_map/ppermute | solution.py:385
  136.4 30.0 %collective-permute-start.40 = (f32[256,512]{1,0:T(8,128)S(1)}, f32[256,512]{1,0:T(8,128)S(1)}, u32[]{:S(2)}, u32[]{:S(2)}) collective-permute-start(f32[256,512]{1,0:T(8,128)S(1)} %get-tuple-element.80.x.refs_3_), channel_id=1, source_target_pairs={{0,1},{1,0},{2,3},{3,2},{4,5},{5,4},{6,7},{7,6},{8,9},{9,8},{10,11... | collective-permute-start | bytes 1572872 | tf_op jit(solution)/shard_map/ppermute | solution.py:376
  142.6 9.5 %collective-permute-start.36 = (bf16[2,256,256]{2,1,0:T(8,128)(2,1)S(1)}, bf16[2,256,256]{2,1,0:T(8,128)(2,1)S(1)}, u32[]{:S(2)}, u32[]{:S(2)}) collective-permute-start(bf16[2,256,256]{2,1,0:T(8,128)(2,1)S(1)} %get-tuple-element.82.refs_0_), channel_id=1, source_target_pairs={{0,4},{2,6},{8,12},{10,14},{4,16},{6,18},{16,20},{18,22},{12,24},{... | collective-permute-start | bytes 786440 | tf_op jit(solution)/shard_map/ppermute | solution.py:391
  145.4 7.3 %collective-permute-start.35 = (bf16[2,256,256]{2,1,0:T(8,128)(2,1)S(1)}, bf16[2,256,256]{2,1,0:T(8,128)(2,1)S(1)}, u32[]{:S(2)}, u32[]{:S(2)}) collective-permute-start(bf16[2,256,256]{2,1,0:T(8,128)(2,1)S(1)} %collective-permute-done.34.refs_2_), channel_id=1, source_target_pairs={{0,2},{2,0},{4,6},{6,4},{8,10},{10,8},{12,14},{14,12},{16,18},{18,... | collective-permute-start | bytes 786440 | tf_op jit(solution)/shard_map/ppermute | solution.py:380
  146.6 9.4 %collective-permute-start.38 = (bf16[2,256,256]{2,1,0:T(8,128)(2,1)S(1)}, bf16[2,256,256]{2,1,0:T(8,128)(2,1)S(1)}, u32[]{:S(2)}, u32[]{:S(2)}) collective-permute-start(bf16[2,256,256]{2,1,0:T(8,128)(2,1)S(1)} %collective-permute-done.34.refs_2_), channel_id=1, source_target_pairs={{0,4},{2,6},{4,0},{6,2},{8,12},{10,14},{12,8},{14,10},{16,20},{18,... | collective-permute-start | bytes 786440 | tf_op jit(solution)/shard_map/ppermute | solution.py:380
  156.0 9.0 %collective-permute-start.42 = (bf16[2,256,256]{2,1,0:T(8,128)(2,1)S(1)}, bf16[2,256,256]{2,1,0:T(8,128)(2,1)S(1)}, u32[]{:S(2)}, u32[]{:S(2)}) collective-permute-start(bf16[2,256,256]{2,1,0:T(8,128)(2,1)S(1)} %get-tuple-element.92), channel_id=1, source_target_pairs={{0,4},{2,6},{4,0},{6,2},{8,12},{10,14},{12,8},{14,10},{16,20},{18,... | collective-permute-start | bytes 786440 | tf_op jit(solution)/shard_map/ppermute | solution.py:380
  158.5 10.5 %collective-permute-start.41 = (bf16[2,256,256]{2,1,0:T(8,128)(2,1)S(1)}, bf16[2,256,256]{2,1,0:T(8,128)(2,1)S(1)}, u32[]{:S(2)}, u32[]{:S(2)}) collective-permute-start(bf16[2,256,256]{2,1,0:T(8,128)(2,1)S(1)} %collective-permute-done.33.refs_1_), channel_id=1, source_target_pairs={{0,1},{1,0},{2,3},{3,2},{4,5},{5,4},{6,7},{7,6},{8,9},{9,8},{10,11... | collective-permute-start | bytes 786440 | tf_op jit(solution)/shard_map/ppermute | solution.py:376
  158.5 11.1 %collective-permute-start.37 = (bf16[2,256,256]{2,1,0:T(8,128)(2,1)S(1)}, bf16[2,256,256]{2,1,0:T(8,128)(2,1)S(1)}, u32[]{:S(2)}, u32[]{:S(2)}) collective-permute-start(bf16[2,256,256]{2,1,0:T(8,128)(2,1)S(1)} %collective-permute-done.36.refs_4_), channel_id=1, source_target_pairs={{0,2},{2,0},{4,6},{6,4},{8,10},{10,8},{12,14},{14,12},{16,18},{18,... | collective-permute-start | bytes 786440 | tf_op jit(solution)/shard_map/ppermute | solution.py:380
  159.6 11.0 %collective-permute-start.39 = (bf16[2,256,256]{2,1,0:T(8,128)(2,1)S(1)}, bf16[2,256,256]{2,1,0:T(8,128)(2,1)S(1)}, u32[]{:S(2)}, u32[]{:S(2)}) collective-permute-start(bf16[2,256,256]{2,1,0:T(8,128)(2,1)S(1)} %collective-permute-done.35.refs_3_), channel_id=1, source_target_pairs={{0,4},{2,6},{4,0},{6,2},{8,12},{10,14},{12,8},{14,10},{16,20},{18,... | collective-permute-start | bytes 786440 | tf_op jit(solution)/shard_map/ppermute | solution.py:380
  164.9 9.3 %collective-permute-start.45 = (bf16[2,256,256]{2,1,0:T(8,128)(2,1)S(1)}, bf16[2,256,256]{2,1,0:T(8,128)(2,1)S(1)}, u32[]{:S(2)}, u32[]{:S(2)}) collective-permute-start(bf16[2,256,256]{2,1,0:T(8,128)(2,1)S(1)} %get-tuple-element.95), channel_id=1, source_target_pairs={{0,2},{2,0},{4,6},{6,4},{8,10},{10,8},{12,14},{14,12},{16,18},{18,... | collective-permute-start | bytes 786440 | tf_op jit(solution)/shard_map/ppermute | solution.py:380
  166.4 8.1 %collective-permute-start.44 = (bf16[2,256,256]{2,1,0:T(8,128)(2,1)S(1)}, bf16[2,256,256]{2,1,0:T(8,128)(2,1)S(1)}, u32[]{:S(2)}, u32[]{:S(2)}) collective-permute-start(bf16[2,256,256]{2,1,0:T(8,128)(2,1)S(1)} %get-tuple-element.93), channel_id=1, source_target_pairs={{0,4},{2,6},{4,0},{6,2},{8,12},{10,14},{12,8},{14,10},{16,20},{18,... | collective-permute-start | bytes 786440 | tf_op jit(solution)/shard_map/ppermute | solution.py:380
  169.0 9.5 %collective-permute-start.43 = (bf16[2,256,256]{2,1,0:T(8,128)(2,1)S(1)}, bf16[2,256,256]{2,1,0:T(8,128)(2,1)S(1)}, u32[]{:S(2)}, u32[]{:S(2)}) collective-permute-start(bf16[2,256,256]{2,1,0:T(8,128)(2,1)S(1)} %add_convert_fusion.2), channel_id=1, source_target_pairs={{0,2},{2,0},{4,6},{6,4},{8,10},{10,8},{12,14},{14,12},{16,18},{18,... | collective-permute-start | bytes 786440 | tf_op jit(solution)/shard_map/ppermute | solution.py:380
  182.1 9.3 %collective-permute-start.50 = (bf16[2,256,256]{2,1,0:T(8,128)(2,1)S(1)}, bf16[2,256,256]{2,1,0:T(8,128)(2,1)S(1)}, u32[]{:S(2)}, u32[]{:S(2)}) collective-permute-start(bf16[2,256,256]{2,1,0:T(8,128)(2,1)S(1)} %add_convert_fusion), channel_id=1, source_target_pairs={{4,0},{6,2},{12,8},{14,10},{16,4},{18,6},{20,16},{22,18},{24,12},{... | collective-permute-start | bytes 786440 | tf_op jit(solution)/shard_map/ppermute | solution.py:391
  183.4 8.0 %collective-permute-start.49 = (bf16[2,256,256]{2,1,0:T(8,128)(2,1)S(1)}, bf16[2,256,256]{2,1,0:T(8,128)(2,1)S(1)}, u32[]{:S(2)}, u32[]{:S(2)}) collective-permute-start(bf16[2,256,256]{2,1,0:T(8,128)(2,1)S(1)} %get-tuple-element.97), channel_id=1, source_target_pairs={{0,2},{2,0},{4,6},{6,4},{8,10},{10,8},{12,14},{14,12},{16,18},{18,... | collective-permute-start | bytes 786440 | tf_op jit(solution)/shard_map/ppermute | solution.py:380
  184.6 12.9 %collective-permute-start.51 = (bf16[2,256,256]{2,1,0:T(8,128)(2,1)S(1)}, bf16[2,256,256]{2,1,0:T(8,128)(2,1)S(1)}, u32[]{:S(2)}, u32[]{:S(2)}) collective-permute-start(bf16[2,256,256]{2,1,0:T(8,128)(2,1)S(1)} %add_convert_fusion.1), channel_id=1, source_target_pairs={{8,0},{10,2},{12,4},{14,6},{16,8},{18,10},{20,12},{22,14},{24,16},... | collective-permute-start | bytes 786440 | tf_op jit(solution)/shard_map/ppermute | solution.py:385
  200.3 8.2 %collective-permute-start.53 = (f32[28,256]{1,0:T(8,128)S(1)}, f32[28,256]{1,0:T(8,128)S(1)}, u32[]{:S(2)}, u32[]{:S(2)}) collective-permute-start(f32[28,256]{1,0:T(8,128)S(1)} %get-tuple-element.133), channel_id=1, source_target_pairs={{0,8},{2,10},{4,12},{6,14},{8,0},{10,2},{12,4},{14,6},{16,24},{18,... | collective-permute-start | bytes 86024 | tf_op jit(solution)/shard_map/ppermute | solution.py:380
  214.0 7.5 %collective-permute-start.59 = (f32[108,256]{1,0:T(8,128)S(1)}, f32[108,256]{1,0:T(8,128)S(1)}, u32[]{:S(2)}, u32[]{:S(2)}) collective-permute-start(f32[108,256]{1,0:T(8,128)S(1)} %pad_maximum_fusion.3), channel_id=1, source_target_pairs={{0,24},{2,26},{4,28},{6,30},{8,16},{10,18},{12,20},{14,22},{16,8},... | collective-permute-start | bytes 331784 | tf_op jit(solution)/shard_map/ppermute | solution.py:380
  215.4 9.7 %collective-permute-start.60 = (f32[108,256]{1,0:T(8,128)S(1)}, f32[108,256]{1,0:T(8,128)S(1)}, u32[]{:S(2)}, u32[]{:S(2)}) collective-permute-start(f32[108,256]{1,0:T(8,128)S(1)} %pad_maximum_fusion.3), channel_id=1, source_target_pairs={{0,16},{2,18},{4,20},{6,22},{8,24},{10,26},{12,28},{14,30},{16,0},... | collective-permute-start | bytes 331784 | tf_op jit(solution)/shard_map/ppermute | solution.py:380
  216.5 8.6 %collective-permute-start.61 = (f32[108,256]{1,0:T(8,128)S(1)}, f32[108,256]{1,0:T(8,128)S(1)}, u32[]{:S(2)}, u32[]{:S(2)}) collective-permute-start(f32[108,256]{1,0:T(8,128)S(1)} %pad_maximum_fusion.3), channel_id=1, source_target_pairs={{0,8},{2,10},{4,12},{6,14},{8,0},{10,2},{12,4},{14,6},{16,24},{18,... | collective-permute-start | bytes 331784 | tf_op jit(solution)/shard_map/ppermute | solution.py:380
  225.5 8.7 %collective-permute-start.62 = (f32[192,256]{1,0:T(8,128)S(1)}, f32[192,256]{1,0:T(8,128)S(1)}, u32[]{:S(2)}, u32[]{:S(2)}) collective-permute-start(f32[192,256]{1,0:T(8,128)S(1)} %concatenate.30), channel_id=1, source_target_pairs={{0,6},{2,4},{4,2},{6,0},{8,14},{10,12},{12,10},{14,8},{16,22},{18,... | collective-permute-start | bytes 589832 | tf_op jit(solution)/shard_map/ppermute | solution.py:380
  228.0 7.9 %collective-permute-start.63 = (f32[192,256]{1,0:T(8,128)S(1)}, f32[192,256]{1,0:T(8,128)S(1)}, u32[]{:S(2)}, u32[]{:S(2)}) collective-permute-start(f32[192,256]{1,0:T(8,128)S(1)} %concatenate.30), channel_id=1, source_target_pairs={{0,4},{2,6},{4,0},{6,2},{8,12},{10,14},{12,8},{14,10},{16,20},{18,... | collective-permute-start | bytes 589832 | tf_op jit(solution)/shard_map/ppermute | solution.py:380
  228.1 8.6 %collective-permute-start.64 = (f32[192,256]{1,0:T(8,128)S(1)}, f32[192,256]{1,0:T(8,128)S(1)}, u32[]{:S(2)}, u32[]{:S(2)}) collective-permute-start(f32[192,256]{1,0:T(8,128)S(1)} %concatenate.30), channel_id=1, source_target_pairs={{0,2},{2,0},{4,6},{6,4},{8,10},{10,8},{12,14},{14,12},{16,18},{18,... | collective-permute-start | bytes 589832 | tf_op jit(solution)/shard_map/ppermute | solution.py:380
  (34 other events, 166.2 us)
